TPU v7x, 256 devices: a whole 4x4x8 slice. The times are simulated.
256 devices in a mesh: row: 16 (over y, z_lo, core), col: 16 (over x, z_hi).
Axes of the slice: x: 4, y: 4, z: 8 (z_hi: 4, z_lo: 2; z = z_hi * 2 + z_lo), core: 2. Of those that a mesh axis runs over, the one named last changes fastest.
Arguments:
- rates: bfloat16 [192, 16384], P(None, 'col'), may hold values from -1 to 1
- targets: bfloat16 [192, 16384], P(None, 'row'), may hold values from -6 to 6
- readout_goal: float32 [16, 192], replicated, may hold values from -6 to 6
- inverse_corr: float32 [16384, 16384], P('row', 'col'), may hold values from -0.1 to 3.1, as said below
- recurrent: bfloat16 [16384, 16384], P('row', 'col'), may hold values from -0.046875 to 0.046875
- readout: float32 [16, 16384], P(None, 'col'), may hold values from -0.046875 to 0.046875
Outputs:
- corr_out: float32 [16384, 16384], P('row', 'col')
- recurrent_out: bfloat16 [16384, 16384], P('row', 'col')
- readout_out: float32 [16, 16384], P(None, 'col')
Inputs may be any that keep to these rules, and one draw needn't show every extreme that they name: `inverse_corr`: symmetric and positive definite.
All inputs are finite; a program needn't handle non-finite values.
Results may differ from a plain program's by a relative error of at most 0.0057.
Values may be sent and summed in bfloat16 or wider, within the bound.
A program may use at most 64 MiB of HBM per device.

v0:
```python
import jax
import jax.numpy as jnp
from jax import lax
from jax.sharding import PartitionSpec as P

STEPS = 64
BLOCKS = 3


def on_device(rates, targets, readout_goal, inverse_corr, recurrent, readout):
    high = lax.Precision.HIGHEST
    cols_local = inverse_corr.shape[1]
    col_index = lax.axis_index("col")
    corr = inverse_corr
    weights = recurrent
    outward = readout
    eye = jnp.eye(STEPS, dtype=jnp.float32)
    for window in range(BLOCKS):
        start = window * STEPS
        rate_bf = rates[start : start + STEPS]
        rate32 = rate_bf.astype(jnp.float32)
        prod_part = jnp.dot(rate32, corr.T, precision=high)
        drive_part = jnp.dot(rate_bf, weights.T, preferred_element_type=jnp.float32)
        guess_part = jnp.dot(outward, rate32.T, precision=high)
        prod_rows, drive, guess = lax.psum((prod_part, drive_part, guess_part), "col")
        gathered = lax.all_gather(prod_rows, "row", axis=1, tiled=True)
        prod_cols = lax.dynamic_slice_in_dim(gathered, col_index * cols_local, cols_local, 1)
        cap_part = jnp.dot(rate32, prod_cols.T, precision=high)
        capacity = eye + lax.psum(cap_part, "col")
        factor = jnp.linalg.cholesky(capacity)
        cinverse = jax.scipy.linalg.cho_solve((factor, True), eye)
        coef_p = jnp.dot(cinverse, prod_rows, precision=high)
        err_j = drive - targets[start : start + STEPS].astype(jnp.float32)
        coef_j = jnp.dot(cinverse, err_j, precision=high)
        err_w = guess - readout_goal[:, start : start + STEPS]
        coef_w = jnp.dot(err_w, cinverse, precision=high)
        corr = corr - jnp.dot(coef_p.T, prod_cols, precision=high)
        outward = outward - jnp.dot(coef_w, prod_cols, precision=high)
        weights = (
            weights.astype(jnp.float32) - jnp.dot(coef_j.T, prod_cols, precision=high)
        ).astype(jnp.bfloat16)
    return (corr, weights, outward)


def solution(mesh):
    placed = (P(None, "col"), P(None, "row"), P(), P("row", "col"), P("row", "col"), P(None, "col"))
    return jax.shard_map(
        on_device,
        mesh=mesh,
        in_specs=placed,
        out_specs=(P("row", "col"), P("row", "col"), P(None, "col")),
        check_vma=False,
    )
```

profile of v0, /device:TPU:1, one launch (start us, length us, event | category | flops | bytes accessed | tf_op | source)
XLA Modules:
  0.0 959.3 jit_solution(4560875908762550271)
XLA Ops:
  7.2 5.3 fusion.45
  12.6 1.5 fusion.42
  14.1 161.0 %all-reduce.14.cloned.1.call-done = (f32[64,1024]{1,0:T(8,128)}, f32[64,1024]{1,0:T(8,128)}) async-done(((f32[64,1024]{1,0:T(8,128)}, f32[64,1024]{1,0:T(8,128)}), (f32[64,1024]{1,0:T(8,128)}, f32[64,1024]{1,0:T(8,128)})) %all-reduce.14.cloned.1.call-update) | async-done | bytes 524304 | tf_op jit(solution)/shard_map/psum | solution.py:25
  175.4 49.9 %all-gather.4.cloned.1.call-done = f32[64,16384]{1,0:T(8,128)} async-done(((f32[64,1024]{1,0:T(8,128)}), f32[64,16384]{1,0:T(8,128)}) %all-gather.4.cloned.1.call-update) | async-done | bytes 4194320 | tf_op jit(solution)/shard_map/all_gather | solution.py:26
  225.3 1.2 convolution_bitcast_fusion.6
  226.5 68.7 %all-reduce.2 = (f32[64,64]{0,1:T(8,128)S(1)}, f32[16,64]{1,0:T(8,128)S(1)}) all-reduce(f32[64,64]{0,1:T(8,128)S(1)} %convolution_bitcast_fusion.6, f32[16,64]{1,0:T(8,128)S(1)} %fusion.40), channel_id=1, replica_groups=mesh['row'=16,'col'=16] {'col'}, use_global_device_ids=true, to_apply=%region_1.0 | all-reduce | flops 5120 | bytes 40960 | tf_op jit(solution)/shard_map/psum | solution.py:29
  295.3 5.8 cholesky.59
  301.2 0.6 compare_reduce_fusion.2
  301.8 0.7 fusion.47
  302.5 4.9 custom-call.9
  307.4 0.3 fusion.28
  307.8 1.3 fusion.83
  309.1 5.4 convolution_subtract_fusion.2
  314.6 3.0 convolution_bitcast_fusion.1
  317.6 0.4 fusion.6
  318.0 4.8 subtract_convert_fusion.2
  322.8 1.3 copy-done.3
  324.1 1.5 convolution_bitcast_fusion.3
  325.6 163.8 %all-reduce.12.cloned.1.call-done = (f32[64,1024]{1,0:T(8,128)}, f32[64,1024]{1,0:T(8,128)}) async-done(((f32[64,1024]{1,0:T(8,128)}, f32[64,1024]{1,0:T(8,128)}), (f32[64,1024]{1,0:T(8,128)}, f32[64,1024]{1,0:T(8,128)})) %all-reduce.12.cloned.1.call-update) | async-done | bytes 524304 | tf_op jit(solution)/shard_map/psum | solution.py:25
  489.6 1.2 convolution_subtract_fusion.5
  491.0 48.3 %all-gather.6.cloned.1.call-done = f32[64,16384]{1,0:T(8,128)} async-done(((f32[64,1024]{1,0:T(8,128)}), f32[64,16384]{1,0:T(8,128)}) %all-gather.6.cloned.1.call-update) | async-done | bytes 4194320 | tf_op jit(solution)/shard_map/all_gather | solution.py:26
  539.3 1.2 convolution_bitcast_fusion.5
  540.5 68.8 %all-reduce.1 = (f32[64,64]{0,1:T(8,128)S(1)}, f32[16,64]{1,0:T(8,128)S(1)}) all-reduce(f32[64,64]{0,1:T(8,128)S(1)} %convolution_bitcast_fusion.5, f32[16,64]{1,0:T(8,128)S(1)} %fusion.35), channel_id=1, replica_groups=mesh['row'=16,'col'=16] {'col'}, use_global_device_ids=true, to_apply=%region_5.0 | all-reduce | flops 5120 | bytes 40960 | tf_op jit(solution)/shard_map/psum | solution.py:29
  609.5 5.8 cholesky.70
  615.3 0.6 compare_reduce_fusion.1
  616.0 0.7 fusion.48
  616.6 4.9 custom-call.10
  621.5 0.3 fusion.26
  622.0 1.3 fusion.84
  623.3 1.3 fusion.3
  624.6 5.4 convolution_subtract_fusion.1
  630.1 3.0 convolution_bitcast_fusion
  633.2 4.8 subtract_convert_fusion.1
  638.0 1.5 convolution_bitcast_fusion.2
  639.5 163.7 %all-reduce.10.cloned.1.call-done = (f32[64,1024]{1,0:T(8,128)}, f32[64,1024]{1,0:T(8,128)}) async-done(((f32[64,1024]{1,0:T(8,128)}, f32[64,1024]{1,0:T(8,128)}), (f32[64,1024]{1,0:T(8,128)}, f32[64,1024]{1,0:T(8,128)})) %all-reduce.10.cloned.1.call-update) | async-done | bytes 524304 | tf_op jit(solution)/shard_map/psum | solution.py:25
  803.5 1.2 convolution_subtract_fusion.4
  804.8 48.4 %all-gather.8.cloned.1.call-done = f32[64,16384]{1,0:T(8,128)} async-done(((f32[64,1024]{1,0:T(8,128)}), f32[64,16384]{1,0:T(8,128)}) %all-gather.8.cloned.1.call-update) | async-done | bytes 4194320 | tf_op jit(solution)/shard_map/all_gather | solution.py:26
  853.3 1.2 convolution_bitcast_fusion.4
  854.5 68.7 %all-reduce = (f32[64,64]{0,1:T(8,128)S(1)}, f32[16,64]{1,0:T(8,128)S(1)}) all-reduce(f32[64,64]{0,1:T(8,128)S(1)} %convolution_bitcast_fusion.4, f32[16,64]{1,0:T(8,128)S(1)} %fusion.30), channel_id=1, replica_groups=mesh['row'=16,'col'=16] {'col'}, use_global_device_ids=true, to_apply=%region_7.0 | all-reduce | flops 5120 | bytes 40960 | tf_op jit(solution)/shard_map/psum | solution.py:29
  923.3 5.8 cholesky.81
  929.1 0.6 compare_reduce_fusion
  929.8 0.7 fusion.49
  930.4 4.9 custom-call.11
  935.8 1.5 fusion.85
  937.4 1.3 fusion
  938.8 1.8 convolution_subtract_fusion.3
  940.6 5.7 subtract_convert_fusion
  946.3 6.1 convolution_subtract_fusion
  (55 shorter events, 2.6 us)
Async XLA Ops:
  7.2 5.4 copy-start.6
  7.2 5.4 copy-start.5
  7.2 168.0 %copy-start.8 = (f32[16,1024]{1,0:T(8,128)S(1)}, f32[16,1024]{1,0:T(8,128)}, u32[]{:S(2)}) copy-start(f32[16,1024]{1,0:T(8,128)} %param.14) | copy-start | bytes 196612
  7.2 167.9 %all-reduce.14.cloned.1.call-start = ((), (), s32[]{:S(2)}) async-start(), calls=%async_computation.5 | async-start | bytes 1048576 | tf_op jit(solution)/shard_map/psum | solution.py:25
  14.1 211.2 %all-gather.4.cloned.1.call-start = ((), (), s32[]{:S(2)}) async-start(), calls=%async_computation | async-start | bytes 4456448 | tf_op jit(solution)/shard_map/all_gather | solution.py:26
  175.1 314.3 %all-reduce.12.cloned.1.call-start = ((), (), s32[]{:S(2)}) async-start(), calls=%async_computation.4 | async-start | bytes 1048576 | tf_op jit(solution)/shard_map/psum | solution.py:25
  314.5 8.2 copy-start.2
  314.5 3.0 copy-start.7
  314.6 3.0 copy-start.9
  317.6 171.9 %copy-start.10 = (f32[16,192]{1,0:T(8,128)S(1)}, f32[16,192]{1,0:T(8,128)}, u32[]{:S(2)}) copy-start(f32[16,192]{1,0:T(8,128)} %param.11) | copy-start | bytes 36868
  322.8 1.3 copy-start.3
  325.6 213.7 %all-gather.6.cloned.1.call-start = ((), (), s32[]{:S(2)}) async-start(), calls=%async_computation.1 | async-start | bytes 4456448 | tf_op jit(solution)/shard_map/all_gather | solution.py:26
  489.4 313.8 %all-reduce.10.cloned.1.call-start = ((), (), s32[]{:S(2)}) async-start(), calls=%async_computation.3 | async-start | bytes 1048576 | tf_op jit(solution)/shard_map/psum | solution.py:25
  630.0 7.9 copy-start
  630.1 3.1 copy-start.4
  639.5 213.8 %all-gather.8.cloned.1.call-start = ((), (), s32[]{:S(2)}) async-start(), calls=%async_computation.2 | async-start | bytes 4456448 | tf_op jit(solution)/shard_map/all_gather | solution.py:26
  935.3 11.0 %copy-start.1 = (f32[1024,1024]{1,0:T(8,128)S(1)}, f32[1024,1024]{1,0:T(8,128)}, u32[]{:S(2)}) copy-start(f32[1024,1024]{1,0:T(8,128)} %copy-done) | copy-start | bytes 12582916
Sparse Core Ops, SparseCore 0:
  14.2 160.8 all-reduce.13
  177.0 48.1 all-gather.3
  325.7 163.6 all-reduce.11
  491.0 48.1 all-gather.5
  639.6 163.5 all-reduce.9
  805.0 48.2 all-gather.7
where the time goes:
time: 972 us; the launch traced here: 959 us
  waiting for transfers between devices  635 us (65%)
  blocking collectives  206 us (21%)
  matrix products  65.2 us (7%)
  other arithmetic  36.3 us (4%)
  between operations  14.5 us (1%)
    psum x3, waiting for transfers between devices, on_device(): lax.psum((prod_part, drive_part, guess_part), 'col')  488 us
    psum x3, blocking collectives, on_device(): capacity = eye + lax.psum(cap_part, 'col')  206 us
    all_gather x3, waiting for transfers between devices, on_device(): gathered = lax.all_gather(prod_rows, 'row', axis=1, tiled=True)  147 us
    another operation x9, other arithmetic, on_device(): factor = jnp.linalg.cholesky(capacity)  19.6 us
  transfers between devices with their start and end apart: 6, of which 6 were waited for; matrix products, arithmetic and copies ran while one was open for 0% of the time, Pallas kernels for 0%

commit v1 on v0

v1 whole, which is shorter than its diff:
```python
import jax
import jax.numpy as jnp
from jax import lax
from jax.sharding import PartitionSpec as P


def on_device(rates, targets, readout_goal, inverse_corr, recurrent, readout):
    high = lax.Precision.HIGHEST
    steps = rates.shape[0]
    cols_local = inverse_corr.shape[1]
    col_index = lax.axis_index("col")
    eye = jnp.eye(steps, dtype=jnp.float32)
    rate32 = rates.astype(jnp.float32)
    prod_part = jnp.dot(rate32, inverse_corr.T, precision=high)
    drive_part = jnp.dot(rates, recurrent.T, preferred_element_type=jnp.float32)
    guess_part = jnp.dot(readout, rate32.T, precision=high)
    prod_rows, drive, guess = lax.psum((prod_part, drive_part, guess_part), "col")
    gathered = lax.all_gather(prod_rows, "row", axis=1, tiled=True)
    prod_cols = lax.dynamic_slice_in_dim(gathered, col_index * cols_local, cols_local, 1)
    cap_part = jnp.dot(rate32, prod_cols.T, precision=high)
    capacity = eye + lax.psum(cap_part, "col")
    factor = jnp.linalg.cholesky(capacity)
    cinverse = jax.scipy.linalg.cho_solve((factor, True), eye)
    scaled = jnp.dot(cinverse, prod_cols, precision=high)
    err_j = drive - targets.astype(jnp.float32)
    err_w = guess - readout_goal
    corr = inverse_corr - jnp.dot(prod_rows.T, scaled, precision=high)
    outward = readout - jnp.dot(err_w, scaled, precision=high)
    weights = (
        recurrent.astype(jnp.float32) - jnp.dot(err_j.T, scaled, precision=high)
    ).astype(jnp.bfloat16)
    return (corr, weights, outward)


def solution(mesh):
    placed = (P(None, "col"), P(None, "row"), P(), P("row", "col"), P("row", "col"), P(None, "col"))
    return jax.shard_map(
        on_device,
        mesh=mesh,
        in_specs=placed,
        out_specs=(P("row", "col"), P("row", "col"), P(None, "col")),
        check_vma=False,
    )
```

time: 972 us -> 523 us (0.54)
  waiting for transfers between devices: 635 us -> 336 us
  blocking collectives: 206 us -> 70.5 us
  matrix products: 65.2 us -> 31.4 us
  other arithmetic: 36.3 us -> 55.9 us
    psum x3 -> x1, waiting for transfers between devices: 488 us -> 162 us  [on_device(): lax.psum((prod_part, drive_part, guess_part), 'col')]
    psum x3 -> x1, blocking collectives: 206 us -> 70.5 us  [on_device(): lax.psum((prod_part, drive_part, guess_part), 'col')]
    psum x0 -> x1, waiting for transfers between devices: none -> 90.9 us  [on_device(): capacity = eye + lax.psum(cap_part, 'col')]
    all_gather x3 -> x1, waiting for transfers between devices: 147 us -> 83.1 us  [on_device(): gathered = lax.all_gather(prod_rows, 'row', axis=1, tiled=True)]
    dot_general x27 -> x7, matrix products: 60.4 us -> 22.4 us  [the longest x1 6.22 us: on_device(): jnp.dot(err_j.T, scaled, precision=high)]
    another operation x9 -> x7, other arithmetic: 19.6 us -> 32.7 us  [on_device(): factor = jnp.linalg.cholesky(capacity)]
  transfers between devices with their start and end apart: 6 -> 3, of which waited for: 6 -> 3; matrix products, arithmetic and copies ran while one was open for 0% -> 1% of each run, Pallas kernels for 0% -> 0%
where the time goes in v1:
time: 523 us; the launch traced here: 513 us
  waiting for transfers between devices  336 us (64%)
  blocking collectives  70.5 us (13%)
  other arithmetic  55.9 us (11%)
  matrix products  31.4 us (6%)
  between operations  15.3 us (3%)
    psum x1, waiting for transfers between devices, on_device(): lax.psum((prod_part, drive_part, guess_part), 'col')  162 us
    psum x1, waiting for transfers between devices, on_device(): capacity = eye + lax.psum(cap_part, 'col')  90.9 us
    all_gather x1, waiting for transfers between devices, on_device(): gathered = lax.all_gather(prod_rows, 'row', axis=1, tiled=True)  83.1 us
    psum x1, blocking collectives, on_device(): lax.psum((prod_part, drive_part, guess_part), 'col')  70.5 us
    another operation x7, other arithmetic, on_device(): factor = jnp.linalg.cholesky(capacity)  32.7 us
    another operation x6, other arithmetic, on_device(): cinverse = jax.scipy.linalg.cho_solve((factor, True), eye)  19.8 us
  transfers between devices with their start and end apart: 3, of which 3 were waited for; matrix products, arithmetic and copies ran while one was open for 1% of the time, Pallas kernels for 0%

profile of v1, /device:TPU:1, one launch (start us, length us, event | category | flops | bytes accessed | tf_op | source)
XLA Modules:
  0.0 513.4 jit_solution(4884457856750534474)
XLA Ops:
  7.2 0.0 copy-start
  7.2 0.0 all-reduce.7.cloned.1.call-start
  7.2 0.9 copy-done
  8.2 5.5 %fusion.25 = f32[192,1024]{1,0:T(8,128)} fusion(bf16[192,1024]{1,0:T(8,128)(2,1)S(1)} %copy-done, f32[1024,1024]{1,0:T(8,128)} %param.9), kind=kOutput, calls=%fused_computation.55 | convolution fusion | flops 2415919104 | bytes 5373952 | tf_op jit(solution)/shard_map/dot_general | solution.py:14
  13.7 0.0 all-reduce.7.cloned.1.call-update
  13.7 0.0 all-gather.2.cloned.1.call-start
  13.7 162.2 %all-reduce.7.cloned.1.call-done = f32[192,1024]{1,0:T(8,128)} async-done(((f32[192,1024]{1,0:T(8,128)}), f32[192,1024]{1,0:T(8,128)}) %all-reduce.7.cloned.1.call-update) | async-done | bytes 786448 | tf_op jit(solution)/shard_map/psum | solution.py:17
  176.0 0.0 all-gather.2.cloned.1.call-update
  176.0 0.0 all-reduce.9.cloned.1.call-start
  176.0 1.7 fusion.26
  177.8 83.1 %all-gather.2.cloned.1.call-done = f32[192,16384]{1,0:T(8,128)} async-done(((f32[192,1024]{1,0:T(8,128)}), f32[192,16384]{1,0:T(8,128)}) %all-gather.2.cloned.1.call-update) | async-done | bytes 12582928 | tf_op jit(solution)/shard_map/all_gather | solution.py:18
  260.9 2.3 convolution_bitcast_fusion
  263.2 0.0 all-reduce.9.cloned.1.call-update
  263.3 0.4 fusion.27
  263.7 70.5 %psum.31 = f32[16,192]{1,0:T(8,128)S(1)} all-reduce(f32[16,192]{1,0:T(8,128)S(1)} %fusion.27), channel_id=1, replica_groups=mesh['row'=16,'col'=16] {'col'}, use_global_device_ids=true, to_apply=%region_7.8 | all-reduce | flops 3072 | bytes 24576 | tf_op jit(solution)/shard_map/psum | solution.py:17
  334.2 0.6 iota_compare_fusion
  334.8 0.7 fusion.11
  335.5 90.9 %all-reduce.9.cloned.1.call-done = (f32[192,192]{0,1:T(8,128)}, f32[192,1024]{1,0:T(8,128)}) async-done(((f32[192,192]{0,1:T(8,128)}, f32[192,1024]{1,0:T(8,128)}), (f32[192,192]{0,1:T(8,128)}, f32[192,1024]{1,0:T(8,128)})) %all-reduce.9.cloned.1.call-update) | async-done | bytes 933904 | tf_op jit(solution)/shard_map/psum | solution.py:21
  426.4 1.0 convert_add_fusion
  427.4 0.8 copy.9
  428.2 1.1 fusion.8
  429.3 0.0 copy-start.6
  429.3 0.7 copy-done.6
  429.9 11.7 %cholesky.51 = f32[128,128]{1,0:T(8,128)S(1)} custom-call(f32[128,128]{1,0:T(8,128)S(1)} %cholesky.124), custom_call_target="Cholesky" | custom-call | tf_op jit(solution)/shard_map/jit(cholesky)/cholesky | solution.py:22
  441.7 0.6 select_reduce_fusion
  442.3 0.0 copy-done.7
  442.3 10.4 %custom-call.18 = f32[1,128,128]{1,2,0:T(8,128)} custom-call(f32[1,128,128]{2,1,0:T(8,128)S(1)} %get-tuple-element.26), custom_call_target="InvertDiagBlocksLowerTriangular" | custom-call | tf_op jit(solution)/shard_map/jit(cholesky)/cholesky | solution.py:22
  452.7 0.9 cholesky.119
  453.6 1.0 constant_dynamic-update-slice_fusion.1
  454.6 1.6 convolution_subtract_fusion.4
  456.2 7.2 %cholesky.110 = f32[64,64]{1,0:T(8,128)} custom-call(f32[64,64]{1,0:T(8,128)} %convolution_subtract_fusion.4), custom_call_target="Cholesky" | custom-call | tf_op jit(solution)/shard_map/jit(cholesky)/cholesky | solution.py:22
  463.4 0.8 select_reduce_fusion.1
  464.2 0.6 compare_reduce_fusion
  464.8 1.3 compare_reduce_fusion.1
  467.5 0.0 copy-start.5
  467.5 0.7 copy-done.5
  468.1 0.1 fusion.12
  468.3 19.7 %custom-call.19 = f32[2,128,128]{1,2,0:T(8,128)S(1)} custom-call(f32[2,128,128]{2,1,0:T(8,128)S(1)} %pad_maximum_fusion), custom_call_target="InvertDiagBlocksLowerTriangular" | custom-call | tf_op jit(solution)/shard_map/jit(_cho_solve)/triangular_solve | solution.py:23
  487.9 0.9 fusion.9
  488.9 1.1 convolution_subtract_fusion.2
  490.0 0.3 fusion.18
  490.4 0.2 fusion.17
  490.6 1.1 convolution_subtract_fusion.1
  491.7 0.3 fusion.15
  492.1 2.1 fusion.2
  494.2 6.2 %subtract_convert_fusion = bf16[1024,1024]{1,0:T(8,128)(2,1)} fusion(bf16[1024,1024]{1,0:T(8,128)(2,1)S(1)} %copy-done.2, f32[192,1024]{1,0:T(8,128)S(1)} %fusion.2, f32[192,1024]{1,0:T(8,128)S(1)} %copy-done.4, bf16[192,1024]{1,0:T(8,128)(2,1)} %param.7), kind=kOutput, calls=%fused_computation | convolution fusion | flops 2419458048 | bytes 6160384 | tf_op jit(solution)/shard_map/dot_general | solution.py:30
  500.5 1.1 convolution_subtract_fusion.3
  501.6 5.3 %convolution_subtract_fusion = f32[1024,1024]{1,0:T(8,128)} fusion(f32[1024,1024]{1,0:T(8,128)S(1)} %copy-done.1, f32[192,1024]{1,0:T(8,128)S(1)} %copy-done.3, f32[192,1024]{1,0:T(8,128)S(1)} %fusion.2), kind=kOutput, calls=%fused_computation.1 | convolution fusion | flops 2416967680 | bytes 9961472 | tf_op jit(solution)/shard_map/dot_general | solution.py:27
  (21 shorter events, 0.1 us)
Async XLA Ops:
  7.2 1.0 copy-start
  7.2 168.9 %copy-start.2 = (bf16[1024,1024]{1,0:T(8,128)(2,1)S(1)}, bf16[1024,1024]{1,0:T(8,128)(2,1)}, u32[]{:S(2)}) copy-start(bf16[1024,1024]{1,0:T(8,128)(2,1)} %param.10) | copy-start | bytes 6291460
  7.2 168.8 %all-reduce.7.cloned.1.call-start = ((), (), s32[]{:S(2)}) async-start(), calls=%async_computation | async-start | bytes 1572864 | tf_op jit(solution)/shard_map/psum | solution.py:17
  13.7 249.6 %copy-start.8 = (f32[16,1024]{1,0:T(8,128)S(1)}, f32[16,1024]{1,0:T(8,128)}, u32[]{:S(2)}) copy-start(f32[16,1024]{1,0:T(8,128)} %param.11) | copy-start | bytes 196612
  13.7 247.2 %all-gather.2.cloned.1.call-start = ((), (), s32[]{:S(2)}) async-start(), calls=%async_computation.1 | async-start | bytes 13369344 | tf_op jit(solution)/shard_map/all_gather | solution.py:18
  176.0 250.4 %all-reduce.9.cloned.1.call-start = ((), (), s32[]{:S(2)}) async-start(), calls=%async_computation.2 | async-start | bytes 1966080 | tf_op jit(solution)/shard_map/psum | solution.py:21
  426.4 67.8 %copy-start.4 = (f32[192,1024]{1,0:T(8,128)S(1)}, f32[192,1024]{1,0:T(8,128)}, u32[]{:S(2)}) copy-start(f32[192,1024]{1,0:T(8,128)} %get-tuple-element.24) | copy-start | bytes 2359300
  429.3 0.7 copy-start.6
  441.6 0.6 copy-start.7
  467.5 0.7 copy-start.5
  490.6 9.9 %copy-start.9 = (f32[16,1024]{1,0:T(8,128)S(1)}, f32[16,1024]{1,0:T(8,128)}, u32[]{:S(2)}) copy-start(f32[16,1024]{1,0:T(8,128)} %param.11) | copy-start | bytes 196612
  490.6 9.9 %copy-start.10 = (f32[16,192]{1,0:T(8,128)S(1)}, f32[16,192]{1,0:T(8,128)}, u32[]{:S(2)}) copy-start(f32[16,192]{1,0:T(8,128)} %param.8) | copy-start | bytes 36868
  492.1 9.5 %copy-start.1 = (f32[1024,1024]{1,0:T(8,128)S(1)}, f32[1024,1024]{1,0:T(8,128)}, u32[]{:S(2)}) copy-start(f32[1024,1024]{1,0:T(8,128)} %param.9) | copy-start | bytes 12582916
  492.1 9.5 %copy-start.3 = (f32[192,1024]{1,0:T(8,128)S(1)}, f32[192,1024]{1,0:T(8,128)}, u32[]{:S(2)}) copy-start(f32[192,1024]{1,0:T(8,128)} %all-reduce.7.cloned.1.call-done) | copy-start | bytes 2359300
Sparse Core Ops, SparseCore 0:
  13.8 162.1 all-reduce.6
  177.9 82.9 all-gather.1
  264.4 161.9 all-reduce.8

commit v2 on v1

v2 whole, which is shorter than its diff:
```python
import functools

import jax
import jax.numpy as jnp
from jax import lax
from jax.experimental import pallas as pl
from jax.experimental.pallas import tpu as pltpu
from jax.sharding import PartitionSpec as P

MESH = pl.DeviceIdType.MESH
BF, F32 = jnp.bfloat16, jnp.float32
HIGH = lax.Precision.HIGHEST

STEPS = 192
LOCAL = 1024
OUTS = 16
QUARTER = 256
SLICE = 48
HALF = 96
PIECE = 16
BLOCK = 64
PACKED = 3 * BLOCK + 2 * OUTS
OWNERS = PACKED // PIECE
LANES = 128
NT = (((1,), (1,)), ((), ()))
TN = (((0,), (0,)), ((), ()))
VMEM_LIMIT = 50 * 1024 * 1024


def split2(x):
    hi = x.astype(BF)
    return hi, (x - hi.astype(F32)).astype(BF)


def aligned(start, size):
    return pl.ds(pl.multiple_of(start, size), size)


class Sems:
    def __init__(self):
        self.at = 0

    def take(self, count):
        first = self.at
        self.at += count
        return first


def comm_kernel(
    rates_hbm, targets_hbm, readout_hbm, corr_hbm, rec_hbm,
    cap, gcol, grow, err,
    rates, rates_t, targets, readout, rrow, corr_v, rec_v, h,
    drive_out, drive_hold, drive_relay, drive_sum, drive_x, drive_mid, drive_z, drive_low,
    kpart, krow, ksum, kz, kmid, kx,
    hcore, gone, gy_relay, gy_sum, gy, gtwo, gz, gpiece,
    load_sem, send_sem, recv_sem,
):
    i = lax.axis_index("row")
    j = lax.axis_index("col")
    y, zl, c = i // 4, (i // 2) % 2, i % 2
    x, zh = j // 4, j % 4

    def sigma(z):
        return (z % 2) * 2 + z // 2

    def quarter(q):
        return aligned((q % 4) * QUARTER, QUARTER)

    my_steps = aligned(sigma(zh) * SLICE, SLICE)
    my_quarter = quarter(x)
    row_steps = aligned((c * 2 + zl) * SLICE, SLICE)
    row_quarter = quarter(y)
    half_steps = aligned(c * HALF, HALF)
    sems = Sems()

    def remote(src, dst, at, dev, land=None):
        return pltpu.make_async_remote_copy(
            src_ref=src, dst_ref=dst, send_sem=send_sem.at[at], recv_sem=recv_sem.at[at if land is None else land],
            device_id=dev, device_id_type=MESH,
        )

    def load(src, dst, at):
        copy = pltpu.make_async_copy(src, dst, load_sem.at[at])
        copy.start()
        return copy

    rates_load = load(rates_hbm, rates, 8)
    rec_loads, corr_loads = {}, {}
    for d in (2, 1, 3, 0):
        part = quarter(x + d)
        rec_loads[d] = load(rec_hbm.at[part], rec_v.at[part], d)
    for d in (0, 3, 1, 2):
        part = quarter(x + d)
        corr_loads[d] = load(corr_hbm.at[part], corr_v.at[part], 4 + d)
    readout_load = load(readout_hbm, readout, 9)
    targets_load = load(targets_hbm, targets, 10)

    barrier = pltpu.get_barrier_semaphore()

    def greet(dev):
        pl.semaphore_signal(barrier, inc=1, device_id=dev, device_id_type=MESH)

    @pl.loop(1, 16)
    def _(d):
        greet({"row": (i + d) % 16})

    for d in range(1, 4):
        greet({"col": x * 4 + (zh + d) % 4})
        greet({"col": ((x + d) % 4) * 4 + zh})

    for e in range(4):
        source = x * 4 + e

        @pl.when((source != i) | (i != j))
        def _():
            greet({"row": source, "col": i})

    pl.semaphore_wait(barrier, jnp.where(i == j, 24, 25))

    def z_dev(d):
        return {"col": x * 4 + (zh + d) % 4}

    def x_dev(d):
        return {"col": ((x + d) % 4) * 4 + zh}

    def y_dev(d):
        return {"row": ((y + d) % 4) * 4 + zl * 2 + c}

    sibling = {"row": i + 1 - 2 * c}
    neighbour = {"row": y * 4 + (1 - zl) * 2 + c}

    def swap_each(src, buf, at, act_remote, act_local):
        for z in range(4):
            dst = buf.at[row_steps, row_quarter]
            land = at + zl * 2 + c

            @pl.when((i != j) | (zh != z))
            def _():
                act_remote(remote(src, dst, at + z, {"row": j, "col": y * 4 + z}, land))

            if act_local is not None:

                @pl.when((i == j) & (zh == z))
                def _():
                    act_local(pltpu.make_async_copy(src, dst, recv_sem.at[land]))

    def swap_start(src, buf, at):
        swap_each(src, buf, at, lambda copy: copy.start(), lambda copy: copy.start())

    def swap_wait_send(src, buf, at):
        swap_each(src, buf, at, lambda copy: copy.wait_send(), None)

    def swap_wait_recv(src, buf, at):
        for e in range(4):
            dst = buf.at[aligned(((e % 2) * 2 + e // 2) * SLICE, SLICE), my_quarter]
            source = x * 4 + e

            @pl.when((source != i) | (i != j))
            def _():
                remote(src, dst, at, {"row": source, "col": i}, at + e).wait_recv()

            @pl.when((source == i) & (i == j))
            def _():
                pltpu.make_async_copy(src, dst, recv_sem.at[at + e]).wait()

    def gather_z_start(buf, at):
        for d in range(1, 4):
            mine = buf.at[my_steps, my_quarter]
            remote(mine, mine, at + d - 1, z_dev(d)).start()

    def gather_z_wait(buf, at):
        for d in range(1, 4):
            theirs = buf.at[aligned(sigma((zh + 4 - d) % 4) * SLICE, SLICE), my_quarter]
            copy = remote(theirs, theirs, at + d - 1, z_dev(d))
            copy.wait_recv()
            copy.wait_send()

    class Ring:
        def __init__(self, buf, base, half, me, dev):
            self.buf, self.me, self.dev = buf, me, dev
            self.rows = (aligned(base, half), aligned(base + half, half))
            self.at = sems.take(6)

        def copy(self, k, owner):
            rows = self.rows[(0, 1, 1, 0, 0, 1)[k]]
            block = self.buf.at[rows, quarter(owner)]
            return remote(block, block, self.at + k, self.dev((1, 1, 3, 3, 1, 3)[k]))

        def start(self):
            for k in (0, 2, 1, 3):
                self.copy(k, self.me).start()

        def forward(self):
            self.copy(0, self.me + 3).wait_recv()
            self.copy(4, self.me + 3).start()
            self.copy(2, self.me + 1).wait_recv()
            self.copy(5, self.me + 1).start()

        def wait_sides(self):
            self.copy(1, self.me + 3).wait_recv()
            self.copy(3, self.me + 1).wait_recv()

        def wait_far(self):
            self.copy(4, self.me + 2).wait_recv()
            self.copy(5, self.me + 2).wait_recv()

        def wait_sends(self):
            for k in range(4):
                self.copy(k, self.me).wait_send()
            self.copy(4, self.me + 3).wait_send()
            self.copy(5, self.me + 1).wait_send()

    rates_load.wait()
    r_t = sems.take(4)
    r_src = rates.at[row_steps, row_quarter]
    swap_start(r_src, rrow, r_t)

    d_x = sems.take(6)
    top, low = pl.ds(0, HALF), pl.ds(HALF, HALF)

    def drive_quarter(d):
        rec_loads[d].wait()
        return lax.dot_general(rates[...], rec_v[quarter(x + d), :], NT, preferred_element_type=F32)

    drive_out[0] = drive_quarter(2).astype(BF)
    d_copies = [
        remote(drive_out.at[0, top], drive_relay.at[0], d_x, x_dev(1)),
        remote(drive_out.at[0, low], drive_relay.at[1], d_x + 1, x_dev(3)),
        remote(drive_out.at[1, low], drive_x.at[0], d_x + 2, x_dev(1)),
        remote(drive_out.at[2, top], drive_x.at[1], d_x + 3, x_dev(3)),
        remote(drive_sum.at[0], drive_x.at[2], d_x + 4, x_dev(1)),
        remote(drive_sum.at[1], drive_x.at[3], d_x + 5, x_dev(3)),
    ]
    d_copies[0].start()
    d_copies[1].start()
    part = drive_quarter(1)
    drive_hold[0] = part[:HALF]
    drive_out[1] = part.astype(BF)
    part = drive_quarter(3)
    drive_hold[1] = part[HALF:]
    drive_out[2] = part.astype(BF)

    rates_t[...] = rates[...].T

    swap_wait_recv(r_src, rrow, r_t)
    r_ring = Ring(rrow, 0, HALF, x, x_dev)
    r_ring.start()
    d_copies[2].start()
    d_copies[3].start()

    def corr_quarter(d):
        corr_loads[d].wait()
        hi, lo = split2(corr_v[quarter(x + d), :])
        left = rrow[:, quarter(x + d)]
        return jnp.dot(left, hi, preferred_element_type=F32) + jnp.dot(left, lo, preferred_element_type=F32)

    drive_mid[...] = drive_quarter(0)
    h[...] = corr_quarter(0)
    r_ring.forward()

    d_copies[0].wait_recv()
    drive_sum[0] = (drive_hold[0] + drive_relay[0].astype(F32)).astype(BF)
    d_copies[4].start()
    d_copies[1].wait_recv()
    drive_sum[1] = (drive_hold[1] + drive_relay[1].astype(F32)).astype(BF)
    d_copies[5].start()

    readout_load.wait()
    guess = sum(
        jnp.dot(term, rates_t[...], preferred_element_type=F32) for term in split2(readout[...] * (1.0 / 16.0))
    )
    kpart[3 * BLOCK : 3 * BLOCK + OUTS, :] = guess[:, : 2 * BLOCK]
    kpart[3 * BLOCK + OUTS :, :] = jnp.concatenate([guess[:, 2 * BLOCK :], guess[:, 2 * BLOCK :]], axis=1)

    r_ring.wait_sides()
    h[...] += corr_quarter(3)
    h[...] += corr_quarter(1)
    r_ring.wait_far()
    h[...] += corr_quarter(2)

    g_c = sems.take(1)
    core_copy = remote(h.at[aligned((1 - c) * HALF, HALF)], hcore, g_c, sibling)
    whole = sum(jnp.dot(term, rates_t[...], preferred_element_type=F32) for term in split2(h[...]))
    kb = [[whole[r * BLOCK : (r + 1) * BLOCK, s * BLOCK : (s + 1) * BLOCK] for s in range(3)] for r in range(3)]
    kpart[:BLOCK, :] = jnp.concatenate([kb[0][0], kb[1][1]], axis=1)
    kpart[BLOCK : 2 * BLOCK, :] = jnp.concatenate([kb[2][2], kb[1][0]], axis=1)
    kpart[2 * BLOCK : 3 * BLOCK, :] = jnp.concatenate([kb[2][0], kb[2][1]], axis=1)
    k_r = sems.take(16)

    def k_copy(owner, d):
        return remote(kpart.at[aligned(owner * PIECE, PIECE)], krow.at[d - 1], k_r + d, {"row": owner})

    @pl.loop(1, 16)
    def _(d):
        owner = (i + d) % 16

        @pl.when(owner < OWNERS)
        def _():
            k_copy(owner, d).start()

    core_copy.start()

    for k in (2, 3, 4, 5):
        d_copies[k].wait_recv()
    total = drive_mid[...] + jnp.concatenate(
        [drive_x[2].astype(F32) + drive_x[1].astype(F32), drive_x[0].astype(F32) + drive_x[3].astype(F32)], axis=0
    )
    drive_mid[...] = total
    drive_low[...] = total.astype(BF)
    d_z = sems.take(3)

    def drive_z_copy(d):
        theirs = aligned(sigma((zh + d) % 4) * SLICE, SLICE)
        return remote(drive_low.at[theirs], drive_z.at[d - 1], d_z + d - 1, z_dev(d))

    for d in range(1, 4):
        drive_z_copy(d).start()

    k_z = sems.take(3)
    k_x = sems.take(3)

    @pl.when(i < OWNERS)
    def _():
        @pl.loop(1, 16)
        def _(d):
            remote(kpart.at[pl.ds(0, PIECE)], krow.at[d - 1], k_r + d, {"row": (i + 16 - d) % 16}).wait_recv()

        acc = kpart[aligned(i * PIECE, PIECE), :]
        for d in range(15):
            acc = acc + krow[d]
        ksum[...] = acc
        for d in range(1, 4):
            remote(ksum, kz.at[d - 1], k_z + d - 1, z_dev(d)).start()

    core_copy.wait_recv()
    gone[...] = h[half_steps, :] + hcore[...]
    g_y = sems.take(6)
    upper, lower = pl.ds(0, SLICE), pl.ds(SLICE, SLICE)
    y_copies = [
        remote(gone.at[upper, quarter(y + 2)], gy_relay.at[0], g_y, y_dev(1)),
        remote(gone.at[lower, quarter(y + 2)], gy_relay.at[1], g_y + 1, y_dev(3)),
        remote(gone.at[lower, quarter(y + 1)], gy.at[0], g_y + 2, y_dev(1)),
        remote(gone.at[upper, quarter(y + 3)], gy.at[1], g_y + 3, y_dev(3)),
        remote(gy_sum.at[0], gy.at[2], g_y + 4, y_dev(1)),
        remote(gy_sum.at[1], gy.at[3], g_y + 5, y_dev(3)),
    ]
    for k in range(4):
        y_copies[k].start()

    @pl.when(i < OWNERS)
    def _():
        acc = ksum[...]
        for d in range(1, 4):
            copy = remote(ksum, kz.at[d - 1], k_z + d - 1, z_dev(d))
            copy.wait_recv()
            copy.wait_send()
            acc = acc + kz[d - 1]
        kmid[...] = acc
        for d in range(1, 4):
            remote(kmid, kx.at[d - 1], k_x + d - 1, x_dev(d)).start()

    y_copies[0].wait_recv()
    gy_sum[0] = gone[upper, quarter(y + 1)] + gy_relay[0]
    y_copies[4].start()
    y_copies[1].wait_recv()
    gy_sum[1] = gone[lower, quarter(y + 3)] + gy_relay[1]
    y_copies[5].start()

    k_g = sems.take(16)
    own_rows = aligned(i * PIECE, PIECE)

    @pl.when(i < OWNERS)
    def _():
        acc = kmid[...]
        for d in range(1, 4):
            copy = remote(kmid, kx.at[d - 1], k_x + d - 1, x_dev(d))
            copy.wait_recv()
            copy.wait_send()
            acc = acc + kx[d - 1]
        cap[own_rows, :] = acc

        @pl.loop(1, 16)
        def _(d):
            remote(cap.at[own_rows], cap.at[own_rows], k_g + d, {"row": (i + d) % 16}).start()

    targets_load.wait()
    total = drive_mid[my_steps, :]
    for d in range(1, 4):
        copy = drive_z_copy(d)
        copy.wait_recv()
        copy.wait_send()
        total = total + drive_z[d - 1].astype(F32)
    total = total - targets[my_steps, my_quarter].astype(F32)
    err[my_steps, my_quarter] = total.astype(BF)
    e_z = sems.take(3)
    gather_z_start(err, e_z)

    for k in (2, 3, 4, 5):
        y_copies[k].wait_recv()
    gtwo[upper, :] = gone[upper, row_quarter] + gy[2] + gy[1]
    gtwo[lower, :] = gone[lower, row_quarter] + gy[0] + gy[3]
    g_z = sems.take(1)
    gz_copy = remote(gtwo.at[aligned((1 - zl) * SLICE, SLICE)], gz, g_z, neighbour)
    gz_copy.start()

    gather_z_wait(err, e_z)
    e_ring = Ring(err, 0, HALF, x, x_dev)
    e_ring.start()

    gz_copy.wait_recv()
    piece = gtwo[aligned(zl * SLICE, SLICE), :] + gz[...]
    gcol[row_steps, row_quarter] = piece
    gpiece[...] = piece.astype(BF)
    a_z = sems.take(1)
    mine = gcol.at[row_steps, row_quarter]
    az_copy = remote(mine, mine, a_z, neighbour)
    az_copy.start()
    t_g = sems.take(4)
    swap_start(gpiece, grow, t_g)

    e_ring.forward()

    theirs = gcol.at[aligned((c * 2 + 1 - zl) * SLICE, SLICE), row_quarter]
    remote(theirs, theirs, a_z, neighbour).wait_recv()
    y_ring = Ring(gcol, c * HALF, SLICE, y, y_dev)
    y_ring.start()

    swap_wait_recv(gpiece, grow, t_g)
    g_ring = Ring(grow, 0, HALF, x, x_dev)
    g_ring.start()

    @pl.loop(1, 16)
    def _(d):
        owner = (i + 16 - d) % 16

        @pl.when(owner < OWNERS)
        def _():
            theirs = cap.at[aligned(owner * PIECE, PIECE)]
            remote(theirs, theirs, k_g + d, {"row": owner}).wait_recv()

    y_ring.forward()
    g_ring.forward()
    y_ring.wait_sides()
    y_ring.wait_far()
    a_c = sems.take(1)
    mine = gcol.at[half_steps]
    ac_copy = remote(mine, mine, a_c, sibling)
    ac_copy.start()

    e_ring.wait_sides()
    e_ring.wait_far()
    g_ring.wait_sides()
    g_ring.wait_far()
    theirs = gcol.at[aligned((1 - c) * HALF, HALF)]
    remote(theirs, theirs, a_c, sibling).wait_recv()

    swap_wait_send(r_src, rrow, r_t)
    swap_wait_send(gpiece, grow, t_g)
    for copy in d_copies + y_copies + [core_copy, gz_copy, az_copy, ac_copy]:
        copy.wait_send()
    for ring in (r_ring, e_ring, y_ring, g_ring):
        ring.wait_sends()

    @pl.loop(1, 16)
    def _(d):
        owner = (i + d) % 16

        @pl.when(owner < OWNERS)
        def _():
            k_copy(owner, d).wait_send()

        @pl.when(i < OWNERS)
        def _():
            remote(cap.at[own_rows], cap.at[own_rows], k_g + d, {"row": owner}).wait_send()


N_SEMS = 112


def gather_all(rates, targets, readout, corr, rec):
    vmem = pl.BlockSpec(memory_space=pltpu.VMEM)
    hbm = pl.BlockSpec(memory_space=pl.ANY)
    return pl.pallas_call(
        comm_kernel,
        out_shape=[
            jax.ShapeDtypeStruct((PACKED, LANES), F32),
            jax.ShapeDtypeStruct((STEPS, LOCAL), F32),
            jax.ShapeDtypeStruct((STEPS, LOCAL), BF),
            jax.ShapeDtypeStruct((STEPS, LOCAL), BF),
        ],
        in_specs=[hbm] * 5,
        out_specs=[vmem] * 4,
        scratch_shapes=[
            pltpu.VMEM((STEPS, LOCAL), BF),
            pltpu.VMEM((LOCAL, STEPS), BF),
            pltpu.VMEM((STEPS, LOCAL), BF),
            pltpu.VMEM((OUTS, LOCAL), F32),
            pltpu.VMEM((STEPS, LOCAL), BF),
            pltpu.VMEM((LOCAL, LOCAL), F32),
            pltpu.VMEM((LOCAL, LOCAL), BF),
            pltpu.VMEM((STEPS, LOCAL), F32),
            pltpu.VMEM((3, STEPS, QUARTER), BF),
            pltpu.VMEM((2, HALF, QUARTER), F32),
            pltpu.VMEM((2, HALF, QUARTER), BF),
            pltpu.VMEM((2, HALF, QUARTER), BF),
            pltpu.VMEM((4, HALF, QUARTER), BF),
            pltpu.VMEM((STEPS, QUARTER), F32),
            pltpu.VMEM((3, SLICE, QUARTER), BF),
            pltpu.VMEM((STEPS, QUARTER), BF),
            pltpu.VMEM((PACKED, LANES), F32),
            pltpu.VMEM((15, PIECE, LANES), F32),
            pltpu.VMEM((PIECE, LANES), F32),
            pltpu.VMEM((3, PIECE, LANES), F32),
            pltpu.VMEM((PIECE, LANES), F32),
            pltpu.VMEM((3, PIECE, LANES), F32),
            pltpu.VMEM((HALF, LOCAL), F32),
            pltpu.VMEM((HALF, LOCAL), F32),
            pltpu.VMEM((2, SLICE, QUARTER), F32),
            pltpu.VMEM((2, SLICE, QUARTER), F32),
            pltpu.VMEM((4, SLICE, QUARTER), F32),
            pltpu.VMEM((HALF, QUARTER), F32),
            pltpu.VMEM((SLICE, QUARTER), F32),
            pltpu.VMEM((SLICE, QUARTER), BF),
            pltpu.SemaphoreType.DMA((11,)),
            pltpu.SemaphoreType.DMA((N_SEMS,)),
            pltpu.SemaphoreType.DMA((N_SEMS,)),
        ],
        compiler_params=pltpu.CompilerParams(
            collective_id=0, has_side_effects=True, vmem_limit_bytes=VMEM_LIMIT
        ),
        name="exchange",
    )(rates, targets, readout, corr, rec)


SUBS = 8
WIDE = 4


def reciprocal(v):
    r = pl.reciprocal(v, approx=True)
    r = r * (2.0 - v * r)
    return r * (2.0 - v * r)


def factor_two(a, b, d):
    ra = reciprocal(a)
    return b * ra, ra, a * reciprocal(a * d - b * b)


def factor_four(s):
    l = [[None] * WIDE for _ in range(WIDE)]
    l[1][0], rd0, rd1 = factor_two(s[0][0], s[1][0], s[1][1])
    c = {}
    for r in (2, 3):
        l[r][0] = s[r][0] * rd0
        c[r] = s[r][1] - l[1][0] * s[r][0]
        l[r][1] = c[r] * rd1

    def left(r, t):
        return s[r][t] - (l[r][0] * s[t][0] + l[r][1] * c[t])

    l[3][2], rd2, rd3 = factor_two(left(2, 2), left(3, 2), left(3, 3))
    return l, (rd0, rd1, rd2, rd3)


def eliminate(l, v):
    v1 = v[1] - l[1][0] * v[0]
    v2 = v[2] - l[2][0] * v[0] - l[2][1] * v1
    v3 = v[3] - l[3][0] * v[0] - l[3][1] * v1 - l[3][2] * v2
    return v[0], v1, v2, v3


def inverse_block(a):
    rows = [a[u * SUBS : (u + 1) * SUBS] for u in range(BLOCK // SUBS)]
    shape = (SUBS, BLOCK)
    lane = lax.broadcasted_iota(jnp.int32, shape, 1)
    sub = lax.broadcasted_iota(jnp.int32, shape, 0)
    for k in range(0, BLOCK, WIDE):
        v, first = k // SUBS, k % SUBS
        span = range(WIDE)
        col = [[jnp.broadcast_to(row[:, k + b : k + b + 1], shape) for row in rows] for b in span]
        s = [[jnp.broadcast_to(col[b][v][first + a : first + a + 1], shape) for b in range(a + 1)] for a in span]
        inside = (lane >= k) & (lane < k + WIDE)
        top = [
            jnp.where(inside, jnp.where(lane == k + b, 1.0, 0.0), jnp.broadcast_to(rows[v][first + b : first + b + 1], shape))
            for b in span
        ]
        l, rd = factor_four(s)
        top = eliminate(l, top)
        new = [None] * WIDE
        for a in reversed(span):
            new[a] = rd[a] * top[a]
            for b in range(a + 1, WIDE):
                new[a] = new[a] - l[b][a] * new[b]
        for u in range(len(rows)):
            m = eliminate(l, [col[b][u] for b in span])
            drop = ((m[0] * rd[0]) * top[0] + (m[1] * rd[1]) * top[1]) + ((m[2] * rd[2]) * top[2] + (m[3] * rd[3]) * top[3])
            rows[u] = jnp.where(inside, 0.0, rows[u]) - drop
        for a in span:
            rows[v] = jnp.where(sub == first + a, new[a], rows[v])
    return jnp.concatenate(rows, axis=0)


def dot32(a, b):
    return jnp.dot(a, b, precision=HIGH, preferred_element_type=F32)


def update_kernel(
    cap, gcol, grow, err, goal, readout, corr, rec, corr_out, rec_out, readout_out,
    minv, d_hi, d_lo,
):
    @pl.when(pl.program_id(0) == 0)
    def _():
        blocks = range(STEPS // BLOCK)
        eye = jnp.where(
            lax.broadcasted_iota(jnp.int32, (BLOCK, BLOCK), 0) == lax.broadcasted_iota(jnp.int32, (BLOCK, BLOCK), 1),
            1.0, 0.0,
        )
        packed = [
            [cap[r * BLOCK : (r + 1) * BLOCK, :BLOCK], cap[r * BLOCK : (r + 1) * BLOCK, BLOCK:]] for r in blocks
        ]
        (k00, k11), (k22, k10), (k20, k21) = packed
        a = [[k00 + eye, k10.T, k20.T], [k10, k11 + eye, k21.T], [k20, k21, k22 + eye]]
        for k in blocks:
            inv = inverse_block(a[k][k])
            new = [[None] * len(blocks) for _ in blocks]
            new[k][k] = inv
            for s in blocks:
                if s != k:
                    new[k][s] = dot32(inv, a[k][s])
            for r in blocks:
                if r != k:
                    new[r][k] = -dot32(a[r][k], inv)
                    for s in blocks:
                        if s != k:
                            new[r][s] = a[r][s] - dot32(a[r][k], new[k][s])
            a = new
        for r in blocks:
            for s in blocks:
                minv[r * BLOCK : (r + 1) * BLOCK, s * BLOCK : (s + 1) * BLOCK] = a[r][s]
        scaled = dot32(minv[...], gcol[...])
        hi, lo = split2(scaled)
        d_hi[...] = hi
        d_lo[...] = lo
        guess = jnp.concatenate(
            [cap[3 * BLOCK : 3 * BLOCK + OUTS, :], cap[3 * BLOCK + OUTS :, :BLOCK]], axis=1
        )
        readout_out[...] = readout[...] - dot32(guess - goal[...], scaled)

    def times(left):
        return lax.dot_general(left, d_hi[...], TN, preferred_element_type=F32) + lax.dot_general(
            left, d_lo[...], TN, preferred_element_type=F32
        )

    corr_out[...] = corr[...] - times(grow[...])
    rec_out[...] = (rec[...].astype(F32) - times(err[...])).astype(BF)


TILE = 128


def update(cap, gcol, grow, err, goal, readout, corr, rec):
    def whole(shape):
        return pl.BlockSpec(shape, lambda g: (0, 0))

    rows = pl.BlockSpec((TILE, LOCAL), lambda g: (g, 0))
    left = pl.BlockSpec((STEPS, TILE), lambda g: (0, g))
    return pl.pallas_call(
        update_kernel,
        grid=(LOCAL // TILE,),
        out_shape=[
            jax.ShapeDtypeStruct((LOCAL, LOCAL), F32),
            jax.ShapeDtypeStruct((LOCAL, LOCAL), BF),
            jax.ShapeDtypeStruct((OUTS, LOCAL), F32),
        ],
        in_specs=[
            whole((PACKED, LANES)), whole((STEPS, LOCAL)), left, left, whole((OUTS, STEPS)), whole((OUTS, LOCAL)),
            rows, rows,
        ],
        out_specs=[rows, rows, whole((OUTS, LOCAL))],
        scratch_shapes=[
            pltpu.VMEM((STEPS, STEPS), F32),
            pltpu.VMEM((STEPS, LOCAL), BF),
            pltpu.VMEM((STEPS, LOCAL), BF),
        ],
        compiler_params=pltpu.CompilerParams(vmem_limit_bytes=VMEM_LIMIT),
        name="update",
    )(cap, gcol, grow, err, goal, readout, corr, rec)


def on_device(rates, targets, goal, corr, rec, readout):
    cap, gcol, grow, err = gather_all(rates, targets, readout, corr, rec)
    return tuple(update(cap, gcol, grow, err, goal, readout, corr, rec))


def solution(mesh):
    placed = (P(None, "col"), P(None, "row"), P(), P("row", "col"), P("row", "col"), P(None, "col"))
    return jax.shard_map(
        on_device,
        mesh=mesh,
        in_specs=placed,
        out_specs=(P("row", "col"), P("row", "col"), P(None, "col")),
        check_vma=False,
    )
```

time: 523 us -> 86.8 us (0.17); the launches traced: 513 us -> 86.5 us
  waiting for transfers between devices: 336 us -> 0 us
  Pallas kernels: 0 us -> 82.9 us
  blocking collectives: 70.5 us -> 0 us
  other arithmetic: 55.9 us -> 0 us
  matrix products: 31.4 us -> 0 us
  between operations: 15.3 us -> 0.67 us
    psum x2 -> x0, waiting for transfers between devices: 253 us -> none  [the longest x1 162 us: on_device(): lax.psum((prod_part, drive_part, guess_part), 'col')]
    all_gather x1 -> x0, waiting for transfers between devices: 83.1 us -> none  [on_device(): gathered = lax.all_gather(prod_rows, 'row', axis=1, tiled=True)]
    pallas_call x0 -> x2, Pallas kernels: none -> 82.9 us  [the longest x1 62.9 us: gather_all(): pl.pallas_call(comm_kernel, out_shape=[jax.ShapeDtypeStruct((PACKED, LANE...]
    psum x1 -> x0, blocking collectives: 70.5 us -> none  [on_device(): lax.psum((prod_part, drive_part, guess_part), 'col')]
    another operation x13 -> x0, other arithmetic: 52.5 us -> none  [the longest x7 32.7 us: on_device(): factor = jnp.linalg.cholesky(capacity)]
    dot_general x8 -> x0, matrix products: 24.7 us -> none  [the longest x1 6.22 us: on_device(): jnp.dot(err_j.T, scaled, precision=high)]
    another operation x8 -> x0, matrix products: 6.7 us -> none  [the longest x6 4.09 us: on_device(): cinverse = jax.scipy.linalg.cho_solve((factor, True), eye)]
  transfers between devices with their start and end apart: 3 -> 0, of which waited for: 3 -> 0; matrix products, arithmetic and copies ran while one was open for 1% -> 0% of each run, Pallas kernels for 0% -> 0%
where the time goes in v2:
time: 86.8 us; the launch traced here: 86.5 us
  Pallas kernels  82.9 us (96%)
  local copies, waits for them, and re-layouts  2.98 us (3%)
    pallas_call x1, Pallas kernels, gather_all(): pl.pallas_call(comm_kernel, out_shape=[jax.ShapeDtypeStruct((PACKED, LANE...  62.9 us
    pallas_call x1, Pallas kernels, update(): pl.pallas_call(update_kernel, grid=(LOCAL // TILE,), out_shape=[jax.Shape...  20 us
    unnamed x10, local copies, waits for them, and re-layouts  2.98 us

profile of v2, /device:TPU:1, one launch (start us, length us, event | category | flops | bytes accessed | tf_op | source)
XLA Modules:
  0.0 86.5 jit_solution(15485840072742687534)
XLA Ops:
  0.6 0.0 copy-start
  0.6 0.0 copy-start.1
  0.7 1.1 %copy-done.1 = bf16[192,1024]{1,0:T(8,128)(2,1)S(1)} copy-done((bf16[192,1024]{1,0:T(8,128)(2,1)S(1)}, bf16[192,1024]{1,0:T(8,128)(2,1)}, u32[]{:S(2)}) %copy-start.1) | copy-done | bytes 393240
  1.8 0.0 copy-start.2
  1.8 1.0 %copy-done.2 = bf16[192,1024]{1,0:T(8,128)(2,1)S(1)} copy-done((bf16[192,1024]{1,0:T(8,128)(2,1)S(1)}, bf16[192,1024]{1,0:T(8,128)(2,1)}, u32[]{:S(2)}) %copy-start.2) | copy-done | bytes 393240
  2.8 0.0 copy-start.3
  2.8 0.8 copy-done.3
  3.6 0.0 copy-start.4
  3.6 62.9 %exchange.1 = (f32[224,128]{1,0:T(8,128)S(1)}, f32[192,1024]{1,0:T(8,128)S(1)}, bf16[192,1024]{1,0:T(8,128)(2,1)S(1)}, bf16[192,1024]{1,0:T(8,128)(2,1)S(1)}) custom-call(bf16[192,1024]{1,0:T(8,128)(2,1)S(1)} %copy-done.1, bf16[192,1024]{1,0:T(8,128)(2,1)S(1)} %copy-done.2, f32[16,1024]{1,0:T(8,128)S(1)} %copy-done.3, f32[1024,1024]{1,0:T(8,128)} %corr.1, ...), custom_call_target="tpu_custom_call" | custom-call | tf_op jit(solution)/shard_map/exchange/pallas_call | solution.py:483
  66.5 0.0 copy-done
  66.5 0.0 copy-done.4
  66.5 20.0 %update.1 = (f32[1024,1024]{1,0:T(8,128)}, bf16[1024,1024]{1,0:T(8,128)(2,1)}, f32[16,1024]{1,0:T(8,128)}) custom-call(f32[224,128]{1,0:T(8,128)S(1)} %get-tuple-element.7.cap, f32[192,1024]{1,0:T(8,128)S(1)} %get-tuple-element.8.gcol, bf16[192,1024]{1,0:T(8,128)(2,1)S(1)} %get-tuple-element.9.grow, bf16[192,1024]{1,0:T(8,128)(2,1)S(1)} %get-tuple-element.10.err, ...), custom_call_target="tpu_custom_call" | custom-call | tf_op jit(solution)/shard_map/update/pallas_call | solution.py:668
Async XLA Ops:
  0.6 65.9 %copy-start = (bf16[1024,1024]{1,0:T(8,128)(2,1)S(1)}, bf16[1024,1024]{1,0:T(8,128)(2,1)}, u32[]{:S(2)}) copy-start(bf16[1024,1024]{1,0:T(8,128)(2,1)} %rec.1) | copy-start | bytes 6291460
  0.6 1.1 %copy-start.1 = (bf16[192,1024]{1,0:T(8,128)(2,1)S(1)}, bf16[192,1024]{1,0:T(8,128)(2,1)}, u32[]{:S(2)}) copy-start(bf16[192,1024]{1,0:T(8,128)(2,1)} %rates_hbm.1) | copy-start | bytes 1179652
  1.8 1.0 %copy-start.2 = (bf16[192,1024]{1,0:T(8,128)(2,1)S(1)}, bf16[192,1024]{1,0:T(8,128)(2,1)}, u32[]{:S(2)}) copy-start(bf16[192,1024]{1,0:T(8,128)(2,1)} %targets_hbm.1) | copy-start | bytes 1179652
  2.8 0.8 copy-start.3
  3.6 62.9 %copy-start.4 = (f32[16,192]{1,0:T(8,128)S(1)}, f32[16,192]{1,0:T(8,128)}, u32[]{:S(2)}) copy-start(f32[16,192]{1,0:T(8,128)} %goal.1) | copy-start | bytes 36868

commit v3 on v1

v3 whole, which is shorter than its diff:
```python
import functools

import jax
import jax.numpy as jnp
from jax import lax
from jax.experimental import pallas as pl
from jax.experimental.pallas import tpu as pltpu
from jax.sharding import PartitionSpec as P

MESH = pl.DeviceIdType.MESH
BF, F32 = jnp.bfloat16, jnp.float32
HIGH = lax.Precision.HIGHEST

STEPS = 192
LOCAL = 1024
OUTS = 16
QUARTER = 256
GROUP = 64
PIECE = 16
BLOCK = 64
PACKED = 3 * BLOCK + 2 * OUTS
OWNERS = PACKED // PIECE
LANES = 128
FOLDED = GROUP * STEPS // LANES
NT = (((1,), (1,)), ((), ()))
VMEM_LIMIT = 60 * 1024 * 1024


def split2(x):
    hi = x.astype(BF)
    return hi, (x - hi.astype(F32)).astype(BF)


def aligned(start, size):
    return pl.ds(pl.multiple_of(start, size), size)


def fold(v):
    low = jnp.concatenate([v[: GROUP // 2, LANES:], v[GROUP // 2 :, LANES:]], axis=1)
    return jnp.concatenate([v[:, :LANES], low], axis=0)


def unfold(v):
    rest = STEPS - LANES
    high = jnp.concatenate([v[GROUP:, :rest], v[GROUP:, rest:]], axis=0)
    return jnp.concatenate([v[:GROUP], high], axis=1)


def groups(v):
    return [v[g * GROUP : (g + 1) * GROUP] for g in range(v.shape[0] // GROUP)]


class Sems:
    def __init__(self):
        self.at = 0

    def take(self, count):
        first = self.at
        self.at += count
        return first


SUBS = 8
WIDE = 4


def reciprocal(v):
    r = pl.reciprocal(v, approx=True)
    r = r * (2.0 - v * r)
    return r * (2.0 - v * r)


def factor_two(a, b, d):
    ra = reciprocal(a)
    return b * ra, ra, a * reciprocal(a * d - b * b)


def factor_four(s):
    l = [[None] * WIDE for _ in range(WIDE)]
    l[1][0], rd0, rd1 = factor_two(s[0][0], s[1][0], s[1][1])
    c = {}
    for r in (2, 3):
        l[r][0] = s[r][0] * rd0
        c[r] = s[r][1] - l[1][0] * s[r][0]
        l[r][1] = c[r] * rd1

    def left(r, t):
        return s[r][t] - (l[r][0] * s[t][0] + l[r][1] * c[t])

    l[3][2], rd2, rd3 = factor_two(left(2, 2), left(3, 2), left(3, 3))
    return l, (rd0, rd1, rd2, rd3)


def eliminate(l, v):
    v1 = v[1] - l[1][0] * v[0]
    v2 = v[2] - l[2][0] * v[0] - l[2][1] * v1
    v3 = v[3] - l[3][0] * v[0] - l[3][1] * v1 - l[3][2] * v2
    return v[0], v1, v2, v3


def inverse_block(a, services):
    rows = [a[u * SUBS : (u + 1) * SUBS] for u in range(BLOCK // SUBS)]
    shape = (SUBS, BLOCK)
    lane = lax.broadcasted_iota(jnp.int32, shape, 1)
    sub = lax.broadcasted_iota(jnp.int32, shape, 0)
    for k in range(0, BLOCK, WIDE):
        v, first = k // SUBS, k % SUBS
        span = range(WIDE)
        col = [[jnp.broadcast_to(row[:, k + b : k + b + 1], shape) for row in rows] for b in span]
        s = [[jnp.broadcast_to(col[b][v][first + a : first + a + 1], shape) for b in range(a + 1)] for a in span]
        inside = (lane >= k) & (lane < k + WIDE)
        top = [
            jnp.where(inside, jnp.where(lane == k + b, 1.0, 0.0), jnp.broadcast_to(rows[v][first + b : first + b + 1], shape))
            for b in span
        ]
        l, rd = factor_four(s)
        top = eliminate(l, top)
        new = [None] * WIDE
        for a in reversed(span):
            new[a] = rd[a] * top[a]
            for b in range(a + 1, WIDE):
                new[a] = new[a] - l[b][a] * new[b]
        for u in range(len(rows)):
            m = eliminate(l, [col[b][u] for b in span])
            drop = ((m[0] * rd[0]) * top[0] + (m[1] * rd[1]) * top[1]) + ((m[2] * rd[2]) * top[2] + (m[3] * rd[3]) * top[3])
            rows[u] = jnp.where(inside, 0.0, rows[u]) - drop
        for a in span:
            rows[v] = jnp.where(sub == first + a, new[a], rows[v])
        if k % (4 * WIDE) == 3 * WIDE:
            for serve in services:
                serve()
                break
    return jnp.concatenate(rows, axis=0)


def dot32(a, b):
    return jnp.dot(a, b, precision=HIGH, preferred_element_type=F32)


def invert(cap, minv, services):
    blocks = range(STEPS // BLOCK)
    shape = (BLOCK, BLOCK)
    eye = jnp.where(lax.broadcasted_iota(jnp.int32, shape, 0) == lax.broadcasted_iota(jnp.int32, shape, 1), 1.0, 0.0)
    (k00, k11), (k22, k10), (k20, k21) = [
        [cap[r * BLOCK : (r + 1) * BLOCK, :BLOCK], cap[r * BLOCK : (r + 1) * BLOCK, BLOCK:]] for r in blocks
    ]
    a = [[k00 + eye, k10.T, k20.T], [k10, k11 + eye, k21.T], [k20, k21, k22 + eye]]
    for k in blocks:
        inv = inverse_block(a[k][k], services)
        new = [[None] * len(blocks) for _ in blocks]
        new[k][k] = inv
        for s in blocks:
            if s != k:
                new[k][s] = dot32(inv, a[k][s])
        for r in blocks:
            if r != k:
                new[r][k] = -dot32(a[r][k], inv)
                for s in blocks:
                    if s != k:
                        new[r][s] = a[r][s] - dot32(a[r][k], new[k][s])
        a = new
    for r in blocks:
        for s in blocks:
            minv[r * BLOCK : (r + 1) * BLOCK, s * BLOCK : (s + 1) * BLOCK] = a[r][s]


def comm_kernel(
    rates_hbm, targets_hbm, readout_hbm, corr_hbm, rec_hbm,
    minv_out, guess_out, gcol_out, left_out,
    rates, rates_t, targets, readout, rx, corr_v, rec_v,
    g_part, g_mid, g_relay, g_sum, g_x, g_z, g_piece, g_all, g_col,
    e_part, e_hold, e_mid, e_relay, e_sum, e_x, e_low, e_z, left,
    kpart, krow, ksum, kz, kmid, kx, cap, minv,
    load_sem, store_sem, send_sem, recv_sem,
):
    i = lax.axis_index("row")
    j = lax.axis_index("col")
    y, zl, c = i // 4, (i // 2) % 2, i % 2
    x, zh = j // 4, j % 4
    sems = Sems()

    def quarter(q):
        return aligned((q % 4) * QUARTER, QUARTER)

    def remote(src, dst, at, dev, land=None):
        return pltpu.make_async_remote_copy(
            src_ref=src, dst_ref=dst, send_sem=send_sem.at[at], recv_sem=recv_sem.at[at if land is None else land],
            device_id=dev, device_id_type=MESH,
        )

    def load(src, dst, at):
        copy = pltpu.make_async_copy(src, dst, load_sem.at[at])
        copy.start()
        return copy

    rates_load = load(rates_hbm, rates, 8)
    rec_loads, corr_loads = {}, {}
    for d in (2, 1, 3, 0):
        part = quarter(x + d)
        corr_loads[d] = load(corr_hbm.at[part], corr_v.at[part], 4 + d)
    for d in (2, 1, 3, 0):
        part = quarter(x + d)
        rec_loads[d] = load(rec_hbm.at[part], rec_v.at[part], d)
    readout_load = load(readout_hbm, readout, 9)
    targets_load = load(targets_hbm, targets, 10)

    barrier = pltpu.get_barrier_semaphore()

    def greet(dev):
        pl.semaphore_signal(barrier, inc=1, device_id=dev, device_id_type=MESH)

    @pl.loop(1, 16)
    def _(d):
        greet({"row": (i + d) % 16})

    for d in range(1, 4):
        greet({"col": x * 4 + (zh + d) % 4})
        greet({"col": ((x + d) % 4) * 4 + zh})

    for z in range(4):

        @pl.when((i != j) | (zh != z))
        def _():
            greet({"row": j, "col": y * 4 + z})

    rates_load.wait()
    rates_t[...] = rates[...].T
    pl.semaphore_wait(barrier, jnp.where(i == j, 24, 25))

    def z_dev(d):
        return {"col": x * 4 + (zh + d) % 4}

    def x_dev(d):
        return {"col": ((x + d) % 4) * 4 + zh}

    def y_dev(d):
        return {"row": ((y + d) % 4) * 4 + zl * 2 + c}

    class RingSum:
        def __init__(self, part, hold, relay, total, landed):
            self.part, self.hold, self.relay, self.total, self.landed = part, hold, relay, total, landed
            at = sems.take(6)
            top, low = pl.ds(0, 2), pl.ds(2, 2)
            self.copies = [
                remote(part.at[0, top], relay.at[0], at, x_dev(1)),
                remote(part.at[0, low], relay.at[1], at + 1, x_dev(3)),
                remote(part.at[1, low], landed.at[0], at + 2, x_dev(1)),
                remote(part.at[2, top], landed.at[1], at + 3, x_dev(3)),
                remote(total.at[0], landed.at[2], at + 4, x_dev(1)),
                remote(total.at[1], landed.at[3], at + 5, x_dev(3)),
            ]

        def start(self, *which):
            for k in which:
                self.copies[k].start()

        def forward(self):
            for k in range(2):
                self.copies[k].wait_recv()
                self.total[k] = (self.hold(k) + self.relay[k].astype(F32)).astype(self.total.dtype)
                self.copies[4 + k].start()

        def finish(self, own):
            for k in range(2, 6):
                self.copies[k].wait_recv()
            got = [self.landed[k].astype(F32) for k in range(4)]
            own[:2] = own[:2] + got[2] + got[1]
            own[2:] = own[2:] + got[0] + got[3]

        def wait_sends(self):
            for copy in self.copies:
                copy.wait_send()

    class Ring:
        def __init__(self, block, me, dev):
            self.block, self.me, self.dev = block, me, dev
            self.at = sems.take(6)

        def copy(self, k, owner):
            block = self.block((0, 1, 1, 0, 0, 1)[k], owner % 4)
            return remote(block, block, self.at + k, self.dev((1, 1, 3, 3, 1, 3)[k]))

        def start(self):
            for k in (0, 2, 1, 3):
                self.copy(k, self.me).start()

        def forward(self):
            self.copy(0, self.me + 3).wait_recv()
            self.copy(4, self.me + 3).start()
            self.copy(2, self.me + 1).wait_recv()
            self.copy(5, self.me + 1).start()

        def finish(self):
            self.copy(1, self.me + 3).wait_recv()
            self.copy(3, self.me + 1).wait_recv()
            self.copy(4, self.me + 2).wait_recv()
            self.copy(5, self.me + 2).wait_recv()

        def wait_sends(self):
            for k in range(4):
                self.copy(k, self.me).wait_send()
            self.copy(4, self.me + 3).wait_send()
            self.copy(5, self.me + 1).wait_send()

    def prod_quarter(d, out):
        corr_loads[d].wait()
        hi, lo = split2(corr_v[quarter(x + d), :])
        value = jnp.dot(hi, rates_t[...], preferred_element_type=F32) + jnp.dot(
            lo, rates_t[...], preferred_element_type=F32
        )
        for g, part in enumerate(groups(value)):
            out[g] = fold(part)

    def drive_quarter(d):
        rec_loads[d].wait()
        value = jnp.dot(rec_v[quarter(x + d), :], rates_t[...], preferred_element_type=F32)
        return [fold(part) for part in groups(value)]

    g_ring = RingSum(g_part, lambda k: g_part[1, :2] if k == 0 else g_part[2, 2:], g_relay, g_sum, g_x)
    prod_quarter(2, g_part.at[0])
    g_ring.start(0, 1)
    prod_quarter(1, g_part.at[1])
    g_ring.start(2)
    prod_quarter(3, g_part.at[2])
    g_ring.start(3)

    r_t = sems.take(1)
    r_src = rates.at[:, quarter(y)]

    @pl.when(i != j)
    def _():
        remote(r_src, rx, r_t, {"row": j, "col": i}).start()

    @pl.when(i == j)
    def _():
        pltpu.make_async_copy(r_src, rx, recv_sem.at[r_t]).start()

    prod_quarter(0, g_mid)
    g_ring.forward()

    e_ring = RingSum(e_part, lambda k: e_hold[k], e_relay, e_sum, e_x)
    for g, part in enumerate(drive_quarter(2)):
        e_part[0, g] = part.astype(BF)
    e_ring.start(0, 1)
    for g, part in enumerate(drive_quarter(1)):
        if g < 2:
            e_hold[0, g] = part
        else:
            e_part[1, g] = part.astype(BF)
    e_ring.start(2)
    for g, part in enumerate(drive_quarter(3)):
        if g < 2:
            e_part[2, g] = part.astype(BF)
        else:
            e_hold[1, g - 2] = part
    e_ring.start(3)

    readout_load.wait()
    guess = sum(
        jnp.dot(term, rates_t[...], preferred_element_type=F32) for term in split2(readout[...] * (1.0 / 16.0))
    )
    kpart[3 * BLOCK : 3 * BLOCK + OUTS, :] = guess[:, :LANES]
    kpart[3 * BLOCK + OUTS :, :] = jnp.concatenate([guess[:, LANES:], guess[:, LANES:]], axis=1)

    g_ring.finish(g_mid)
    g_at = sems.take(3)

    def g_z_copy(d):
        return remote(g_mid.at[(zh + d) % 4], g_z.at[d - 1], g_at + d - 1, z_dev(d))

    for d in range(1, 4):
        g_z_copy(d).start()

    @pl.when(i != j)
    def _():
        remote(r_src, rx, r_t, {"row": j, "col": i}).wait_recv()

    @pl.when(i == j)
    def _():
        pltpu.make_async_copy(r_src, rx, recv_sem.at[r_t]).wait()

    whole = sum(
        jnp.dot(rx[...], term, preferred_element_type=F32)
        for term in split2(jnp.concatenate([unfold(g_mid[g]) for g in range(4)], axis=0))
    )
    kb = [[whole[r * BLOCK : (r + 1) * BLOCK, s * BLOCK : (s + 1) * BLOCK] for s in range(3)] for r in range(3)]
    kpart[:BLOCK, :] = jnp.concatenate([kb[0][0], kb[1][1]], axis=1)
    kpart[BLOCK : 2 * BLOCK, :] = jnp.concatenate([kb[2][2], kb[1][0]], axis=1)
    kpart[2 * BLOCK : 3 * BLOCK, :] = jnp.concatenate([kb[2][0], kb[2][1]], axis=1)

    k_r = sems.take(16)

    def k_copy(owner, d):
        return remote(kpart.at[aligned(owner * PIECE, PIECE)], krow.at[d - 1], k_r + d, {"row": owner})

    @pl.loop(1, 16)
    def _(d):
        owner = (i + d) % 16

        @pl.when(owner < OWNERS)
        def _():
            k_copy(owner, d).start()

    e_ring.forward()
    for g, part in enumerate(drive_quarter(0)):
        e_mid[g] = part

    k_z = sems.take(3)
    k_x = sems.take(3)

    @pl.when(i < OWNERS)
    def _():
        @pl.loop(1, 16)
        def _(d):
            remote(kpart.at[pl.ds(0, PIECE)], krow.at[d - 1], k_r + d, {"row": (i + 16 - d) % 16}).wait_recv()

        acc = kpart[aligned(i * PIECE, PIECE), :]
        for d in range(15):
            acc = acc + krow[d]
        ksum[...] = acc
        for d in range(1, 4):
            remote(ksum, kz.at[d - 1], k_z + d - 1, z_dev(d)).start()

    for d in range(1, 4):
        g_z_copy(d).wait_recv()
    piece = g_mid[zh] + g_z[0] + g_z[1] + g_z[2]
    g_piece[...] = piece
    own = aligned(x * QUARTER + zh * GROUP, GROUP)
    left[own, STEPS:] = unfold(piece).astype(BF)
    s_t = sems.take(4)

    def swap_each(act_remote, act_local):
        for e in range(4):
            dst = g_all.at[x * 4 + zh]

            @pl.when((i != j) | (i % 4 != e))
            def _():
                act_remote(remote(g_piece, dst, s_t + e, {"row": x * 4 + e, "col": i}, s_t + zh))

            if act_local is not None:

                @pl.when((i == j) & (i % 4 == e))
                def _():
                    act_local(pltpu.make_async_copy(g_piece, dst, recv_sem.at[s_t + zh]))

    swap_each(lambda copy: copy.start(), lambda copy: copy.start())

    e_ring.finish(e_mid)
    e_low[...] = e_mid[...].astype(BF)
    e_at = sems.take(3)

    def e_z_copy(d):
        return remote(e_low.at[(zh + d) % 4], e_z.at[d - 1], e_at + d - 1, z_dev(d))

    for d in range(1, 4):
        e_z_copy(d).start()

    @pl.when(i < OWNERS)
    def _():
        acc = ksum[...]
        for d in range(1, 4):
            copy = remote(ksum, kz.at[d - 1], k_z + d - 1, z_dev(d))
            copy.wait_recv()
            copy.wait_send()
            acc = acc + kz[d - 1]
        kmid[...] = acc
        for d in range(1, 4):
            remote(kmid, kx.at[d - 1], k_x + d - 1, x_dev(d)).start()

    targets_load.wait()
    aims = targets[:, quarter(x)].T
    e_hold[0] = jnp.stack([fold(part) for part in groups(aims[:LANES].astype(F32))])
    e_hold[1] = jnp.stack([fold(part) for part in groups(aims[LANES:].astype(F32))])

    k_g = sems.take(16)
    own_rows = aligned(i * PIECE, PIECE)

    @pl.when(i < OWNERS)
    def _():
        acc = kmid[...]
        for d in range(1, 4):
            copy = remote(kmid, kx.at[d - 1], k_x + d - 1, x_dev(d))
            copy.wait_recv()
            copy.wait_send()
            acc = acc + kx[d - 1]
        cap[own_rows, :] = acc

        @pl.loop(1, 16)
        def _(d):
            remote(cap.at[own_rows], cap.at[own_rows], k_g + d, {"row": (i + d) % 16}).start()

    for d in range(1, 4):
        e_z_copy(d).wait_recv()
    total = e_mid[zh] - e_hold[zh // 2, zh % 2]
    for d in range(3):
        total = total + e_z[d].astype(F32)
    left[own, :STEPS] = unfold(total).astype(BF)
    l_z = sems.take(3)

    def l_z_copy(d, z):
        rows = left.at[aligned(x * QUARTER + (z % 4) * GROUP, GROUP)]
        return remote(rows, rows, l_z + d - 1, z_dev(d))

    for d in range(1, 4):
        l_z_copy(d, zh).start()

    for z in range(4):
        dst = g_all.at[y * 4 + z]

        @pl.when((i != j) | (zh != z))
        def _():
            remote(g_piece, dst, s_t, {"row": j, "col": y * 4 + z}, s_t + z).wait_recv()

        @pl.when((i == j) & (zh == z))
        def _():
            pltpu.make_async_copy(g_piece, dst, recv_sem.at[s_t + z]).wait()

    y_ring = Ring(lambda half, owner: g_all.at[pl.ds(owner * 4 + half * 2, 2)], y, y_dev)
    y_ring.start()

    for d in range(1, 4):
        l_z_copy(d, zh + 4 - d).wait_recv()
    l_ring = Ring(lambda half, owner: left.at[aligned(owner * QUARTER + half * LANES, LANES)], x, x_dev)
    l_ring.start()

    @pl.loop(1, 16)
    def _(d):
        owner = (i + 16 - d) % 16

        @pl.when(owner < OWNERS)
        def _():
            theirs = cap.at[aligned(owner * PIECE, PIECE)]
            remote(theirs, theirs, k_g + d, {"row": owner}).wait_recv()

    stores = [
        pltpu.make_async_copy(left, left_out, store_sem.at[0]),
        pltpu.make_async_copy(g_col, gcol_out, store_sem.at[1]),
        pltpu.make_async_copy(cap.at[pl.ds(3 * BLOCK, 2 * OUTS)], guess_out, store_sem.at[2]),
        pltpu.make_async_copy(minv, minv_out, store_sem.at[3]),
    ]
    stores[2].start()

    def serve_left():
        l_ring.finish()
        stores[0].start()

    def serve_y():
        y_ring.finish()

        @pl.loop(0, LOCAL // GROUP)
        def _(g):
            g_col[aligned(g * GROUP, GROUP), :] = unfold(g_all[g])

        stores[1].start()

    def rest():
        pass

    invert(cap, minv, iter((rest, y_ring.forward, l_ring.forward, rest, rest, serve_y, rest, serve_left)))
    stores[3].start()

    @pl.when(i != j)
    def _():
        remote(r_src, rx, r_t, {"row": j, "col": i}).wait_send()

    swap_each(lambda copy: copy.wait_send(), None)
    for d in range(1, 4):
        g_z_copy(d).wait_send()
        e_z_copy(d).wait_send()
        l_z_copy(d, zh).wait_send()
    for ring in (g_ring, e_ring, y_ring, l_ring):
        ring.wait_sends()

    @pl.loop(1, 16)
    def _(d):
        owner = (i + d) % 16

        @pl.when(owner < OWNERS)
        def _():
            k_copy(owner, d).wait_send()

        @pl.when(i < OWNERS)
        def _():
            remote(cap.at[own_rows], cap.at[own_rows], k_g + d, {"row": owner}).wait_send()

    for store in stores:
        store.wait()


N_SEMS = 96


def gather_all(rates, targets, readout, corr, rec):
    hbm = pl.BlockSpec(memory_space=pl.ANY)

    def folded(dtype, *lead):
        return pltpu.VMEM((*lead, FOLDED, LANES), dtype)

    return pl.pallas_call(
        comm_kernel,
        out_shape=[
            jax.ShapeDtypeStruct((STEPS, STEPS), F32),
            jax.ShapeDtypeStruct((2 * OUTS, LANES), F32),
            jax.ShapeDtypeStruct((LOCAL, STEPS), F32),
            jax.ShapeDtypeStruct((LOCAL, 2 * STEPS), BF),
        ],
        in_specs=[hbm] * 5,
        out_specs=[hbm] * 4,
        scratch_shapes=[
            pltpu.VMEM((STEPS, LOCAL), BF),
            pltpu.VMEM((LOCAL, STEPS), BF),
            pltpu.VMEM((STEPS, LOCAL), BF),
            pltpu.VMEM((OUTS, LOCAL), F32),
            pltpu.VMEM((STEPS, QUARTER), BF),
            pltpu.VMEM((LOCAL, LOCAL), F32),
            pltpu.VMEM((LOCAL, LOCAL), BF),
            folded(F32, 3, 4),
            folded(F32, 4),
            folded(F32, 2, 2),
            folded(F32, 2, 2),
            folded(F32, 4, 2),
            folded(F32, 3),
            folded(F32),
            folded(F32, 16),
            pltpu.VMEM((LOCAL, STEPS), F32),
            folded(BF, 3, 4),
            folded(F32, 2, 2),
            folded(F32, 4),
            folded(BF, 2, 2),
            folded(BF, 2, 2),
            folded(BF, 4, 2),
            folded(BF, 4),
            folded(BF, 3),
            pltpu.VMEM((LOCAL, 2 * STEPS), BF),
            pltpu.VMEM((PACKED, LANES), F32),
            pltpu.VMEM((15, PIECE, LANES), F32),
            pltpu.VMEM((PIECE, LANES), F32),
            pltpu.VMEM((3, PIECE, LANES), F32),
            pltpu.VMEM((PIECE, LANES), F32),
            pltpu.VMEM((3, PIECE, LANES), F32),
            pltpu.VMEM((PACKED, LANES), F32),
            pltpu.VMEM((STEPS, STEPS), F32),
            pltpu.SemaphoreType.DMA((11,)),
            pltpu.SemaphoreType.DMA((4,)),
            pltpu.SemaphoreType.DMA((N_SEMS,)),
            pltpu.SemaphoreType.DMA((N_SEMS,)),
        ],
        compiler_params=pltpu.CompilerParams(
            collective_id=0, has_side_effects=True, vmem_limit_bytes=VMEM_LIMIT
        ),
        name="exchange",
    )(rates, targets, readout, corr, rec)


def update_kernel(
    minv, guess, gcol, left, goal, readout, corr, rec, corr_out, rec_out, readout_out, scaled,
):
    @pl.when(pl.program_id(0) == 0)
    def _():
        m_hi, m_lo = split2(minv[...])
        g_hi, g_lo = split2(gcol[...])
        value = sum(
            lax.dot_general(m, g, NT, preferred_element_type=F32) for m, g in ((m_hi, g_lo), (m_lo, g_hi), (m_hi, g_hi))
        )
        scaled[...] = value.astype(BF)
        drive = jnp.concatenate([guess[:OUTS, :], guess[OUTS:, : STEPS - LANES]], axis=1)
        readout_out[...] = readout[...] - dot32(drive - goal[...], value)

    drop = jnp.dot(left[:, STEPS:], scaled[...], preferred_element_type=F32)
    corr_out[...] = corr[...] - drop
    drop = jnp.dot(left[:, :STEPS], scaled[...], preferred_element_type=F32)
    rec_out[...] = (rec[...].astype(F32) - drop).astype(BF)


TILE = 256


def update(minv, guess, gcol, left, goal, readout, corr, rec):
    def whole(shape):
        return pl.BlockSpec(shape, lambda g: (0, 0))

    rows = pl.BlockSpec((TILE, LOCAL), lambda g: (g, 0))
    factors = pl.BlockSpec((TILE, 2 * STEPS), lambda g: (g, 0))
    return pl.pallas_call(
        update_kernel,
        grid=(LOCAL // TILE,),
        out_shape=[
            jax.ShapeDtypeStruct((LOCAL, LOCAL), F32),
            jax.ShapeDtypeStruct((LOCAL, LOCAL), BF),
            jax.ShapeDtypeStruct((OUTS, LOCAL), F32),
        ],
        in_specs=[
            whole((STEPS, STEPS)), whole((2 * OUTS, LANES)), whole((LOCAL, STEPS)), factors, whole((OUTS, STEPS)),
            whole((OUTS, LOCAL)), rows, rows,
        ],
        out_specs=[rows, rows, whole((OUTS, LOCAL))],
        scratch_shapes=[pltpu.VMEM((STEPS, LOCAL), BF)],
        compiler_params=pltpu.CompilerParams(vmem_limit_bytes=VMEM_LIMIT),
        name="update",
    )(minv, guess, gcol, left, goal, readout, corr, rec)


def on_device(rates, targets, goal, corr, rec, readout):
    minv, guess, gcol, left = gather_all(rates, targets, readout, corr, rec)
    return tuple(update(minv, guess, gcol, left, goal, readout, corr, rec))


def solution(mesh):
    placed = (P(None, "col"), P(None, "row"), P(), P("row", "col"), P("row", "col"), P(None, "col"))
    return jax.shard_map(
        on_device,
        mesh=mesh,
        in_specs=placed,
        out_specs=(P("row", "col"), P("row", "col"), P(None, "col")),
        check_vma=False,
    )
```

time: 523 us -> 76 us (0.15); the launches traced: 513 us -> 75.3 us
  waiting for transfers between devices: 336 us -> 0 us
  Pallas kernels: 0 us -> 74.7 us
  blocking collectives: 70.5 us -> 0 us
  other arithmetic: 55.9 us -> 0 us
  matrix products: 31.4 us -> 0 us
  between operations: 15.3 us -> 0.64 us
    psum x2 -> x0, waiting for transfers between devices: 253 us -> none  [the longest x1 162 us: on_device(): lax.psum((prod_part, drive_part, guess_part), 'col')]
    all_gather x1 -> x0, waiting for transfers between devices: 83.1 us -> none  [on_device(): gathered = lax.all_gather(prod_rows, 'row', axis=1, tiled=True)]
    pallas_call x0 -> x2, Pallas kernels: none -> 74.7 us  [the longest x1 66.4 us: gather_all(): pl.pallas_call(comm_kernel, out_shape=[jax.ShapeDtypeStruct((STEPS, STEPS...]
    psum x1 -> x0, blocking collectives: 70.5 us -> none  [on_device(): lax.psum((prod_part, drive_part, guess_part), 'col')]
    another operation x13 -> x0, other arithmetic: 52.5 us -> none  [the longest x7 32.7 us: on_device(): factor = jnp.linalg.cholesky(capacity)]
    dot_general x8 -> x0, matrix products: 24.7 us -> none  [the longest x1 6.22 us: on_device(): jnp.dot(err_j.T, scaled, precision=high)]
    another operation x8 -> x0, matrix products: 6.7 us -> none  [the longest x6 4.09 us: on_device(): cinverse = jax.scipy.linalg.cho_solve((factor, True), eye)]
  transfers between devices with their start and end apart: 3 -> 0, of which waited for: 3 -> 0; matrix products, arithmetic and copies ran while one was open for 1% -> 0% of each run, Pallas kernels for 0% -> 0%
where the time goes in v3:
time: 76 us; the launch traced here: 75.3 us
  Pallas kernels  74.7 us (98%)
    pallas_call x1, Pallas kernels, gather_all(): pl.pallas_call(comm_kernel, out_shape=[jax.ShapeDtypeStruct((STEPS, STEPS...  66.4 us
    pallas_call x1, Pallas kernels, update(): pl.pallas_call(update_kernel, grid=(LOCAL // TILE,), out_shape=[jax.Shape...  8.22 us

profile of v3, /device:TPU:1, one launch (start us, length us, event | category | flops | bytes accessed | tf_op | source)
XLA Modules:
  0.0 75.3 jit_solution(7839535104166429051)
XLA Ops:
  0.6 66.4 %exchange.1 = (f32[192,192]{1,0:T(8,128)}, f32[32,128]{1,0:T(8,128)}, f32[1024,192]{1,0:T(8,128)}, bf16[1024,384]{1,0:T(8,128)(2,1)}) custom-call(bf16[192,1024]{1,0:T(8,128)(2,1)} %rates_hbm.1, bf16[192,1024]{1,0:T(8,128)(2,1)} %targets_hbm.1, f32[16,1024]{1,0:T(8,128)} %readout.1, f32[1024,1024]{1,0:T(8,128)} %corr.1, bf16[1024,1024]{1,0:T(8,128)(2,1)} %rec.1), custom_call_target="tpu_custom_call" | custom-call | tf_op jit(solution)/shard_map/exchange/pallas_call | solution.py:599
  67.1 8.2 %update.1 = (f32[1024,1024]{1,0:T(8,128)}, bf16[1024,1024]{1,0:T(8,128)(2,1)}, f32[16,1024]{1,0:T(8,128)}) custom-call(f32[192,192]{1,0:T(8,128)} %get-tuple-element.7.minv, f32[32,128]{1,0:T(8,128)} %get-tuple-element.8.guess, f32[1024,192]{1,0:T(8,128)} %get-tuple-element.9.gcol, bf16[1024,384]{1,0:T(8,128)(2,1)} %get-tuple-element.10.left, ...), custom_call_target="tpu_custom_call" | custom-call | tf_op jit(solution)/shard_map/update/pallas_call | solution.py:684

commit v4 on v3

--- a/solution.py
+++ b/solution.py
@@ -65,9 +65,7 @@
 
 
 def reciprocal(v):
-    r = pl.reciprocal(v, approx=True)
-    r = r * (2.0 - v * r)
-    return r * (2.0 - v * r)
+    return pl.reciprocal(v, approx=True)
 
 
 def factor_two(a, b, d):
@@ -165,10 +163,10 @@
 
 
 def comm_kernel(
-    rates_hbm, targets_hbm, readout_hbm, corr_hbm, rec_hbm,
-    minv_out, guess_out, gcol_out, left_out,
-    rates, rates_t, targets, readout, rx, corr_v, rec_v,
-    g_part, g_mid, g_relay, g_sum, g_x, g_z, g_piece, g_all, g_col,
+    rates_hbm, targets_hbm, goal_hbm, readout_hbm, corr_hbm, rec_hbm,
+    scaled_out, readout_new, left_out,
+    rates, rates_t, targets, goal, readout, rx, corr_v, rec_v,
+    g_part, g_mid, g_relay, g_sum, g_x, g_z, g_piece, g_all, g_hi, g_lo, scaled,
     e_part, e_hold, e_mid, e_relay, e_sum, e_x, e_low, e_z, left,
     kpart, krow, ksum, kz, kmid, kx, cap, minv,
     load_sem, store_sem, send_sem, recv_sem,
@@ -195,22 +193,19 @@
 
     rates_load = load(rates_hbm, rates, 8)
     rec_loads, corr_loads = {}, {}
-    for d in (2, 1, 3, 0):
+
+    def load_quarter(d, loads, src, dst, at):
         part = quarter(x + d)
-        corr_loads[d] = load(corr_hbm.at[part], corr_v.at[part], 4 + d)
-    for d in (2, 1, 3, 0):
-        part = quarter(x + d)
-        rec_loads[d] = load(rec_hbm.at[part], rec_v.at[part], d)
-    readout_load = load(readout_hbm, readout, 9)
-    targets_load = load(targets_hbm, targets, 10)
+        loads[d] = load(src.at[part], dst.at[part], at + d)
+
+    load_quarter(2, corr_loads, corr_hbm, corr_v, 4)
 
     barrier = pltpu.get_barrier_semaphore()
 
     def greet(dev):
         pl.semaphore_signal(barrier, inc=1, device_id=dev, device_id_type=MESH)
 
-    @pl.loop(1, 16)
-    def _(d):
+    for d in range(1, 16):
         greet({"row": (i + d) % 16})
 
     for d in range(1, 4):
@@ -223,9 +218,16 @@
         def _():
             greet({"row": j, "col": y * 4 + z})
 
+    for d in (1, 3, 0):
+        load_quarter(d, corr_loads, corr_hbm, corr_v, 4)
+    for d in (2, 1, 3, 0):
+        load_quarter(d, rec_loads, rec_hbm, rec_v, 0)
+    readout_load = load(readout_hbm, readout, 9)
+    targets_load = load(targets_hbm, targets, 10)
+    goal_load = load(goal_hbm, goal, 11)
+
     rates_load.wait()
     rates_t[...] = rates[...].T
-    pl.semaphore_wait(barrier, jnp.where(i == j, 24, 25))
 
     def z_dev(d):
         return {"col": x * 4 + (zh + d) % 4}
@@ -244,11 +246,12 @@
             self.copies = [
                 remote(part.at[0, top], relay.at[0], at, x_dev(1)),
                 remote(part.at[0, low], relay.at[1], at + 1, x_dev(3)),
-                remote(part.at[1, low], landed.at[0], at + 2, x_dev(1)),
-                remote(part.at[2, top], landed.at[1], at + 3, x_dev(3)),
-                remote(total.at[0], landed.at[2], at + 4, x_dev(1)),
-                remote(total.at[1], landed.at[3], at + 5, x_dev(3)),
+                remote(part.at[1, low], landed.at[0], at + 2, x_dev(1), at + 2),
+                remote(part.at[2, top], landed.at[1], at + 3, x_dev(3), at + 2),
+                remote(total.at[0], landed.at[2], at + 4, x_dev(1), at + 2),
+                remote(total.at[1], landed.at[3], at + 5, x_dev(3), at + 2),
             ]
+            self.all = remote(landed, landed, at + 2, x_dev(1))
 
         def start(self, *which):
             for k in which:
@@ -261,8 +264,7 @@
                 self.copies[4 + k].start()
 
         def finish(self, own):
-            for k in range(2, 6):
-                self.copies[k].wait_recv()
+            self.all.wait_recv()
             got = [self.landed[k].astype(F32) for k in range(4)]
             own[:2] = own[:2] + got[2] + got[1]
             own[2:] = own[2:] + got[0] + got[3]
@@ -318,6 +320,7 @@
 
     g_ring = RingSum(g_part, lambda k: g_part[1, :2] if k == 0 else g_part[2, 2:], g_relay, g_sum, g_x)
     prod_quarter(2, g_part.at[0])
+    pl.semaphore_wait(barrier, jnp.where(i == j, 24, 25))
     g_ring.start(0, 1)
     prod_quarter(1, g_part.at[1])
     g_ring.start(2)
@@ -336,11 +339,11 @@
         pltpu.make_async_copy(r_src, rx, recv_sem.at[r_t]).start()
 
     prod_quarter(0, g_mid)
-    g_ring.forward()
 
     e_ring = RingSum(e_part, lambda k: e_hold[k], e_relay, e_sum, e_x)
     for g, part in enumerate(drive_quarter(2)):
         e_part[0, g] = part.astype(BF)
+    g_ring.forward()
     e_ring.start(0, 1)
     for g, part in enumerate(drive_quarter(1)):
         if g < 2:
@@ -366,7 +369,7 @@
     g_at = sems.take(3)
 
     def g_z_copy(d):
-        return remote(g_mid.at[(zh + d) % 4], g_z.at[d - 1], g_at + d - 1, z_dev(d))
+        return remote(g_mid.at[(zh + d) % 4], g_z.at[d - 1], g_at + d - 1, z_dev(d), g_at)
 
     for d in range(1, 4):
         g_z_copy(d).start()
@@ -388,109 +391,92 @@
     kpart[BLOCK : 2 * BLOCK, :] = jnp.concatenate([kb[2][2], kb[1][0]], axis=1)
     kpart[2 * BLOCK : 3 * BLOCK, :] = jnp.concatenate([kb[2][0], kb[2][1]], axis=1)
 
-    k_r = sems.take(16)
-
-    def k_copy(owner, d):
-        return remote(kpart.at[aligned(owner * PIECE, PIECE)], krow.at[d - 1], k_r + d, {"row": owner})
-
-    @pl.loop(1, 16)
-    def _(d):
+    k_r = sems.take(1)
+
+    for d in range(1, 16):
         owner = (i + d) % 16
 
         @pl.when(owner < OWNERS)
         def _():
-            k_copy(owner, d).start()
+            remote(kpart.at[aligned(owner * PIECE, PIECE)], krow.at[d - 1], k_r, {"row": owner}).start()
 
     e_ring.forward()
     for g, part in enumerate(drive_quarter(0)):
         e_mid[g] = part
 
+    remote(g_z, g_z, g_at, z_dev(1)).wait_recv()
+    piece = g_mid[zh] + g_z[0] + g_z[1] + g_z[2]
+    g_piece[...] = piece
+    own = aligned(x * QUARTER + zh * GROUP, GROUP)
+    left[own, STEPS:] = unfold(piece).astype(BF)
+    s_t = sems.take(4)
+
+    def swap_each(act_remote, act_local):
+        for e in range(4):
+            dst = g_all.at[x * 4 + zh]
+
+            @pl.when((i != j) | (i % 4 != e))
+            def _():
+                act_remote(remote(g_piece, dst, s_t + e, {"row": x * 4 + e, "col": i}, s_t + zh))
+
+            if act_local is not None:
+
+                @pl.when((i == j) & (i % 4 == e))
+                def _():
+                    act_local(pltpu.make_async_copy(g_piece, dst, recv_sem.at[s_t + zh]))
+
+    swap_each(lambda copy: copy.start(), lambda copy: copy.start())
+
     k_z = sems.take(3)
     k_x = sems.take(3)
 
     @pl.when(i < OWNERS)
     def _():
-        @pl.loop(1, 16)
-        def _(d):
-            remote(kpart.at[pl.ds(0, PIECE)], krow.at[d - 1], k_r + d, {"row": (i + 16 - d) % 16}).wait_recv()
-
+        remote(krow, krow, k_r, {"row": (i + 1) % 16}).wait_recv()
         acc = kpart[aligned(i * PIECE, PIECE), :]
         for d in range(15):
             acc = acc + krow[d]
         ksum[...] = acc
         for d in range(1, 4):
-            remote(ksum, kz.at[d - 1], k_z + d - 1, z_dev(d)).start()
-
-    for d in range(1, 4):
-        g_z_copy(d).wait_recv()
-    piece = g_mid[zh] + g_z[0] + g_z[1] + g_z[2]
-    g_piece[...] = piece
-    own = aligned(x * QUARTER + zh * GROUP, GROUP)
-    left[own, STEPS:] = unfold(piece).astype(BF)
-    s_t = sems.take(4)
-
-    def swap_each(act_remote, act_local):
-        for e in range(4):
-            dst = g_all.at[x * 4 + zh]
-
-            @pl.when((i != j) | (i % 4 != e))
-            def _():
-                act_remote(remote(g_piece, dst, s_t + e, {"row": x * 4 + e, "col": i}, s_t + zh))
-
-            if act_local is not None:
-
-                @pl.when((i == j) & (i % 4 == e))
-                def _():
-                    act_local(pltpu.make_async_copy(g_piece, dst, recv_sem.at[s_t + zh]))
-
-    swap_each(lambda copy: copy.start(), lambda copy: copy.start())
+            remote(ksum, kz.at[d - 1], k_z + d - 1, z_dev(d), k_z).start()
 
     e_ring.finish(e_mid)
     e_low[...] = e_mid[...].astype(BF)
     e_at = sems.take(3)
 
     def e_z_copy(d):
-        return remote(e_low.at[(zh + d) % 4], e_z.at[d - 1], e_at + d - 1, z_dev(d))
+        return remote(e_low.at[(zh + d) % 4], e_z.at[d - 1], e_at + d - 1, z_dev(d), e_at)
 
     for d in range(1, 4):
         e_z_copy(d).start()
 
     @pl.when(i < OWNERS)
     def _():
-        acc = ksum[...]
+        remote(kz, kz, k_z, z_dev(1)).wait_recv()
+        kmid[...] = ksum[...] + kz[0] + kz[1] + kz[2]
         for d in range(1, 4):
-            copy = remote(ksum, kz.at[d - 1], k_z + d - 1, z_dev(d))
-            copy.wait_recv()
-            copy.wait_send()
-            acc = acc + kz[d - 1]
-        kmid[...] = acc
-        for d in range(1, 4):
-            remote(kmid, kx.at[d - 1], k_x + d - 1, x_dev(d)).start()
+            remote(kmid, kx.at[d - 1], k_x + d - 1, x_dev(d), k_x).start()
 
     targets_load.wait()
     aims = targets[:, quarter(x)].T
     e_hold[0] = jnp.stack([fold(part) for part in groups(aims[:LANES].astype(F32))])
     e_hold[1] = jnp.stack([fold(part) for part in groups(aims[LANES:].astype(F32))])
 
-    k_g = sems.take(16)
-    own_rows = aligned(i * PIECE, PIECE)
-
-    @pl.when(i < OWNERS)
-    def _():
-        acc = kmid[...]
-        for d in range(1, 4):
-            copy = remote(kmid, kx.at[d - 1], k_x + d - 1, x_dev(d))
-            copy.wait_recv()
-            copy.wait_send()
-            acc = acc + kx[d - 1]
-        cap[own_rows, :] = acc
-
-        @pl.loop(1, 16)
-        def _(d):
-            remote(cap.at[own_rows], cap.at[own_rows], k_g + d, {"row": (i + d) % 16}).start()
-
-    for d in range(1, 4):
-        e_z_copy(d).wait_recv()
+    for z in range(4):
+        dst = g_all.at[y * 4 + z]
+
+        @pl.when((i != j) | (zh != z))
+        def _():
+            remote(g_piece, dst, s_t, {"row": j, "col": y * 4 + z}, s_t + z).wait_recv()
+
+        @pl.when((i == j) & (zh == z))
+        def _():
+            pltpu.make_async_copy(g_piece, dst, recv_sem.at[s_t + z]).wait()
+
+    y_ring = Ring(lambda half, owner: g_all.at[pl.ds(owner * 4 + half * 2, 2)], y, y_dev)
+    y_ring.start()
+
+    remote(e_z, e_z, e_at, z_dev(1)).wait_recv()
     total = e_mid[zh] - e_hold[zh // 2, zh % 2]
     for d in range(3):
         total = total + e_z[d].astype(F32)
@@ -504,60 +490,66 @@
     for d in range(1, 4):
         l_z_copy(d, zh).start()
 
-    for z in range(4):
-        dst = g_all.at[y * 4 + z]
-
-        @pl.when((i != j) | (zh != z))
-        def _():
-            remote(g_piece, dst, s_t, {"row": j, "col": y * 4 + z}, s_t + z).wait_recv()
-
-        @pl.when((i == j) & (zh == z))
-        def _():
-            pltpu.make_async_copy(g_piece, dst, recv_sem.at[s_t + z]).wait()
-
-    y_ring = Ring(lambda half, owner: g_all.at[pl.ds(owner * 4 + half * 2, 2)], y, y_dev)
-    y_ring.start()
+    k_g = sems.take(1)
+    own_rows = aligned(i * PIECE, PIECE)
+
+    @pl.when(i < OWNERS)
+    def _():
+        remote(kx, kx, k_x, x_dev(1)).wait_recv()
+        cap[own_rows, :] = kmid[...] + kx[0] + kx[1] + kx[2]
+        for d in range(1, 16):
+            remote(cap.at[own_rows], cap.at[own_rows], k_g, {"row": (i + d) % 16}).start()
+
+    y_ring.forward()
 
     for d in range(1, 4):
         l_z_copy(d, zh + 4 - d).wait_recv()
     l_ring = Ring(lambda half, owner: left.at[aligned(owner * QUARTER + half * LANES, LANES)], x, x_dev)
     l_ring.start()
 
-    @pl.loop(1, 16)
-    def _(d):
-        owner = (i + 16 - d) % 16
-
-        @pl.when(owner < OWNERS)
-        def _():
-            theirs = cap.at[aligned(owner * PIECE, PIECE)]
-            remote(theirs, theirs, k_g + d, {"row": owner}).wait_recv()
-
-    stores = [
-        pltpu.make_async_copy(left, left_out, store_sem.at[0]),
-        pltpu.make_async_copy(g_col, gcol_out, store_sem.at[1]),
-        pltpu.make_async_copy(cap.at[pl.ds(3 * BLOCK, 2 * OUTS)], guess_out, store_sem.at[2]),
-        pltpu.make_async_copy(minv, minv_out, store_sem.at[3]),
-    ]
-    stores[2].start()
-
-    def serve_left():
-        l_ring.finish()
-        stores[0].start()
+    others = cap.at[pl.ds(0, PACKED - PIECE)]
+
+    @pl.when(i < OWNERS)
+    def _():
+        remote(others, others, k_g, {"row": (i + 1) % 16}).wait_recv()
+
+    @pl.when(i >= OWNERS)
+    def _():
+        remote(cap, cap, k_g, {"row": (i + 1) % 16}).wait_recv()
+
+    def rest():
+        pass
 
     def serve_y():
         y_ring.finish()
 
         @pl.loop(0, LOCAL // GROUP)
         def _(g):
-            g_col[aligned(g * GROUP, GROUP), :] = unfold(g_all[g])
-
-        stores[1].start()
-
-    def rest():
-        pass
-
-    invert(cap, minv, iter((rest, y_ring.forward, l_ring.forward, rest, rest, serve_y, rest, serve_left)))
-    stores[3].start()
+            hi, lo = split2(unfold(g_all[g]))
+            rows = aligned(g * GROUP, GROUP)
+            g_hi[rows, :] = hi
+            g_lo[rows, :] = lo
+
+    invert(cap, minv, iter((rest, rest, l_ring.forward, rest, rest, rest, rest, serve_y)))
+
+    m_hi, m_lo = split2(minv[...])
+    value = sum(
+        lax.dot_general(m, g, NT, preferred_element_type=F32)
+        for m, g in ((m_hi, g_lo[...]), (m_lo, g_hi[...]), (m_hi, g_hi[...]))
+    )
+    scaled[...] = value.astype(BF)
+    stores = [
+        pltpu.make_async_copy(scaled, scaled_out, store_sem.at[0]),
+        pltpu.make_async_copy(left, left_out, store_sem.at[1]),
+        pltpu.make_async_copy(readout, readout_new, store_sem.at[2]),
+    ]
+    stores[0].start()
+    l_ring.finish()
+    stores[1].start()
+    goal_load.wait()
+    guess = jnp.concatenate([cap[3 * BLOCK : 3 * BLOCK + OUTS, :], cap[3 * BLOCK + OUTS :, : STEPS - LANES]], axis=1)
+    readout[...] -= dot32(guess - goal[...], value)
+    stores[2].start()
 
     @pl.when(i != j)
     def _():
@@ -571,17 +563,19 @@
     for ring in (g_ring, e_ring, y_ring, l_ring):
         ring.wait_sends()
 
-    @pl.loop(1, 16)
-    def _(d):
-        owner = (i + d) % 16
-
-        @pl.when(owner < OWNERS)
-        def _():
-            k_copy(owner, d).wait_send()
-
-        @pl.when(i < OWNERS)
-        def _():
-            remote(cap.at[own_rows], cap.at[own_rows], k_g + d, {"row": owner}).wait_send()
+    some = kpart.at[pl.ds(0, PACKED - PIECE)]
+
+    @pl.when(i < OWNERS)
+    def _():
+        remote(some, some, k_r, {"row": (i + 1) % 16}).wait_send()
+        for d in range(1, 4):
+            remote(ksum, kz.at[d - 1], k_z + d - 1, z_dev(d)).wait_send()
+            remote(kmid, kx.at[d - 1], k_x + d - 1, x_dev(d)).wait_send()
+        remote(krow, krow, k_g, {"row": (i + 1) % 16}).wait_send()
+
+    @pl.when(i >= OWNERS)
+    def _():
+        remote(kpart, kpart, k_r, {"row": (i + 1) % 16}).wait_send()
 
     for store in stores:
         store.wait()
@@ -590,7 +584,7 @@
 N_SEMS = 96
 
 
-def gather_all(rates, targets, readout, corr, rec):
+def gather_all(rates, targets, goal, readout, corr, rec):
     hbm = pl.BlockSpec(memory_space=pl.ANY)
 
     def folded(dtype, *lead):
@@ -599,17 +593,17 @@
     return pl.pallas_call(
         comm_kernel,
         out_shape=[
-            jax.ShapeDtypeStruct((STEPS, STEPS), F32),
-            jax.ShapeDtypeStruct((2 * OUTS, LANES), F32),
-            jax.ShapeDtypeStruct((LOCAL, STEPS), F32),
+            jax.ShapeDtypeStruct((STEPS, LOCAL), BF),
+            jax.ShapeDtypeStruct((OUTS, LOCAL), F32),
             jax.ShapeDtypeStruct((LOCAL, 2 * STEPS), BF),
         ],
-        in_specs=[hbm] * 5,
-        out_specs=[hbm] * 4,
+        in_specs=[hbm] * 6,
+        out_specs=[hbm] * 3,
         scratch_shapes=[
             pltpu.VMEM((STEPS, LOCAL), BF),
             pltpu.VMEM((LOCAL, STEPS), BF),
             pltpu.VMEM((STEPS, LOCAL), BF),
+            pltpu.VMEM((OUTS, STEPS), F32),
             pltpu.VMEM((OUTS, LOCAL), F32),
             pltpu.VMEM((STEPS, QUARTER), BF),
             pltpu.VMEM((LOCAL, LOCAL), F32),
@@ -622,7 +616,9 @@
             folded(F32, 3),
             folded(F32),
             folded(F32, 16),
-            pltpu.VMEM((LOCAL, STEPS), F32),
+            pltpu.VMEM((LOCAL, STEPS), BF),
+            pltpu.VMEM((LOCAL, STEPS), BF),
+            pltpu.VMEM((STEPS, LOCAL), BF),
             folded(BF, 3, 4),
             folded(F32, 2, 2),
             folded(F32, 4),
@@ -640,8 +636,8 @@
             pltpu.VMEM((3, PIECE, LANES), F32),
             pltpu.VMEM((PACKED, LANES), F32),
             pltpu.VMEM((STEPS, STEPS), F32),
-            pltpu.SemaphoreType.DMA((11,)),
-            pltpu.SemaphoreType.DMA((4,)),
+            pltpu.SemaphoreType.DMA((12,)),
+            pltpu.SemaphoreType.DMA((3,)),
             pltpu.SemaphoreType.DMA((N_SEMS,)),
             pltpu.SemaphoreType.DMA((N_SEMS,)),
         ],
@@ -649,33 +645,21 @@
             collective_id=0, has_side_effects=True, vmem_limit_bytes=VMEM_LIMIT
         ),
         name="exchange",
-    )(rates, targets, readout, corr, rec)
-
-
-def update_kernel(
-    minv, guess, gcol, left, goal, readout, corr, rec, corr_out, rec_out, readout_out, scaled,
-):
-    @pl.when(pl.program_id(0) == 0)
-    def _():
-        m_hi, m_lo = split2(minv[...])
-        g_hi, g_lo = split2(gcol[...])
-        value = sum(
-            lax.dot_general(m, g, NT, preferred_element_type=F32) for m, g in ((m_hi, g_lo), (m_lo, g_hi), (m_hi, g_hi))
-        )
-        scaled[...] = value.astype(BF)
-        drive = jnp.concatenate([guess[:OUTS, :], guess[OUTS:, : STEPS - LANES]], axis=1)
-        readout_out[...] = readout[...] - dot32(drive - goal[...], value)
-
+    )(rates, targets, goal, readout, corr, rec)
+
+
+def update_kernel(scaled, readout_new, left, corr, rec, corr_out, rec_out, readout_out):
     drop = jnp.dot(left[:, STEPS:], scaled[...], preferred_element_type=F32)
     corr_out[...] = corr[...] - drop
     drop = jnp.dot(left[:, :STEPS], scaled[...], preferred_element_type=F32)
     rec_out[...] = (rec[...].astype(F32) - drop).astype(BF)
+    readout_out[...] = readout_new[...]
 
 
 TILE = 256
 
 
-def update(minv, guess, gcol, left, goal, readout, corr, rec):
+def update(scaled, readout_new, left, corr, rec):
     def whole(shape):
         return pl.BlockSpec(shape, lambda g: (0, 0))
 
@@ -689,20 +673,16 @@
             jax.ShapeDtypeStruct((LOCAL, LOCAL), BF),
             jax.ShapeDtypeStruct((OUTS, LOCAL), F32),
         ],
-        in_specs=[
-            whole((STEPS, STEPS)), whole((2 * OUTS, LANES)), whole((LOCAL, STEPS)), factors, whole((OUTS, STEPS)),
-            whole((OUTS, LOCAL)), rows, rows,
-        ],
+        in_specs=[whole((STEPS, LOCAL)), whole((OUTS, LOCAL)), factors, rows, rows],
         out_specs=[rows, rows, whole((OUTS, LOCAL))],
-        scratch_shapes=[pltpu.VMEM((STEPS, LOCAL), BF)],
         compiler_params=pltpu.CompilerParams(vmem_limit_bytes=VMEM_LIMIT),
         name="update",
-    )(minv, guess, gcol, left, goal, readout, corr, rec)
+    )(scaled, readout_new, left, corr, rec)
 
 
 def on_device(rates, targets, goal, corr, rec, readout):
-    minv, guess, gcol, left = gather_all(rates, targets, readout, corr, rec)
-    return tuple(update(minv, guess, gcol, left, goal, readout, corr, rec))
+    scaled, readout_new, left = gather_all(rates, targets, goal, readout, corr, rec)
+    return tuple(update(scaled, readout_new, left, corr, rec))
 
 
 def solution(mesh):

time: 76 us -> 72.8 us (0.958)
  Pallas kernels: 74.7 us -> 71.2 us
    pallas_call x1, Pallas kernels: 66.4 us -> 64.4 us  [gather_all(): pl.pallas_call(comm_kernel, out_shape=[jax.ShapeDtypeStruct((STEPS, LOCAL...]
    pallas_call x1, Pallas kernels: 8.22 us -> 6.86 us  [update(): pl.pallas_call(update_kernel, grid=(LOCAL // TILE,), out_shape=[jax.Shape...]
where the time goes in v4:
time: 72.8 us; the launch traced here: 71.9 us
  Pallas kernels  71.2 us (98%)
    pallas_call x1, Pallas kernels, gather_all(): pl.pallas_call(comm_kernel, out_shape=[jax.ShapeDtypeStruct((STEPS, LOCAL...  64.4 us
    pallas_call x1, Pallas kernels, update(): pl.pallas_call(update_kernel, grid=(LOCAL // TILE,), out_shape=[jax.Shape...  6.86 us

profile of v4, /device:TPU:1, one launch (start us, length us, event | category | flops | bytes accessed | tf_op | source)
XLA Modules:
  0.0 71.9 jit_solution(13641394138471133031)
XLA Ops:
  0.6 64.4 %exchange.1 = (bf16[192,1024]{1,0:T(8,128)(2,1)}, f32[16,1024]{1,0:T(8,128)}, bf16[1024,384]{1,0:T(8,128)(2,1)}) custom-call(bf16[192,1024]{1,0:T(8,128)(2,1)} %rates_hbm.1, bf16[192,1024]{1,0:T(8,128)(2,1)} %targets_hbm.1, f32[16,192]{1,0:T(8,128)} %goal_hbm.1, f32[16,1024]{1,0:T(8,128)} %readout_hbm.1, f32[1024,1024]{1,0:T(8,128)} %corr.1, ...), custom_call_target="tpu_custom_call" | custom-call | tf_op jit(solution)/shard_map/exchange/pallas_call | solution.py:593
  65.0 6.9 %update.1 = (f32[1024,1024]{1,0:T(8,128)}, bf16[1024,1024]{1,0:T(8,128)(2,1)}, f32[16,1024]{1,0:T(8,128)}) custom-call(bf16[192,1024]{1,0:T(8,128)(2,1)} %get-tuple-element.6.scaled, f32[16,1024]{1,0:T(8,128)} %get-tuple-element.7.readout_new, bf16[1024,384]{1,0:T(8,128)(2,1)} %get-tuple-element.8.left, f32[1024,1024]{1,0:T(8,128)} %corr.1, ...), custom_call_target="tpu_custom_call" | custom-call | tf_op jit(solution)/shard_map/update/pallas_call | solution.py:668

commit v5 on v4

--- a/solution.py
+++ b/solution.py
@@ -23,7 +23,7 @@
 LANES = 128
 FOLDED = GROUP * STEPS // LANES
 NT = (((1,), (1,)), ((), ()))
-VMEM_LIMIT = 60 * 1024 * 1024
+VMEM_LIMIT = 32 * 1024 * 1024
 
 
 def split2(x):
@@ -164,12 +164,12 @@
 
 def comm_kernel(
     rates_hbm, targets_hbm, goal_hbm, readout_hbm, corr_hbm, rec_hbm,
-    scaled_out, readout_new, left_out,
-    rates, rates_t, targets, goal, readout, rx, corr_v, rec_v,
-    g_part, g_mid, g_relay, g_sum, g_x, g_z, g_piece, g_all, g_hi, g_lo, scaled,
-    e_part, e_hold, e_mid, e_relay, e_sum, e_x, e_low, e_z, left,
+    scaled, readout_new, left, corr_v, rec_v,
+    rates, rates_t, targets, goal, readout, rx,
+    g_part, g_mid, g_relay, g_sum, g_x, g_z, g_piece, g_all, g_hi, g_lo,
+    e_part, e_hold, e_mid, e_relay, e_sum, e_x, e_low, e_z,
     kpart, krow, ksum, kz, kmid, kx, cap, minv,
-    load_sem, store_sem, send_sem, recv_sem,
+    load_sem, send_sem, recv_sem,
 ):
     i = lax.axis_index("row")
     j = lax.axis_index("col")
@@ -212,11 +212,16 @@
         greet({"col": x * 4 + (zh + d) % 4})
         greet({"col": ((x + d) % 4) * 4 + zh})
 
-    for z in range(4):
-
-        @pl.when((i != j) | (zh != z))
+    @pl.when(i != j)
+    def _():
+        greet({"row": j, "col": i})
+
+    for z in range(2):
+        source = y * 4 + 2 * c + z
+
+        @pl.when((i != j) | (source != j))
         def _():
-            greet({"row": j, "col": y * 4 + z})
+            greet({"row": j, "col": source})
 
     for d in (1, 3, 0):
         load_quarter(d, corr_loads, corr_hbm, corr_v, 4)
@@ -320,7 +325,7 @@
 
     g_ring = RingSum(g_part, lambda k: g_part[1, :2] if k == 0 else g_part[2, 2:], g_relay, g_sum, g_x)
     prod_quarter(2, g_part.at[0])
-    pl.semaphore_wait(barrier, jnp.where(i == j, 24, 25))
+    pl.semaphore_wait(barrier, jnp.where(i == j, jnp.where(zl == c, 22, 23), 24))
     g_ring.start(0, 1)
     prod_quarter(1, g_part.at[1])
     g_ring.start(2)
@@ -409,21 +414,22 @@
     g_piece[...] = piece
     own = aligned(x * QUARTER + zh * GROUP, GROUP)
     left[own, STEPS:] = unfold(piece).astype(BF)
-    s_t = sems.take(4)
+    s_t = sems.take(2)
 
     def swap_each(act_remote, act_local):
-        for e in range(4):
-            dst = g_all.at[x * 4 + zh]
-
-            @pl.when((i != j) | (i % 4 != e))
+        for e in range(2):
+            dst = g_all.at[x, zh]
+            row = x * 4 + e * 2 + zh // 2
+
+            @pl.when((i != j) | (row != i))
             def _():
-                act_remote(remote(g_piece, dst, s_t + e, {"row": x * 4 + e, "col": i}, s_t + zh))
+                act_remote(remote(g_piece, dst, s_t + e, {"row": row, "col": i}, s_t + zh % 2))
 
             if act_local is not None:
 
-                @pl.when((i == j) & (i % 4 == e))
+                @pl.when((i == j) & (row == i))
                 def _():
-                    act_local(pltpu.make_async_copy(g_piece, dst, recv_sem.at[s_t + zh]))
+                    act_local(pltpu.make_async_copy(g_piece, dst, recv_sem.at[s_t + zh % 2]))
 
     swap_each(lambda copy: copy.start(), lambda copy: copy.start())
 
@@ -462,18 +468,19 @@
     e_hold[0] = jnp.stack([fold(part) for part in groups(aims[:LANES].astype(F32))])
     e_hold[1] = jnp.stack([fold(part) for part in groups(aims[LANES:].astype(F32))])
 
-    for z in range(4):
-        dst = g_all.at[y * 4 + z]
-
-        @pl.when((i != j) | (zh != z))
+    for z in range(2):
+        source = y * 4 + 2 * c + z
+        dst = g_all.at[y, 2 * c + z]
+
+        @pl.when((i != j) | (source != j))
         def _():
-            remote(g_piece, dst, s_t, {"row": j, "col": y * 4 + z}, s_t + z).wait_recv()
-
-        @pl.when((i == j) & (zh == z))
+            remote(g_piece, dst, s_t, {"row": j, "col": source}, s_t + z).wait_recv()
+
+        @pl.when((i == j) & (source == j))
         def _():
             pltpu.make_async_copy(g_piece, dst, recv_sem.at[s_t + z]).wait()
 
-    y_ring = Ring(lambda half, owner: g_all.at[pl.ds(owner * 4 + half * 2, 2)], y, y_dev)
+    y_ring = Ring(lambda half, owner: g_all.at[owner, 2 * c + half], y, y_dev)
     y_ring.start()
 
     remote(e_z, e_z, e_at, z_dev(1)).wait_recv()
@@ -520,17 +527,27 @@
     def rest():
         pass
 
+    a_c = sems.take(1)
+    sibling = {"row": i + 1 - 2 * c}
+    mine = g_all.at[:, pl.ds(2 * c, 2)]
+    theirs = g_all.at[:, pl.ds(2 - 2 * c, 2)]
+
     def serve_y():
         y_ring.finish()
-
-        @pl.loop(0, LOCAL // GROUP)
-        def _(g):
-            hi, lo = split2(unfold(g_all[g]))
-            rows = aligned(g * GROUP, GROUP)
-            g_hi[rows, :] = hi
-            g_lo[rows, :] = lo
-
-    invert(cap, minv, iter((rest, rest, l_ring.forward, rest, rest, rest, rest, serve_y)))
+        remote(mine, mine, a_c, sibling).start()
+
+    def serve_core():
+        remote(theirs, theirs, a_c, sibling).wait_recv()
+
+        @pl.loop(0, 4)
+        def _(q):
+            for g in range(4):
+                hi, lo = split2(unfold(g_all[q, g]))
+                rows = aligned(q * QUARTER + g * GROUP, GROUP)
+                g_hi[rows, :] = hi
+                g_lo[rows, :] = lo
+
+    invert(cap, minv, iter((rest, rest, l_ring.forward, rest, rest, serve_y, rest, rest, serve_core)))
 
     m_hi, m_lo = split2(minv[...])
     value = sum(
@@ -538,18 +555,10 @@
         for m, g in ((m_hi, g_lo[...]), (m_lo, g_hi[...]), (m_hi, g_hi[...]))
     )
     scaled[...] = value.astype(BF)
-    stores = [
-        pltpu.make_async_copy(scaled, scaled_out, store_sem.at[0]),
-        pltpu.make_async_copy(left, left_out, store_sem.at[1]),
-        pltpu.make_async_copy(readout, readout_new, store_sem.at[2]),
-    ]
-    stores[0].start()
-    l_ring.finish()
-    stores[1].start()
     goal_load.wait()
     guess = jnp.concatenate([cap[3 * BLOCK : 3 * BLOCK + OUTS, :], cap[3 * BLOCK + OUTS :, : STEPS - LANES]], axis=1)
-    readout[...] -= dot32(guess - goal[...], value)
-    stores[2].start()
+    readout_new[...] = readout[...] - dot32(guess - goal[...], value)
+    l_ring.finish()
 
     @pl.when(i != j)
     def _():
@@ -577,8 +586,7 @@
     def _():
         remote(kpart, kpart, k_r, {"row": (i + 1) % 16}).wait_send()
 
-    for store in stores:
-        store.wait()
+    remote(mine, mine, a_c, sibling).wait_send()
 
 
 N_SEMS = 96
@@ -596,9 +604,11 @@
             jax.ShapeDtypeStruct((STEPS, LOCAL), BF),
             jax.ShapeDtypeStruct((OUTS, LOCAL), F32),
             jax.ShapeDtypeStruct((LOCAL, 2 * STEPS), BF),
+            jax.ShapeDtypeStruct((LOCAL, LOCAL), F32),
+            jax.ShapeDtypeStruct((LOCAL, LOCAL), BF),
         ],
         in_specs=[hbm] * 6,
-        out_specs=[hbm] * 3,
+        out_specs=[pl.BlockSpec(memory_space=pltpu.VMEM)] * 5,
         scratch_shapes=[
             pltpu.VMEM((STEPS, LOCAL), BF),
             pltpu.VMEM((LOCAL, STEPS), BF),
@@ -606,8 +616,6 @@
             pltpu.VMEM((OUTS, STEPS), F32),
             pltpu.VMEM((OUTS, LOCAL), F32),
             pltpu.VMEM((STEPS, QUARTER), BF),
-            pltpu.VMEM((LOCAL, LOCAL), F32),
-            pltpu.VMEM((LOCAL, LOCAL), BF),
             folded(F32, 3, 4),
             folded(F32, 4),
             folded(F32, 2, 2),
@@ -615,10 +623,9 @@
             folded(F32, 4, 2),
             folded(F32, 3),
             folded(F32),
-            folded(F32, 16),
+            folded(F32, 4, 4),
             pltpu.VMEM((LOCAL, STEPS), BF),
             pltpu.VMEM((LOCAL, STEPS), BF),
-            pltpu.VMEM((STEPS, LOCAL), BF),
             folded(BF, 3, 4),
             folded(F32, 2, 2),
             folded(F32, 4),
@@ -627,7 +634,6 @@
             folded(BF, 4, 2),
             folded(BF, 4),
             folded(BF, 3),
-            pltpu.VMEM((LOCAL, 2 * STEPS), BF),
             pltpu.VMEM((PACKED, LANES), F32),
             pltpu.VMEM((15, PIECE, LANES), F32),
             pltpu.VMEM((PIECE, LANES), F32),
@@ -637,7 +643,6 @@
             pltpu.VMEM((PACKED, LANES), F32),
             pltpu.VMEM((STEPS, STEPS), F32),
             pltpu.SemaphoreType.DMA((12,)),
-            pltpu.SemaphoreType.DMA((3,)),
             pltpu.SemaphoreType.DMA((N_SEMS,)),
             pltpu.SemaphoreType.DMA((N_SEMS,)),
         ],
@@ -648,23 +653,20 @@
     )(rates, targets, goal, readout, corr, rec)
 
 
+TILE = 256
+
+
 def update_kernel(scaled, readout_new, left, corr, rec, corr_out, rec_out, readout_out):
-    drop = jnp.dot(left[:, STEPS:], scaled[...], preferred_element_type=F32)
-    corr_out[...] = corr[...] - drop
-    drop = jnp.dot(left[:, :STEPS], scaled[...], preferred_element_type=F32)
-    rec_out[...] = (rec[...].astype(F32) - drop).astype(BF)
+    rows = aligned(pl.program_id(0) * TILE, TILE)
+    drop = jnp.dot(left[rows, STEPS:], scaled[...], preferred_element_type=F32)
+    corr_out[...] = corr[rows, :] - drop
+    drop = jnp.dot(left[rows, :STEPS], scaled[...], preferred_element_type=F32)
+    rec_out[...] = (rec[rows, :].astype(F32) - drop).astype(BF)
     readout_out[...] = readout_new[...]
 
 
-TILE = 256
-
-
 def update(scaled, readout_new, left, corr, rec):
-    def whole(shape):
-        return pl.BlockSpec(shape, lambda g: (0, 0))
-
     rows = pl.BlockSpec((TILE, LOCAL), lambda g: (g, 0))
-    factors = pl.BlockSpec((TILE, 2 * STEPS), lambda g: (g, 0))
     return pl.pallas_call(
         update_kernel,
         grid=(LOCAL // TILE,),
@@ -673,16 +675,16 @@
             jax.ShapeDtypeStruct((LOCAL, LOCAL), BF),
             jax.ShapeDtypeStruct((OUTS, LOCAL), F32),
         ],
-        in_specs=[whole((STEPS, LOCAL)), whole((OUTS, LOCAL)), factors, rows, rows],
-        out_specs=[rows, rows, whole((OUTS, LOCAL))],
+        in_specs=[pl.BlockSpec(memory_space=pltpu.VMEM)] * 5,
+        out_specs=[rows, rows, pl.BlockSpec((OUTS, LOCAL), lambda g: (0, 0))],
         compiler_params=pltpu.CompilerParams(vmem_limit_bytes=VMEM_LIMIT),
         name="update",
     )(scaled, readout_new, left, corr, rec)
 
 
-def on_device(rates, targets, goal, corr, rec, readout):
-    scaled, readout_new, left = gather_all(rates, targets, goal, readout, corr, rec)
-    return tuple(update(scaled, readout_new, left, corr, rec))
+def on_device(*args):
+    rates, targets, goal, corr, rec, readout = (pltpu.with_memory_space_constraint(v, pltpu.HBM) for v in args)
+    return tuple(update(*gather_all(rates, targets, goal, readout, corr, rec)))
 
 
 def solution(mesh):

time: 72.8 us -> 66.6 us (0.915)
  Pallas kernels: 71.2 us -> 65.8 us
    pallas_call x1, Pallas kernels: 6.86 us -> 3.53 us  [update(): pl.pallas_call(update_kernel, grid=(LOCAL // TILE,), out_shape=[jax.Shape...]
    pallas_call x1, Pallas kernels: 64.4 us -> 62.2 us  [gather_all(): pl.pallas_call(comm_kernel, out_shape=[jax.ShapeDtypeStruct((STEPS, LOCAL...]
where the time goes in v5:
time: 66.6 us; the launch traced here: 66.4 us
  Pallas kernels  65.8 us (99%)
    pallas_call x1, Pallas kernels, gather_all(): pl.pallas_call(comm_kernel, out_shape=[jax.ShapeDtypeStruct((STEPS, LOCAL...  62.2 us
    pallas_call x1, Pallas kernels, update(): pl.pallas_call(update_kernel, grid=(LOCAL // TILE,), out_shape=[jax.Shape...  3.53 us

profile of v5, /device:TPU:1, one launch (start us, length us, event | category | flops | bytes accessed | tf_op | source)
XLA Modules:
  0.0 66.4 jit_solution(3454449542346787011)
XLA Ops:
  0.6 62.2 %exchange.1 = (bf16[192,1024]{1,0:T(8,128)(2,1)S(1)}, f32[16,1024]{1,0:T(8,128)S(1)}, bf16[1024,384]{1,0:T(8,128)(2,1)S(1)}, f32[1024,1024]{1,0:T(8,128)S(1)}, bf16[1024,1024]{1,0:T(8,128)(2,1)S(1)}) custom-call(bf16[192,1024]{1,0:T(8,128)(2,1)} %rates_hbm.1, bf16[192,1024]{1,0:T(8,128)(2,1)} %targets_hbm.1, f32[16,192]{1,0:T(8,128)} %goal_hbm.1, ...), custom_call_target="tpu_custom_call" | custom-call | tf_op jit(solution)/shard_map/exchange/pallas_call | solution.py:601
  62.9 3.5 %update.1 = (f32[1024,1024]{1,0:T(8,128)}, bf16[1024,1024]{1,0:T(8,128)(2,1)}, f32[16,1024]{1,0:T(8,128)}) custom-call(bf16[192,1024]{1,0:T(8,128)(2,1)S(1)} %get-tuple-element.8.scaled, f32[16,1024]{1,0:T(8,128)S(1)} %get-tuple-element.9.readout_new, bf16[1024,384]{1,0:T(8,128)(2,1)S(1)} %get-tuple-element.10.left, ...), custom_call_target="tpu_custom_call" | custom-call | tf_op jit(solution)/shard_map/update/pallas_call | solution.py:670

commit v6 on v5

--- a/solution.py
+++ b/solution.py
@@ -101,17 +101,46 @@
     shape = (SUBS, BLOCK)
     lane = lax.broadcasted_iota(jnp.int32, shape, 1)
     sub = lax.broadcasted_iota(jnp.int32, shape, 0)
+    span = range(WIDE)
+
+    def column(row, k):
+        return jnp.broadcast_to(row[:, k : k + 1], shape)
+
+    def entry(col, r):
+        return jnp.broadcast_to(col[r % SUBS : r % SUBS + 1], shape)
+
+    s = None
     for k in range(0, BLOCK, WIDE):
         v, first = k // SUBS, k % SUBS
-        span = range(WIDE)
-        col = [[jnp.broadcast_to(row[:, k + b : k + b + 1], shape) for row in rows] for b in span]
-        s = [[jnp.broadcast_to(col[b][v][first + a : first + a + 1], shape) for b in range(a + 1)] for a in span]
+        col = [[column(row, k + b) for row in rows] for b in span]
+        if s is None:
+            s = [[entry(col[b][v], k + a) for b in range(a + 1)] for a in span]
+        after = k + WIDE
+        if after < BLOCK:
+            row = rows[after // SUBS]
+            ahead = [column(row, after + b) for b in span]
+            ahead = [[entry(ahead[b], after + a) for b in range(a + 1)] for a in span]
+            links = [[entry(col[b][after // SUBS], after + a) for b in span] for a in span]
         inside = (lane >= k) & (lane < k + WIDE)
         top = [
-            jnp.where(inside, jnp.where(lane == k + b, 1.0, 0.0), jnp.broadcast_to(rows[v][first + b : first + b + 1], shape))
+            jnp.where(inside, jnp.where(lane == k + b, 1.0, 0.0), entry(rows[v], first + b))
             for b in span
         ]
         l, rd = factor_four(s)
+        if after < BLOCK:
+            links = [eliminate(l, link) for link in links]
+            scaled = [[link[b] * rd[b] for b in span] for link in links]
+            s = [
+                [
+                    ahead[a][b]
+                    - (
+                        (scaled[a][0] * links[b][0] + scaled[a][1] * links[b][1])
+                        + (scaled[a][2] * links[b][2] + scaled[a][3] * links[b][3])
+                    )
+                    for b in range(a + 1)
+                ]
+                for a in span
+            ]
         top = eliminate(l, top)
         new = [None] * WIDE
         for a in reversed(span):
@@ -166,7 +195,7 @@
     rates_hbm, targets_hbm, goal_hbm, readout_hbm, corr_hbm, rec_hbm,
     scaled, readout_new, left, corr_v, rec_v,
     rates, rates_t, targets, goal, readout, rx,
-    g_part, g_mid, g_relay, g_sum, g_x, g_z, g_piece, g_all, g_hi, g_lo,
+    g_part, g_mid, g_relay, g_sum, g_x, g_zrelay, g_zsum, g_z, g_piece, g_all, g_hi, g_lo,
     e_part, e_hold, e_mid, e_relay, e_sum, e_x, e_low, e_z,
     kpart, krow, ksum, kz, kmid, kx, cap, minv,
     load_sem, send_sem, recv_sem,
@@ -244,19 +273,18 @@
         return {"row": ((y + d) % 4) * 4 + zl * 2 + c}
 
     class RingSum:
-        def __init__(self, part, hold, relay, total, landed):
-            self.part, self.hold, self.relay, self.total, self.landed = part, hold, relay, total, landed
+        def __init__(self, part, hold, relay, total, landed, dev):
+            self.hold, self.relay, self.total, self.landed = hold, relay, total, landed
             at = sems.take(6)
-            top, low = pl.ds(0, 2), pl.ds(2, 2)
             self.copies = [
-                remote(part.at[0, top], relay.at[0], at, x_dev(1)),
-                remote(part.at[0, low], relay.at[1], at + 1, x_dev(3)),
-                remote(part.at[1, low], landed.at[0], at + 2, x_dev(1), at + 2),
-                remote(part.at[2, top], landed.at[1], at + 3, x_dev(3), at + 2),
-                remote(total.at[0], landed.at[2], at + 4, x_dev(1), at + 2),
-                remote(total.at[1], landed.at[3], at + 5, x_dev(3), at + 2),
+                remote(part(0, 0), relay.at[0], at, dev(1)),
+                remote(part(0, 1), relay.at[1], at + 1, dev(3)),
+                remote(part(1, 1), landed.at[0], at + 2, dev(1), at + 2),
+                remote(part(2, 0), landed.at[1], at + 3, dev(3), at + 2),
+                remote(total.at[0], landed.at[2], at + 4, dev(1), at + 2),
+                remote(total.at[1], landed.at[3], at + 5, dev(3), at + 2),
             ]
-            self.all = remote(landed, landed, at + 2, x_dev(1))
+            self.all = remote(landed, landed, at + 2, dev(1))
 
         def start(self, *which):
             for k in which:
@@ -268,11 +296,10 @@
                 self.total[k] = (self.hold(k) + self.relay[k].astype(F32)).astype(self.total.dtype)
                 self.copies[4 + k].start()
 
-        def finish(self, own):
+        def finish(self):
             self.all.wait_recv()
             got = [self.landed[k].astype(F32) for k in range(4)]
-            own[:2] = own[:2] + got[2] + got[1]
-            own[2:] = own[2:] + got[0] + got[3]
+            return got[2] + got[1], got[0] + got[3]
 
         def wait_sends(self):
             for copy in self.copies:
@@ -323,29 +350,33 @@
         value = jnp.dot(rec_v[quarter(x + d), :], rates_t[...], preferred_element_type=F32)
         return [fold(part) for part in groups(value)]
 
-    g_ring = RingSum(g_part, lambda k: g_part[1, :2] if k == 0 else g_part[2, 2:], g_relay, g_sum, g_x)
+    pl.semaphore_wait(barrier, jnp.where(i == j, jnp.where(zl == c, 22, 23), 24))
+    r_t = sems.take(1)
+    r_src = rates.at[:, quarter(y)]
+
+    @pl.when(i != j)
+    def _():
+        remote(r_src, rx, r_t, {"row": j, "col": i}).start()
+
+    @pl.when(i == j)
+    def _():
+        pltpu.make_async_copy(r_src, rx, recv_sem.at[r_t]).start()
+
+    def pairs(part):
+        return lambda which, half: part.at[which, pl.ds(2 * half, 2)]
+
+    g_ring = RingSum(
+        pairs(g_part), lambda k: g_part[1, :2] if k == 0 else g_part[2, 2:], g_relay, g_sum, g_x, x_dev
+    )
     prod_quarter(2, g_part.at[0])
-    pl.semaphore_wait(barrier, jnp.where(i == j, jnp.where(zl == c, 22, 23), 24))
     g_ring.start(0, 1)
     prod_quarter(1, g_part.at[1])
     g_ring.start(2)
     prod_quarter(3, g_part.at[2])
     g_ring.start(3)
-
-    r_t = sems.take(1)
-    r_src = rates.at[:, quarter(y)]
-
-    @pl.when(i != j)
-    def _():
-        remote(r_src, rx, r_t, {"row": j, "col": i}).start()
-
-    @pl.when(i == j)
-    def _():
-        pltpu.make_async_copy(r_src, rx, recv_sem.at[r_t]).start()
-
     prod_quarter(0, g_mid)
 
-    e_ring = RingSum(e_part, lambda k: e_hold[k], e_relay, e_sum, e_x)
+    e_ring = RingSum(pairs(e_part), lambda k: e_hold[k], e_relay, e_sum, e_x, x_dev)
     for g, part in enumerate(drive_quarter(2)):
         e_part[0, g] = part.astype(BF)
     g_ring.forward()
@@ -370,15 +401,6 @@
     kpart[3 * BLOCK : 3 * BLOCK + OUTS, :] = guess[:, :LANES]
     kpart[3 * BLOCK + OUTS :, :] = jnp.concatenate([guess[:, LANES:], guess[:, LANES:]], axis=1)
 
-    g_ring.finish(g_mid)
-    g_at = sems.take(3)
-
-    def g_z_copy(d):
-        return remote(g_mid.at[(zh + d) % 4], g_z.at[d - 1], g_at + d - 1, z_dev(d), g_at)
-
-    for d in range(1, 4):
-        g_z_copy(d).start()
-
     @pl.when(i != j)
     def _():
         remote(r_src, rx, r_t, {"row": j, "col": i}).wait_recv()
@@ -387,6 +409,9 @@
     def _():
         pltpu.make_async_copy(r_src, rx, recv_sem.at[r_t]).wait()
 
+    got = g_ring.finish()
+    for k in range(2):
+        g_mid[2 * k : 2 * k + 2] = g_mid[2 * k : 2 * k + 2] + got[k]
     whole = sum(
         jnp.dot(rx[...], term, preferred_element_type=F32)
         for term in split2(jnp.concatenate([unfold(g_mid[g]) for g in range(4)], axis=0))
@@ -405,36 +430,18 @@
         def _():
             remote(kpart.at[aligned(owner * PIECE, PIECE)], krow.at[d - 1], k_r, {"row": owner}).start()
 
+    def g_slice(which, half):
+        return g_mid.at[(zh + (2, 1, 3)[which]) % 4, pl.ds(half * (FOLDED // 2), FOLDED // 2)]
+
+    z_ring = RingSum(g_slice, lambda k: g_slice(k + 1, k)[...], g_zrelay, g_zsum, g_z, z_dev)
+    z_ring.start(0, 1, 2, 3)
+
     e_ring.forward()
     for g, part in enumerate(drive_quarter(0)):
         e_mid[g] = part
 
-    remote(g_z, g_z, g_at, z_dev(1)).wait_recv()
-    piece = g_mid[zh] + g_z[0] + g_z[1] + g_z[2]
-    g_piece[...] = piece
-    own = aligned(x * QUARTER + zh * GROUP, GROUP)
-    left[own, STEPS:] = unfold(piece).astype(BF)
-    s_t = sems.take(2)
-
-    def swap_each(act_remote, act_local):
-        for e in range(2):
-            dst = g_all.at[x, zh]
-            row = x * 4 + e * 2 + zh // 2
-
-            @pl.when((i != j) | (row != i))
-            def _():
-                act_remote(remote(g_piece, dst, s_t + e, {"row": row, "col": i}, s_t + zh % 2))
-
-            if act_local is not None:
-
-                @pl.when((i == j) & (row == i))
-                def _():
-                    act_local(pltpu.make_async_copy(g_piece, dst, recv_sem.at[s_t + zh % 2]))
-
-    swap_each(lambda copy: copy.start(), lambda copy: copy.start())
-
+    k_x = sems.take(3)
     k_z = sems.take(3)
-    k_x = sems.take(3)
 
     @pl.when(i < OWNERS)
     def _():
@@ -444,10 +451,15 @@
             acc = acc + krow[d]
         ksum[...] = acc
         for d in range(1, 4):
-            remote(ksum, kz.at[d - 1], k_z + d - 1, z_dev(d), k_z).start()
-
-    e_ring.finish(e_mid)
-    e_low[...] = e_mid[...].astype(BF)
+            remote(ksum, kx.at[d - 1], k_x + d - 1, x_dev(d), k_x).start()
+
+    z_ring.forward()
+
+    got = e_ring.finish()
+    for k in range(2):
+        total = e_mid[2 * k : 2 * k + 2] + got[k]
+        e_mid[2 * k : 2 * k + 2] = total
+        e_low[2 * k : 2 * k + 2] = total.astype(BF)
     e_at = sems.take(3)
 
     def e_z_copy(d):
@@ -458,61 +470,77 @@
 
     @pl.when(i < OWNERS)
     def _():
-        remote(kz, kz, k_z, z_dev(1)).wait_recv()
-        kmid[...] = ksum[...] + kz[0] + kz[1] + kz[2]
+        remote(kx, kx, k_x, x_dev(1)).wait_recv()
+        kmid[...] = ksum[...] + kx[0] + kx[1] + kx[2]
         for d in range(1, 4):
-            remote(kmid, kx.at[d - 1], k_x + d - 1, x_dev(d), k_x).start()
+            remote(kmid, kz.at[d - 1], k_z + d - 1, z_dev(d), k_z).start()
 
     targets_load.wait()
     aims = targets[:, quarter(x)].T
     e_hold[0] = jnp.stack([fold(part) for part in groups(aims[:LANES].astype(F32))])
     e_hold[1] = jnp.stack([fold(part) for part in groups(aims[LANES:].astype(F32))])
 
-    for z in range(2):
-        source = y * 4 + 2 * c + z
-        dst = g_all.at[y, 2 * c + z]
-
-        @pl.when((i != j) | (source != j))
-        def _():
-            remote(g_piece, dst, s_t, {"row": j, "col": source}, s_t + z).wait_recv()
-
-        @pl.when((i == j) & (source == j))
-        def _():
-            pltpu.make_async_copy(g_piece, dst, recv_sem.at[s_t + z]).wait()
-
-    y_ring = Ring(lambda half, owner: g_all.at[owner, 2 * c + half], y, y_dev)
-    y_ring.start()
+    got = z_ring.finish()
+    for k in range(2):
+        part = pl.ds(k * (FOLDED // 2), FOLDED // 2)
+        g_piece[part, :] = g_mid[zh, part, :] + got[k]
+    own = aligned(x * QUARTER + zh * GROUP, GROUP)
+    s_t = sems.take(2)
+
+    def swap_each(act_remote, act_local):
+        for e in range(2):
+            dst = g_all.at[x, zh]
+            row = x * 4 + e * 2 + zh // 2
+
+            @pl.when((i != j) | (row != i))
+            def _():
+                act_remote(remote(g_piece, dst, s_t + e, {"row": row, "col": i}, s_t + zh % 2))
+
+            if act_local is not None:
+
+                @pl.when((i == j) & (row == i))
+                def _():
+                    act_local(pltpu.make_async_copy(g_piece, dst, recv_sem.at[s_t + zh % 2]))
+
+    swap_each(lambda copy: copy.start(), lambda copy: copy.start())
+    left[own, STEPS:] = unfold(g_piece[...]).astype(BF)
 
     remote(e_z, e_z, e_at, z_dev(1)).wait_recv()
     total = e_mid[zh] - e_hold[zh // 2, zh % 2]
     for d in range(3):
         total = total + e_z[d].astype(F32)
     left[own, :STEPS] = unfold(total).astype(BF)
-    l_z = sems.take(3)
-
-    def l_z_copy(d, z):
-        rows = left.at[aligned(x * QUARTER + (z % 4) * GROUP, GROUP)]
-        return remote(rows, rows, l_z + d - 1, z_dev(d))
-
-    for d in range(1, 4):
-        l_z_copy(d, zh).start()
+    lz_ring = Ring(
+        lambda half, owner: left.at[aligned(x * QUARTER + owner * GROUP + half * (GROUP // 2), GROUP // 2)], zh, z_dev
+    )
+    lz_ring.start()
 
     k_g = sems.take(1)
     own_rows = aligned(i * PIECE, PIECE)
 
     @pl.when(i < OWNERS)
     def _():
-        remote(kx, kx, k_x, x_dev(1)).wait_recv()
-        cap[own_rows, :] = kmid[...] + kx[0] + kx[1] + kx[2]
+        remote(kz, kz, k_z, z_dev(1)).wait_recv()
+        cap[own_rows, :] = kmid[...] + kz[0] + kz[1] + kz[2]
         for d in range(1, 16):
             remote(cap.at[own_rows], cap.at[own_rows], k_g, {"row": (i + d) % 16}).start()
 
-    y_ring.forward()
-
-    for d in range(1, 4):
-        l_z_copy(d, zh + 4 - d).wait_recv()
+    for z in range(2):
+        source = y * 4 + 2 * c + z
+        dst = g_all.at[y, 2 * c + z]
+
+        @pl.when((i != j) | (source != j))
+        def _():
+            remote(g_piece, dst, s_t, {"row": j, "col": source}, s_t + z).wait_recv()
+
+        @pl.when((i == j) & (source == j))
+        def _():
+            pltpu.make_async_copy(g_piece, dst, recv_sem.at[s_t + z]).wait()
+
+    y_ring = Ring(lambda half, owner: g_all.at[owner, 2 * c + half], y, y_dev)
+    y_ring.start()
+    lz_ring.forward()
     l_ring = Ring(lambda half, owner: left.at[aligned(owner * QUARTER + half * LANES, LANES)], x, x_dev)
-    l_ring.start()
 
     others = cap.at[pl.ds(0, PACKED - PIECE)]
 
@@ -531,6 +559,10 @@
     sibling = {"row": i + 1 - 2 * c}
     mine = g_all.at[:, pl.ds(2 * c, 2)]
     theirs = g_all.at[:, pl.ds(2 - 2 * c, 2)]
+
+    def serve_left():
+        lz_ring.finish()
+        l_ring.start()
 
     def serve_y():
         y_ring.finish()
@@ -547,7 +579,7 @@
                 g_hi[rows, :] = hi
                 g_lo[rows, :] = lo
 
-    invert(cap, minv, iter((rest, rest, l_ring.forward, rest, rest, serve_y, rest, rest, serve_core)))
+    invert(cap, minv, iter((serve_left, y_ring.forward, rest, rest, l_ring.forward, rest, serve_y, rest, rest, serve_core)))
 
     m_hi, m_lo = split2(minv[...])
     value = sum(
@@ -566,10 +598,8 @@
 
     swap_each(lambda copy: copy.wait_send(), None)
     for d in range(1, 4):
-        g_z_copy(d).wait_send()
         e_z_copy(d).wait_send()
-        l_z_copy(d, zh).wait_send()
-    for ring in (g_ring, e_ring, y_ring, l_ring):
+    for ring in (g_ring, e_ring, z_ring, lz_ring, y_ring, l_ring):
         ring.wait_sends()
 
     some = kpart.at[pl.ds(0, PACKED - PIECE)]
@@ -621,7 +651,9 @@
             folded(F32, 2, 2),
             folded(F32, 2, 2),
             folded(F32, 4, 2),
-            folded(F32, 3),
+            pltpu.VMEM((2, FOLDED // 2, LANES), F32),
+            pltpu.VMEM((2, FOLDED // 2, LANES), F32),
+            pltpu.VMEM((4, FOLDED // 2, LANES), F32),
             folded(F32),
             folded(F32, 4, 4),
             pltpu.VMEM((LOCAL, STEPS), BF),

time: 66.6 us -> 64.1 us (0.962)
  Pallas kernels: 65.8 us -> 62.9 us
    pallas_call x1, Pallas kernels: 62.2 us -> 59.3 us  [gather_all(): pl.pallas_call(comm_kernel, out_shape=[jax.ShapeDtypeStruct((STEPS, LOCAL...]
where the time goes in v6:
time: 64.1 us; the launch traced here: 63.5 us
  Pallas kernels  62.9 us (98%)
    pallas_call x1, Pallas kernels, gather_all(): pl.pallas_call(comm_kernel, out_shape=[jax.ShapeDtypeStruct((STEPS, LOCAL...  59.3 us
    pallas_call x1, Pallas kernels, update(): pl.pallas_call(update_kernel, grid=(LOCAL // TILE,), out_shape=[jax.Shape...  3.53 us

profile of v6, /device:TPU:1, one launch (start us, length us, event | category | flops | bytes accessed | tf_op | source)
XLA Modules:
  0.0 63.5 jit_solution(14120417003995765883)
XLA Ops:
  0.6 59.3 %exchange.1 = (bf16[192,1024]{1,0:T(8,128)(2,1)S(1)}, f32[16,1024]{1,0:T(8,128)S(1)}, bf16[1024,384]{1,0:T(8,128)(2,1)S(1)}, f32[1024,1024]{1,0:T(8,128)S(1)}, bf16[1024,1024]{1,0:T(8,128)(2,1)S(1)}) custom-call(bf16[192,1024]{1,0:T(8,128)(2,1)} %rates_hbm.1, bf16[192,1024]{1,0:T(8,128)(2,1)} %targets_hbm.1, f32[16,192]{1,0:T(8,128)} %goal_hbm.1, ...), custom_call_target="tpu_custom_call" | custom-call | tf_op jit(solution)/shard_map/exchange/pallas_call | solution.py:631
  60.0 3.5 %update.1 = (f32[1024,1024]{1,0:T(8,128)}, bf16[1024,1024]{1,0:T(8,128)(2,1)}, f32[16,1024]{1,0:T(8,128)}) custom-call(bf16[192,1024]{1,0:T(8,128)(2,1)S(1)} %get-tuple-element.8.scaled, f32[16,1024]{1,0:T(8,128)S(1)} %get-tuple-element.9.readout_new, bf16[1024,384]{1,0:T(8,128)(2,1)S(1)} %get-tuple-element.10.left, ...), custom_call_target="tpu_custom_call" | custom-call | tf_op jit(solution)/shard_map/update/pallas_call | solution.py:702

commit v7 on v6

--- a/solution.py
+++ b/solution.py
@@ -193,10 +193,11 @@
 
 def comm_kernel(
     rates_hbm, targets_hbm, goal_hbm, readout_hbm, corr_hbm, rec_hbm,
-    scaled, readout_new, left, corr_v, rec_v,
+    scaled, readout_new, e_all, corr_v, rec_v,
     rates, rates_t, targets, goal, readout, rx,
     g_part, g_mid, g_relay, g_sum, g_x, g_zrelay, g_zsum, g_z, g_piece, g_all, g_hi, g_lo,
-    e_part, e_hold, e_mid, e_relay, e_sum, e_x, e_low, e_z,
+    g_left,
+    e_part, e_hold, e_aim, e_mid, e_relay, e_sum, e_x, e_low, e_zrelay, e_zsum, e_z,
     kpart, krow, ksum, kz, kmid, kx, cap, minv,
     load_sem, send_sem, recv_sem,
 ):
@@ -401,6 +402,13 @@
     kpart[3 * BLOCK : 3 * BLOCK + OUTS, :] = guess[:, :LANES]
     kpart[3 * BLOCK + OUTS :, :] = jnp.concatenate([guess[:, LANES:], guess[:, LANES:]], axis=1)
 
+    for g, part in enumerate(drive_quarter(0)):
+        e_mid[g] = part
+    targets_load.wait()
+    aims = targets[:, quarter(x)].T.astype(F32)
+    for g, part in enumerate(groups(aims)):
+        e_aim[g] = fold(part)
+
     @pl.when(i != j)
     def _():
         remote(r_src, rx, r_t, {"row": j, "col": i}).wait_recv()
@@ -412,6 +420,13 @@
     got = g_ring.finish()
     for k in range(2):
         g_mid[2 * k : 2 * k + 2] = g_mid[2 * k : 2 * k + 2] + got[k]
+
+    def g_slice(which, half):
+        return g_mid.at[(zh + (2, 1, 3)[which]) % 4, pl.ds(half * (FOLDED // 2), FOLDED // 2)]
+
+    z_ring = RingSum(g_slice, lambda k: g_slice(k + 1, k)[...], g_zrelay, g_zsum, g_z, z_dev)
+    z_ring.start(0, 1, 2, 3)
+
     whole = sum(
         jnp.dot(rx[...], term, preferred_element_type=F32)
         for term in split2(jnp.concatenate([unfold(g_mid[g]) for g in range(4)], axis=0))
@@ -421,6 +436,8 @@
     kpart[BLOCK : 2 * BLOCK, :] = jnp.concatenate([kb[2][2], kb[1][0]], axis=1)
     kpart[2 * BLOCK : 3 * BLOCK, :] = jnp.concatenate([kb[2][0], kb[2][1]], axis=1)
 
+    e_ring.forward()
+
     k_r = sems.take(1)
 
     for d in range(1, 16):
@@ -430,16 +447,7 @@
         def _():
             remote(kpart.at[aligned(owner * PIECE, PIECE)], krow.at[d - 1], k_r, {"row": owner}).start()
 
-    def g_slice(which, half):
-        return g_mid.at[(zh + (2, 1, 3)[which]) % 4, pl.ds(half * (FOLDED // 2), FOLDED // 2)]
-
-    z_ring = RingSum(g_slice, lambda k: g_slice(k + 1, k)[...], g_zrelay, g_zsum, g_z, z_dev)
-    z_ring.start(0, 1, 2, 3)
-
-    e_ring.forward()
-    for g, part in enumerate(drive_quarter(0)):
-        e_mid[g] = part
-
+    z_ring.forward()
     k_x = sems.take(3)
     k_z = sems.take(3)
 
@@ -453,20 +461,54 @@
         for d in range(1, 4):
             remote(ksum, kx.at[d - 1], k_x + d - 1, x_dev(d), k_x).start()
 
-    z_ring.forward()
-
     got = e_ring.finish()
     for k in range(2):
         total = e_mid[2 * k : 2 * k + 2] + got[k]
         e_mid[2 * k : 2 * k + 2] = total
         e_low[2 * k : 2 * k + 2] = total.astype(BF)
-    e_at = sems.take(3)
-
-    def e_z_copy(d):
-        return remote(e_low.at[(zh + d) % 4], e_z.at[d - 1], e_at + d - 1, z_dev(d), e_at)
-
-    for d in range(1, 4):
-        e_z_copy(d).start()
+
+    def e_slice(buf, which, half):
+        return buf.at[(zh + (2, 1, 3)[which]) % 4, pl.ds(half * (FOLDED // 2), FOLDED // 2)]
+
+    ez_ring = RingSum(
+        functools.partial(e_slice, e_low), lambda k: e_slice(e_mid, k + 1, k)[...], e_zrelay, e_zsum, e_z, z_dev
+    )
+    ez_ring.start(0, 1, 2, 3)
+
+    got = z_ring.finish()
+    for k in range(2):
+        part = pl.ds(k * (FOLDED // 2), FOLDED // 2)
+        g_piece[part, :] = g_mid[zh, part, :] + got[k]
+    s_t = sems.take(2)
+
+    def swap_each(act_remote, act_local):
+        for e in range(2):
+            dst = g_all.at[x, zh]
+            row = x * 4 + e * 2 + zh // 2
+
+            @pl.when((i != j) | (row != i))
+            def _():
+                act_remote(remote(g_piece, dst, s_t + e, {"row": row, "col": i}, s_t + zh % 2))
+
+            if act_local is not None:
+
+                @pl.when((i == j) & (row == i))
+                def _():
+                    act_local(pltpu.make_async_copy(g_piece, dst, recv_sem.at[s_t + zh % 2]))
+
+    swap_each(lambda copy: copy.start(), lambda copy: copy.start())
+
+    def z_gather(buf):
+        return Ring(
+            lambda half, owner: buf.at[x, owner, pl.ds(half * (FOLDED // 2), FOLDED // 2)], zh, z_dev
+        )
+
+    def x_gather(buf):
+        return Ring(lambda half, owner: buf.at[owner, pl.ds(2 * half, 2)], x, x_dev)
+
+    g_left[x, zh] = g_piece[...].astype(BF)
+    gz_gather = z_gather(g_left)
+    gz_gather.start()
 
     @pl.when(i < OWNERS)
     def _():
@@ -475,45 +517,8 @@
         for d in range(1, 4):
             remote(kmid, kz.at[d - 1], k_z + d - 1, z_dev(d), k_z).start()
 
-    targets_load.wait()
-    aims = targets[:, quarter(x)].T
-    e_hold[0] = jnp.stack([fold(part) for part in groups(aims[:LANES].astype(F32))])
-    e_hold[1] = jnp.stack([fold(part) for part in groups(aims[LANES:].astype(F32))])
-
-    got = z_ring.finish()
-    for k in range(2):
-        part = pl.ds(k * (FOLDED // 2), FOLDED // 2)
-        g_piece[part, :] = g_mid[zh, part, :] + got[k]
-    own = aligned(x * QUARTER + zh * GROUP, GROUP)
-    s_t = sems.take(2)
-
-    def swap_each(act_remote, act_local):
-        for e in range(2):
-            dst = g_all.at[x, zh]
-            row = x * 4 + e * 2 + zh // 2
-
-            @pl.when((i != j) | (row != i))
-            def _():
-                act_remote(remote(g_piece, dst, s_t + e, {"row": row, "col": i}, s_t + zh % 2))
-
-            if act_local is not None:
-
-                @pl.when((i == j) & (row == i))
-                def _():
-                    act_local(pltpu.make_async_copy(g_piece, dst, recv_sem.at[s_t + zh % 2]))
-
-    swap_each(lambda copy: copy.start(), lambda copy: copy.start())
-    left[own, STEPS:] = unfold(g_piece[...]).astype(BF)
-
-    remote(e_z, e_z, e_at, z_dev(1)).wait_recv()
-    total = e_mid[zh] - e_hold[zh // 2, zh % 2]
-    for d in range(3):
-        total = total + e_z[d].astype(F32)
-    left[own, :STEPS] = unfold(total).astype(BF)
-    lz_ring = Ring(
-        lambda half, owner: left.at[aligned(x * QUARTER + owner * GROUP + half * (GROUP // 2), GROUP // 2)], zh, z_dev
-    )
-    lz_ring.start()
+    ez_ring.forward()
+    gz_gather.forward()
 
     k_g = sems.take(1)
     own_rows = aligned(i * PIECE, PIECE)
@@ -525,6 +530,13 @@
         for d in range(1, 16):
             remote(cap.at[own_rows], cap.at[own_rows], k_g, {"row": (i + d) % 16}).start()
 
+    got = ez_ring.finish()
+    for k in range(2):
+        part = pl.ds(k * (FOLDED // 2), FOLDED // 2)
+        e_all[x, zh, part, :] = (e_mid[zh, part, :] + got[k] - e_aim[zh, part, :]).astype(BF)
+    ez_gather = z_gather(e_all)
+    ez_gather.start()
+
     for z in range(2):
         source = y * 4 + 2 * c + z
         dst = g_all.at[y, 2 * c + z]
@@ -539,8 +551,11 @@
 
     y_ring = Ring(lambda half, owner: g_all.at[owner, 2 * c + half], y, y_dev)
     y_ring.start()
-    lz_ring.forward()
-    l_ring = Ring(lambda half, owner: left.at[aligned(owner * QUARTER + half * LANES, LANES)], x, x_dev)
+    gz_gather.finish()
+    gx_gather = x_gather(g_left)
+    gx_gather.start()
+    ex_gather = x_gather(e_all)
+    ez_gather.forward()
 
     others = cap.at[pl.ds(0, PACKED - PIECE)]
 
@@ -560,9 +575,9 @@
     mine = g_all.at[:, pl.ds(2 * c, 2)]
     theirs = g_all.at[:, pl.ds(2 - 2 * c, 2)]
 
-    def serve_left():
-        lz_ring.finish()
-        l_ring.start()
+    def serve_error():
+        ez_gather.finish()
+        ex_gather.start()
 
     def serve_y():
         y_ring.finish()
@@ -579,7 +594,10 @@
                 g_hi[rows, :] = hi
                 g_lo[rows, :] = lo
 
-    invert(cap, minv, iter((serve_left, y_ring.forward, rest, rest, l_ring.forward, rest, serve_y, rest, rest, serve_core)))
+    invert(
+        cap, minv,
+        iter((serve_error, y_ring.forward, gx_gather.forward, rest, ex_gather.forward, serve_y, rest, rest, serve_core)),
+    )
 
     m_hi, m_lo = split2(minv[...])
     value = sum(
@@ -590,16 +608,22 @@
     goal_load.wait()
     guess = jnp.concatenate([cap[3 * BLOCK : 3 * BLOCK + OUTS, :], cap[3 * BLOCK + OUTS :, : STEPS - LANES]], axis=1)
     readout_new[...] = readout[...] - dot32(guess - goal[...], value)
-    l_ring.finish()
+    gx_gather.finish()
+
+    @pl.loop(0, 4)
+    def _(q):
+        factor = jnp.concatenate([unfold(g_left[q, g]) for g in range(4)], axis=0)
+        rows = quarter(q)
+        corr_v[rows, :] = corr_v[rows, :] - jnp.dot(factor, scaled[...], preferred_element_type=F32)
+
+    ex_gather.finish()
 
     @pl.when(i != j)
     def _():
         remote(r_src, rx, r_t, {"row": j, "col": i}).wait_send()
 
     swap_each(lambda copy: copy.wait_send(), None)
-    for d in range(1, 4):
-        e_z_copy(d).wait_send()
-    for ring in (g_ring, e_ring, z_ring, lz_ring, y_ring, l_ring):
+    for ring in (g_ring, e_ring, z_ring, ez_ring, gz_gather, gx_gather, ez_gather, ex_gather, y_ring):
         ring.wait_sends()
 
     some = kpart.at[pl.ds(0, PACKED - PIECE)]
@@ -633,7 +657,7 @@
         out_shape=[
             jax.ShapeDtypeStruct((STEPS, LOCAL), BF),
             jax.ShapeDtypeStruct((OUTS, LOCAL), F32),
-            jax.ShapeDtypeStruct((LOCAL, 2 * STEPS), BF),
+            jax.ShapeDtypeStruct((4, 4, FOLDED, LANES), BF),
             jax.ShapeDtypeStruct((LOCAL, LOCAL), F32),
             jax.ShapeDtypeStruct((LOCAL, LOCAL), BF),
         ],
@@ -658,14 +682,18 @@
             folded(F32, 4, 4),
             pltpu.VMEM((LOCAL, STEPS), BF),
             pltpu.VMEM((LOCAL, STEPS), BF),
+            folded(BF, 4, 4),
             folded(BF, 3, 4),
             folded(F32, 2, 2),
+            folded(F32, 4),
             folded(F32, 4),
             folded(BF, 2, 2),
             folded(BF, 2, 2),
             folded(BF, 4, 2),
             folded(BF, 4),
-            folded(BF, 3),
+            pltpu.VMEM((2, FOLDED // 2, LANES), BF),
+            pltpu.VMEM((2, FOLDED // 2, LANES), BF),
+            pltpu.VMEM((4, FOLDED // 2, LANES), BF),
             pltpu.VMEM((PACKED, LANES), F32),
             pltpu.VMEM((15, PIECE, LANES), F32),
             pltpu.VMEM((PIECE, LANES), F32),
@@ -685,33 +713,38 @@
     )(rates, targets, goal, readout, corr, rec)
 
 
-TILE = 256
-
-
-def update_kernel(scaled, readout_new, left, corr, rec, corr_out, rec_out, readout_out):
-    rows = aligned(pl.program_id(0) * TILE, TILE)
-    drop = jnp.dot(left[rows, STEPS:], scaled[...], preferred_element_type=F32)
-    corr_out[...] = corr[rows, :] - drop
-    drop = jnp.dot(left[rows, :STEPS], scaled[...], preferred_element_type=F32)
-    rec_out[...] = (rec[rows, :].astype(F32) - drop).astype(BF)
-    readout_out[...] = readout_new[...]
-
-
-def update(scaled, readout_new, left, corr, rec):
-    rows = pl.BlockSpec((TILE, LOCAL), lambda g: (g, 0))
+def update_kernel(scaled, readout_new, e_all, corr, rec, corr_out, rec_out, readout_out, fresh, sems):
+    copies = [
+        pltpu.make_async_copy(corr, corr_out, sems.at[0]),
+        pltpu.make_async_copy(readout_new, readout_out, sems.at[1]),
+    ]
+    for copy in copies:
+        copy.start()
+    for q in range(4):
+        rows = pl.ds(q * QUARTER, QUARTER)
+        factor = jnp.concatenate([unfold(e_all[q, g]) for g in range(4)], axis=0)
+        drop = jnp.dot(factor, scaled[...], preferred_element_type=F32)
+        fresh[rows, :] = (rec[rows, :].astype(F32) - drop).astype(BF)
+        copies.append(pltpu.make_async_copy(fresh.at[rows], rec_out.at[rows], sems.at[2 + q]))
+        copies[-1].start()
+    for copy in copies:
+        copy.wait()
+
+
+def update(scaled, readout_new, e_all, corr, rec):
     return pl.pallas_call(
         update_kernel,
-        grid=(LOCAL // TILE,),
         out_shape=[
             jax.ShapeDtypeStruct((LOCAL, LOCAL), F32),
             jax.ShapeDtypeStruct((LOCAL, LOCAL), BF),
             jax.ShapeDtypeStruct((OUTS, LOCAL), F32),
         ],
         in_specs=[pl.BlockSpec(memory_space=pltpu.VMEM)] * 5,
-        out_specs=[rows, rows, pl.BlockSpec((OUTS, LOCAL), lambda g: (0, 0))],
+        out_specs=[pl.BlockSpec(memory_space=pl.ANY)] * 3,
+        scratch_shapes=[pltpu.VMEM((LOCAL, LOCAL), BF), pltpu.SemaphoreType.DMA((6,))],
         compiler_params=pltpu.CompilerParams(vmem_limit_bytes=VMEM_LIMIT),
         name="update",
-    )(scaled, readout_new, left, corr, rec)
+    )(scaled, readout_new, e_all, corr, rec)
 
 
 def on_device(*args):

time: 64.1 us -> 67.2 us (1.048)
  Pallas kernels: 62.9 us -> 66.3 us
    pallas_call x1, Pallas kernels: 59.3 us -> 63.6 us  [gather_all(): pl.pallas_call(comm_kernel, out_shape=[jax.ShapeDtypeStruct((STEPS, LOCAL...]
    pallas_call x1, Pallas kernels: 3.53 us -> 2.72 us  [update(): pl.pallas_call(update_kernel, out_shape=[jax.ShapeDtypeStruct((LOCAL, LOC...]
where the time goes in v7:
time: 67.2 us; the launch traced here: 67.1 us
  Pallas kernels  66.3 us (99%)
  between operations  0.8 us (1%)
    pallas_call x1, Pallas kernels, gather_all(): pl.pallas_call(comm_kernel, out_shape=[jax.ShapeDtypeStruct((STEPS, LOCAL...  63.6 us
    pallas_call x1, Pallas kernels, update(): pl.pallas_call(update_kernel, out_shape=[jax.ShapeDtypeStruct((LOCAL, LOC...  2.72 us

profile of v7, /device:TPU:1, one launch (start us, length us, event | category | flops | bytes accessed | tf_op | source)
XLA Modules:
  0.0 67.1 jit_solution(3179917561262679855)
XLA Ops:
  0.6 63.6 %exchange.1 = (bf16[192,1024]{1,0:T(8,128)(2,1)S(1)}, f32[16,1024]{1,0:T(8,128)S(1)}, bf16[4,4,96,128]{3,2,1,0:T(8,128)(2,1)S(1)}, f32[1024,1024]{1,0:T(8,128)S(1)}, bf16[1024,1024]{1,0:T(8,128)(2,1)S(1)}) custom-call(bf16[192,1024]{1,0:T(8,128)(2,1)} %rates_hbm.1, bf16[192,1024]{1,0:T(8,128)(2,1)} %targets_hbm.1, f32[16,192]{1,0:T(8,128)} %goal_hbm.1, ...), custom_call_target="tpu_custom_call" | custom-call | tf_op jit(solution)/shard_map/exchange/pallas_call | solution.py:655
  64.2 2.7 %update.1 = (f32[1024,1024]{1,0:T(8,128)}, bf16[1024,1024]{1,0:T(8,128)(2,1)}, f32[16,1024]{1,0:T(8,128)}) custom-call(bf16[192,1024]{1,0:T(8,128)(2,1)S(1)} %get-tuple-element.8.scaled, f32[16,1024]{1,0:T(8,128)S(1)} %get-tuple-element.9.readout_new, bf16[4,4,96,128]{3,2,1,0:T(8,128)(2,1)S(1)} %get-tuple-element.10.e_all, ...), custom_call_target="tpu_custom_call" | custom-call | tf_op jit(solution)/shard_map/update/pallas_call | solution.py:735

commit v8 on v6

--- a/solution.py
+++ b/solution.py
@@ -196,7 +196,7 @@
     scaled, readout_new, left, corr_v, rec_v,
     rates, rates_t, targets, goal, readout, rx,
     g_part, g_mid, g_relay, g_sum, g_x, g_zrelay, g_zsum, g_z, g_piece, g_all, g_hi, g_lo,
-    e_part, e_hold, e_mid, e_relay, e_sum, e_x, e_low, e_z,
+    e_part, e_hold, e_aim, e_mid, e_relay, e_sum, e_x, e_low, e_z,
     kpart, krow, ksum, kz, kmid, kx, cap, minv,
     load_sem, send_sem, recv_sem,
 ):
@@ -273,18 +273,19 @@
         return {"row": ((y + d) % 4) * 4 + zl * 2 + c}
 
     class RingSum:
-        def __init__(self, part, hold, relay, total, landed, dev):
+        def __init__(self, part, hold, relay, total, landed, sent, dev):
             self.hold, self.relay, self.total, self.landed = hold, relay, total, landed
-            at = sems.take(6)
+            at = sems.take(3)
             self.copies = [
-                remote(part(0, 0), relay.at[0], at, dev(1)),
-                remote(part(0, 1), relay.at[1], at + 1, dev(3)),
-                remote(part(1, 1), landed.at[0], at + 2, dev(1), at + 2),
-                remote(part(2, 0), landed.at[1], at + 3, dev(3), at + 2),
-                remote(total.at[0], landed.at[2], at + 4, dev(1), at + 2),
-                remote(total.at[1], landed.at[3], at + 5, dev(3), at + 2),
+                remote(part(0, 0), relay.at[0], at, dev(1), at),
+                remote(part(0, 1), relay.at[1], at, dev(3), at + 1),
+                remote(part(1, 1), landed.at[0], at, dev(1), at + 2),
+                remote(part(2, 0), landed.at[1], at, dev(3), at + 2),
+                remote(total.at[0], landed.at[2], at, dev(1), at + 2),
+                remote(total.at[1], landed.at[3], at, dev(3), at + 2),
             ]
-            self.all = remote(landed, landed, at + 2, dev(1))
+            self.arrived = remote(landed, landed, at, dev(1), at + 2)
+            self.sent = remote(sent, sent, at, dev(1))
 
         def start(self, *which):
             for k in which:
@@ -297,22 +298,24 @@
                 self.copies[4 + k].start()
 
         def finish(self):
-            self.all.wait_recv()
+            self.arrived.wait_recv()
             got = [self.landed[k].astype(F32) for k in range(4)]
             return got[2] + got[1], got[0] + got[3]
 
         def wait_sends(self):
-            for copy in self.copies:
-                copy.wait_send()
+            self.sent.wait_send()
 
     class Ring:
-        def __init__(self, block, me, dev):
+        def __init__(self, block, me, dev, four, six):
             self.block, self.me, self.dev = block, me, dev
-            self.at = sems.take(6)
+            self.at = sems.take(3)
+            self.arrived = remote(four, four, self.at, dev(1), self.at + 2)
+            self.sent = remote(six, six, self.at, dev(1))
 
         def copy(self, k, owner):
             block = self.block((0, 1, 1, 0, 0, 1)[k], owner % 4)
-            return remote(block, block, self.at + k, self.dev((1, 1, 3, 3, 1, 3)[k]))
+            land = self.at + (0, 2, 1, 2, 2, 2)[k]
+            return remote(block, block, self.at, self.dev((1, 1, 3, 3, 1, 3)[k]), land)
 
         def start(self):
             for k in (0, 2, 1, 3):
@@ -325,16 +328,10 @@
             self.copy(5, self.me + 1).start()
 
         def finish(self):
-            self.copy(1, self.me + 3).wait_recv()
-            self.copy(3, self.me + 1).wait_recv()
-            self.copy(4, self.me + 2).wait_recv()
-            self.copy(5, self.me + 2).wait_recv()
+            self.arrived.wait_recv()
 
         def wait_sends(self):
-            for k in range(4):
-                self.copy(k, self.me).wait_send()
-            self.copy(4, self.me + 3).wait_send()
-            self.copy(5, self.me + 1).wait_send()
+            self.sent.wait_send()
 
     def prod_quarter(d, out):
         corr_loads[d].wait()
@@ -366,7 +363,7 @@
         return lambda which, half: part.at[which, pl.ds(2 * half, 2)]
 
     g_ring = RingSum(
-        pairs(g_part), lambda k: g_part[1, :2] if k == 0 else g_part[2, 2:], g_relay, g_sum, g_x, x_dev
+        pairs(g_part), lambda k: g_part[1, :2] if k == 0 else g_part[2, 2:], g_relay, g_sum, g_x, g_part, x_dev
     )
     prod_quarter(2, g_part.at[0])
     g_ring.start(0, 1)
@@ -376,7 +373,7 @@
     g_ring.start(3)
     prod_quarter(0, g_mid)
 
-    e_ring = RingSum(pairs(e_part), lambda k: e_hold[k], e_relay, e_sum, e_x, x_dev)
+    e_ring = RingSum(pairs(e_part), lambda k: e_hold[k], e_relay, e_sum, e_x, e_part, x_dev)
     for g, part in enumerate(drive_quarter(2)):
         e_part[0, g] = part.astype(BF)
     g_ring.forward()
@@ -401,6 +398,13 @@
     kpart[3 * BLOCK : 3 * BLOCK + OUTS, :] = guess[:, :LANES]
     kpart[3 * BLOCK + OUTS :, :] = jnp.concatenate([guess[:, LANES:], guess[:, LANES:]], axis=1)
 
+    for g, part in enumerate(drive_quarter(0)):
+        e_mid[g] = part
+    targets_load.wait()
+    aims = targets[:, quarter(x)].T.astype(F32)
+    for g, part in enumerate(groups(aims)):
+        e_aim[g] = fold(part)
+
     @pl.when(i != j)
     def _():
         remote(r_src, rx, r_t, {"row": j, "col": i}).wait_recv()
@@ -412,6 +416,13 @@
     got = g_ring.finish()
     for k in range(2):
         g_mid[2 * k : 2 * k + 2] = g_mid[2 * k : 2 * k + 2] + got[k]
+
+    def g_slice(which, half):
+        return g_mid.at[(zh + (2, 1, 3)[which]) % 4, pl.ds(half * (FOLDED // 2), FOLDED // 2)]
+
+    z_ring = RingSum(g_slice, lambda k: g_slice(k + 1, k)[...], g_zrelay, g_zsum, g_z, g_part.at[0, pl.ds(0, 3)], z_dev)
+    z_ring.start(0, 1, 2, 3)
+
     whole = sum(
         jnp.dot(rx[...], term, preferred_element_type=F32)
         for term in split2(jnp.concatenate([unfold(g_mid[g]) for g in range(4)], axis=0))
@@ -421,6 +432,8 @@
     kpart[BLOCK : 2 * BLOCK, :] = jnp.concatenate([kb[2][2], kb[1][0]], axis=1)
     kpart[2 * BLOCK : 3 * BLOCK, :] = jnp.concatenate([kb[2][0], kb[2][1]], axis=1)
 
+    e_ring.forward()
+
     k_r = sems.take(1)
 
     for d in range(1, 16):
@@ -430,18 +443,9 @@
         def _():
             remote(kpart.at[aligned(owner * PIECE, PIECE)], krow.at[d - 1], k_r, {"row": owner}).start()
 
-    def g_slice(which, half):
-        return g_mid.at[(zh + (2, 1, 3)[which]) % 4, pl.ds(half * (FOLDED // 2), FOLDED // 2)]
-
-    z_ring = RingSum(g_slice, lambda k: g_slice(k + 1, k)[...], g_zrelay, g_zsum, g_z, z_dev)
-    z_ring.start(0, 1, 2, 3)
-
-    e_ring.forward()
-    for g, part in enumerate(drive_quarter(0)):
-        e_mid[g] = part
-
-    k_x = sems.take(3)
-    k_z = sems.take(3)
+    z_ring.forward()
+    k_x = sems.take(1)
+    k_z = sems.take(1)
 
     @pl.when(i < OWNERS)
     def _():
@@ -451,19 +455,17 @@
             acc = acc + krow[d]
         ksum[...] = acc
         for d in range(1, 4):
-            remote(ksum, kx.at[d - 1], k_x + d - 1, x_dev(d), k_x).start()
-
-    z_ring.forward()
+            remote(ksum, kx.at[d - 1], k_x, x_dev(d)).start()
 
     got = e_ring.finish()
     for k in range(2):
         total = e_mid[2 * k : 2 * k + 2] + got[k]
         e_mid[2 * k : 2 * k + 2] = total
         e_low[2 * k : 2 * k + 2] = total.astype(BF)
-    e_at = sems.take(3)
+    e_at = sems.take(1)
 
     def e_z_copy(d):
-        return remote(e_low.at[(zh + d) % 4], e_z.at[d - 1], e_at + d - 1, z_dev(d), e_at)
+        return remote(e_low.at[(zh + d) % 4], e_z.at[d - 1], e_at, z_dev(d))
 
     for d in range(1, 4):
         e_z_copy(d).start()
@@ -473,12 +475,7 @@
         remote(kx, kx, k_x, x_dev(1)).wait_recv()
         kmid[...] = ksum[...] + kx[0] + kx[1] + kx[2]
         for d in range(1, 4):
-            remote(kmid, kz.at[d - 1], k_z + d - 1, z_dev(d), k_z).start()
-
-    targets_load.wait()
-    aims = targets[:, quarter(x)].T
-    e_hold[0] = jnp.stack([fold(part) for part in groups(aims[:LANES].astype(F32))])
-    e_hold[1] = jnp.stack([fold(part) for part in groups(aims[LANES:].astype(F32))])
+            remote(kmid, kz.at[d - 1], k_z, z_dev(d)).start()
 
     got = z_ring.finish()
     for k in range(2):
@@ -506,12 +503,13 @@
     left[own, STEPS:] = unfold(g_piece[...]).astype(BF)
 
     remote(e_z, e_z, e_at, z_dev(1)).wait_recv()
-    total = e_mid[zh] - e_hold[zh // 2, zh % 2]
+    total = e_mid[zh] - e_aim[zh]
     for d in range(3):
         total = total + e_z[d].astype(F32)
     left[own, :STEPS] = unfold(total).astype(BF)
     lz_ring = Ring(
-        lambda half, owner: left.at[aligned(x * QUARTER + owner * GROUP + half * (GROUP // 2), GROUP // 2)], zh, z_dev
+        lambda half, owner: left.at[aligned(x * QUARTER + owner * GROUP + half * (GROUP // 2), GROUP // 2)], zh, z_dev,
+        left.at[pl.ds(0, 2 * GROUP)], left.at[pl.ds(0, 3 * GROUP)],
     )
     lz_ring.start()
 
@@ -537,10 +535,13 @@
         def _():
             pltpu.make_async_copy(g_piece, dst, recv_sem.at[s_t + z]).wait()
 
-    y_ring = Ring(lambda half, owner: g_all.at[owner, 2 * c + half], y, y_dev)
+    y_ring = Ring(lambda half, owner: g_all.at[owner, 2 * c + half], y, y_dev, g_all.at[0], g_all.at[pl.ds(0, 3), pl.ds(0, 2)])
     y_ring.start()
     lz_ring.forward()
-    l_ring = Ring(lambda half, owner: left.at[aligned(owner * QUARTER + half * LANES, LANES)], x, x_dev)
+    l_ring = Ring(
+        lambda half, owner: left.at[aligned(owner * QUARTER + half * LANES, LANES)], x, x_dev,
+        left.at[pl.ds(0, 2 * QUARTER)], left.at[pl.ds(0, 3 * QUARTER)],
+    )
 
     others = cap.at[pl.ds(0, PACKED - PIECE)]
 
@@ -597,8 +598,7 @@
         remote(r_src, rx, r_t, {"row": j, "col": i}).wait_send()
 
     swap_each(lambda copy: copy.wait_send(), None)
-    for d in range(1, 4):
-        e_z_copy(d).wait_send()
+    remote(e_z, e_z, e_at, z_dev(1)).wait_send()
     for ring in (g_ring, e_ring, z_ring, lz_ring, y_ring, l_ring):
         ring.wait_sends()
 
@@ -607,9 +607,8 @@
     @pl.when(i < OWNERS)
     def _():
         remote(some, some, k_r, {"row": (i + 1) % 16}).wait_send()
-        for d in range(1, 4):
-            remote(ksum, kz.at[d - 1], k_z + d - 1, z_dev(d)).wait_send()
-            remote(kmid, kx.at[d - 1], k_x + d - 1, x_dev(d)).wait_send()
+        remote(kx, kx, k_x, x_dev(1)).wait_send()
+        remote(kz, kz, k_z, z_dev(1)).wait_send()
         remote(krow, krow, k_g, {"row": (i + 1) % 16}).wait_send()
 
     @pl.when(i >= OWNERS)
@@ -661,6 +660,7 @@
             folded(BF, 3, 4),
             folded(F32, 2, 2),
             folded(F32, 4),
+            folded(F32, 4),
             folded(BF, 2, 2),
             folded(BF, 2, 2),
             folded(BF, 4, 2),

time: 64.1 us -> 63.5 us (level)
  no operation moved by 1% of the time
where the time goes in v8:
time: 63.5 us; the launch traced here: 63.4 us
  Pallas kernels  62.8 us (99%)
  between operations  0.64 us (1%)
    pallas_call x1, Pallas kernels, gather_all(): pl.pallas_call(comm_kernel, out_shape=[jax.ShapeDtypeStruct((STEPS, LOCAL...  59.3 us
    pallas_call x1, Pallas kernels, update(): pl.pallas_call(update_kernel, grid=(LOCAL // TILE,), out_shape=[jax.Shape...  3.53 us

profile of v8, /device:TPU:1, one launch (start us, length us, event | category | flops | bytes accessed | tf_op | source)
XLA Modules:
  0.0 63.4 jit_solution(2658987013383932708)
XLA Ops:
  0.6 59.3 %exchange.1 = (bf16[192,1024]{1,0:T(8,128)(2,1)S(1)}, f32[16,1024]{1,0:T(8,128)S(1)}, bf16[1024,384]{1,0:T(8,128)(2,1)S(1)}, f32[1024,1024]{1,0:T(8,128)S(1)}, bf16[1024,1024]{1,0:T(8,128)(2,1)S(1)}) custom-call(bf16[192,1024]{1,0:T(8,128)(2,1)} %rates_hbm.1, bf16[192,1024]{1,0:T(8,128)(2,1)} %targets_hbm.1, f32[16,192]{1,0:T(8,128)} %goal_hbm.1, ...), custom_call_target="tpu_custom_call" | custom-call | tf_op jit(solution)/shard_map/exchange/pallas_call | solution.py:630
  59.9 3.5 %update.1 = (f32[1024,1024]{1,0:T(8,128)}, bf16[1024,1024]{1,0:T(8,128)(2,1)}, f32[16,1024]{1,0:T(8,128)}) custom-call(bf16[192,1024]{1,0:T(8,128)(2,1)S(1)} %get-tuple-element.8.scaled, f32[16,1024]{1,0:T(8,128)S(1)} %get-tuple-element.9.readout_new, bf16[1024,384]{1,0:T(8,128)(2,1)S(1)} %get-tuple-element.10.left, ...), custom_call_target="tpu_custom_call" | custom-call | tf_op jit(solution)/shard_map/update/pallas_call | solution.py:702

commit v9 on v8

--- a/solution.py
+++ b/solution.py
@@ -444,6 +444,19 @@
             remote(kpart.at[aligned(owner * PIECE, PIECE)], krow.at[d - 1], k_r, {"row": owner}).start()
 
     z_ring.forward()
+    got = e_ring.finish()
+    for k in range(2):
+        total = e_mid[2 * k : 2 * k + 2] + got[k]
+        e_mid[2 * k : 2 * k + 2] = total
+        e_low[2 * k : 2 * k + 2] = total.astype(BF)
+    e_at = sems.take(1)
+
+    def e_z_copy(d):
+        return remote(e_low.at[(zh + d) % 4], e_z.at[d - 1], e_at, z_dev(d))
+
+    for d in range(1, 4):
+        e_z_copy(d).start()
+
     k_x = sems.take(1)
     k_z = sems.take(1)
 
@@ -457,18 +470,10 @@
         for d in range(1, 4):
             remote(ksum, kx.at[d - 1], k_x, x_dev(d)).start()
 
-    got = e_ring.finish()
+    got = z_ring.finish()
     for k in range(2):
-        total = e_mid[2 * k : 2 * k + 2] + got[k]
-        e_mid[2 * k : 2 * k + 2] = total
-        e_low[2 * k : 2 * k + 2] = total.astype(BF)
-    e_at = sems.take(1)
-
-    def e_z_copy(d):
-        return remote(e_low.at[(zh + d) % 4], e_z.at[d - 1], e_at, z_dev(d))
-
-    for d in range(1, 4):
-        e_z_copy(d).start()
+        part = pl.ds(k * (FOLDED // 2), FOLDED // 2)
+        g_piece[part, :] = g_mid[zh, part, :] + got[k]
 
     @pl.when(i < OWNERS)
     def _():
@@ -477,10 +482,6 @@
         for d in range(1, 4):
             remote(kmid, kz.at[d - 1], k_z, z_dev(d)).start()
 
-    got = z_ring.finish()
-    for k in range(2):
-        part = pl.ds(k * (FOLDED // 2), FOLDED // 2)
-        g_piece[part, :] = g_mid[zh, part, :] + got[k]
     own = aligned(x * QUARTER + zh * GROUP, GROUP)
     s_t = sems.take(2)
 
@@ -562,6 +563,7 @@
     theirs = g_all.at[:, pl.ds(2 - 2 * c, 2)]
 
     def serve_left():
+        y_ring.forward()
         lz_ring.finish()
         l_ring.start()
 
@@ -580,7 +582,8 @@
                 g_hi[rows, :] = hi
                 g_lo[rows, :] = lo
 
-    invert(cap, minv, iter((serve_left, y_ring.forward, rest, rest, l_ring.forward, rest, serve_y, rest, rest, serve_core)))
+    invert(cap, minv, iter((serve_left, rest, rest, rest, rest, rest, serve_y, l_ring.forward)))
+    serve_core()
 
     m_hi, m_lo = split2(minv[...])
     value = sum(

time: 63.5 us -> 64.9 us (1.022)
  the two profiles are of different devices: /device:TPU:1 before, /device:TPU:14 now
where the time goes in v9:
time: 64.9 us; the launch traced here: 64.8 us
  Pallas kernels  64.2 us (99%)
    pallas_call x1, Pallas kernels, gather_all(): pl.pallas_call(comm_kernel, out_shape=[jax.ShapeDtypeStruct((STEPS, LOCAL...  60.6 us
    pallas_call x1, Pallas kernels, update(): pl.pallas_call(update_kernel, grid=(LOCAL // TILE,), out_shape=[jax.Shape...  3.53 us

profile of v9, /device:TPU:14, one launch (start us, length us, event | category | flops | bytes accessed | tf_op | source)
XLA Modules:
  0.0 64.8 jit_solution(17950388597262215850)
XLA Ops:
  0.6 60.6 %exchange.1 = (bf16[192,1024]{1,0:T(8,128)(2,1)S(1)}, f32[16,1024]{1,0:T(8,128)S(1)}, bf16[1024,384]{1,0:T(8,128)(2,1)S(1)}, f32[1024,1024]{1,0:T(8,128)S(1)}, bf16[1024,1024]{1,0:T(8,128)(2,1)S(1)}) custom-call(bf16[192,1024]{1,0:T(8,128)(2,1)} %rates_hbm.1, bf16[192,1024]{1,0:T(8,128)(2,1)} %targets_hbm.1, f32[16,192]{1,0:T(8,128)} %goal_hbm.1, ...), custom_call_target="tpu_custom_call" | custom-call | tf_op jit(solution)/shard_map/exchange/pallas_call | solution.py:633
  61.3 3.5 %update.1 = (f32[1024,1024]{1,0:T(8,128)}, bf16[1024,1024]{1,0:T(8,128)(2,1)}, f32[16,1024]{1,0:T(8,128)}) custom-call(bf16[192,1024]{1,0:T(8,128)(2,1)S(1)} %get-tuple-element.8.scaled, f32[16,1024]{1,0:T(8,128)S(1)} %get-tuple-element.9.readout_new, bf16[1024,384]{1,0:T(8,128)(2,1)S(1)} %get-tuple-element.10.left, ...), custom_call_target="tpu_custom_call" | custom-call | tf_op jit(solution)/shard_map/update/pallas_call | solution.py:705

commit v10 on v8

--- a/solution.py
+++ b/solution.py
@@ -165,30 +165,31 @@
 
 
 def invert(cap, minv, services):
-    blocks = range(STEPS // BLOCK)
-    shape = (BLOCK, BLOCK)
-    eye = jnp.where(lax.broadcasted_iota(jnp.int32, shape, 0) == lax.broadcasted_iota(jnp.int32, shape, 1), 1.0, 0.0)
+    count = STEPS // BLOCK
+
+    def at(r):
+        return pl.ds(r * BLOCK, BLOCK)
+
     (k00, k11), (k22, k10), (k20, k21) = [
-        [cap[r * BLOCK : (r + 1) * BLOCK, :BLOCK], cap[r * BLOCK : (r + 1) * BLOCK, BLOCK:]] for r in blocks
+        [cap[at(r), :BLOCK], cap[at(r), BLOCK:]] for r in range(count)
     ]
-    a = [[k00 + eye, k10.T, k20.T], [k10, k11 + eye, k21.T], [k20, k21, k22 + eye]]
-    for k in blocks:
-        inv = inverse_block(a[k][k], services)
-        new = [[None] * len(blocks) for _ in blocks]
-        new[k][k] = inv
-        for s in blocks:
-            if s != k:
-                new[k][s] = dot32(inv, a[k][s])
-        for r in blocks:
-            if r != k:
-                new[r][k] = -dot32(a[r][k], inv)
-                for s in blocks:
-                    if s != k:
-                        new[r][s] = a[r][s] - dot32(a[r][k], new[k][s])
-        a = new
-    for r in blocks:
-        for s in blocks:
-            minv[r * BLOCK : (r + 1) * BLOCK, s * BLOCK : (s + 1) * BLOCK] = a[r][s]
+    minv[at(0), :] = jnp.concatenate([k00, k10.T, k20.T], axis=1)
+    minv[at(1), :] = jnp.concatenate([k10, k11, k21.T], axis=1)
+    minv[at(2), :] = jnp.concatenate([k20, k21, k22], axis=1)
+    shape = (STEPS, STEPS)
+    lane = lax.broadcasted_iota(jnp.int32, shape, 1)
+    minv[...] += jnp.where(lax.broadcasted_iota(jnp.int32, shape, 0) == lane, 1.0, 0.0)
+    lane1 = lax.broadcasted_iota(jnp.int32, (BLOCK, STEPS), 1)
+    sub1 = lax.broadcasted_iota(jnp.int32, (BLOCK, STEPS), 0)
+    for k in range(count):
+        first, last = k * BLOCK, (k + 1) * BLOCK
+        inv = inverse_block(minv[at(k), first:last], services)
+        inside = (lane1 >= first) & (lane1 < last)
+        row = jnp.where(inside, jnp.where(lane1 - first == sub1, 1.0, 0.0), minv[at(k), :])
+        new = dot32(inv, row)
+        drop = dot32(minv[:, first:last], new)
+        minv[...] = jnp.where((lane >= first) & (lane < last), 0.0, minv[...]) - drop
+        minv[at(k), :] = new
 
 
 def comm_kernel(
@@ -580,7 +581,8 @@
                 g_hi[rows, :] = hi
                 g_lo[rows, :] = lo
 
-    invert(cap, minv, iter((serve_left, y_ring.forward, rest, rest, l_ring.forward, rest, serve_y, rest, rest, serve_core)))
+    invert(cap, minv, iter((serve_left, y_ring.forward, rest, rest, rest, rest, serve_y, l_ring.forward)))
+    serve_core()
 
     m_hi, m_lo = split2(minv[...])
     value = sum(
@@ -685,30 +687,38 @@
     )(rates, targets, goal, readout, corr, rec)
 
 
-TILE = 256
-
-
-def update_kernel(scaled, readout_new, left, corr, rec, corr_out, rec_out, readout_out):
-    rows = aligned(pl.program_id(0) * TILE, TILE)
-    drop = jnp.dot(left[rows, STEPS:], scaled[...], preferred_element_type=F32)
-    corr_out[...] = corr[rows, :] - drop
-    drop = jnp.dot(left[rows, :STEPS], scaled[...], preferred_element_type=F32)
-    rec_out[...] = (rec[rows, :].astype(F32) - drop).astype(BF)
-    readout_out[...] = readout_new[...]
+def update_kernel(scaled, readout_new, left, corr, rec, corr_out, rec_out, readout_out, corr_new, rec_new, sems):
+    copies = [pltpu.make_async_copy(readout_new, readout_out, sems.at[8])]
+    copies[0].start()
+    for q in range(4):
+        rows = pl.ds(q * QUARTER, QUARTER)
+        drop = jnp.dot(left[rows, STEPS:], scaled[...], preferred_element_type=F32)
+        corr_new[rows, :] = corr[rows, :] - drop
+        copies.append(pltpu.make_async_copy(corr_new.at[rows], corr_out.at[rows], sems.at[2 * q]))
+        copies[-1].start()
+        drop = jnp.dot(left[rows, :STEPS], scaled[...], preferred_element_type=F32)
+        rec_new[rows, :] = (rec[rows, :].astype(F32) - drop).astype(BF)
+        copies.append(pltpu.make_async_copy(rec_new.at[rows], rec_out.at[rows], sems.at[2 * q + 1]))
+        copies[-1].start()
+    for copy in copies:
+        copy.wait()
 
 
 def update(scaled, readout_new, left, corr, rec):
-    rows = pl.BlockSpec((TILE, LOCAL), lambda g: (g, 0))
     return pl.pallas_call(
         update_kernel,
-        grid=(LOCAL // TILE,),
         out_shape=[
             jax.ShapeDtypeStruct((LOCAL, LOCAL), F32),
             jax.ShapeDtypeStruct((LOCAL, LOCAL), BF),
             jax.ShapeDtypeStruct((OUTS, LOCAL), F32),
         ],
         in_specs=[pl.BlockSpec(memory_space=pltpu.VMEM)] * 5,
-        out_specs=[rows, rows, pl.BlockSpec((OUTS, LOCAL), lambda g: (0, 0))],
+        out_specs=[pl.BlockSpec(memory_space=pl.ANY)] * 3,
+        scratch_shapes=[
+            pltpu.VMEM((LOCAL, LOCAL), F32),
+            pltpu.VMEM((LOCAL, LOCAL), BF),
+            pltpu.SemaphoreType.DMA((9,)),
+        ],
         compiler_params=pltpu.CompilerParams(vmem_limit_bytes=VMEM_LIMIT),
         name="update",
     )(scaled, readout_new, left, corr, rec)

time: 63.5 us -> 60 us (0.945)
  Pallas kernels: 62.8 us -> 58.8 us
    pallas_call x1, Pallas kernels: 59.3 us -> 55.7 us  [gather_all(): pl.pallas_call(comm_kernel, out_shape=[jax.ShapeDtypeStruct((STEPS, LOCAL...]
where the time goes in v10:
time: 60 us; the launch traced here: 59.6 us
  Pallas kernels  58.8 us (98%)
  between operations  0.8 us (1%)
    pallas_call x1, Pallas kernels, gather_all(): pl.pallas_call(comm_kernel, out_shape=[jax.ShapeDtypeStruct((STEPS, LOCAL...  55.7 us
    pallas_call x1, Pallas kernels, update(): pl.pallas_call(update_kernel, out_shape=[jax.ShapeDtypeStruct((LOCAL, LOC...  3.07 us

profile of v10, /device:TPU:1, one launch (start us, length us, event | category | flops | bytes accessed | tf_op | source)
XLA Modules:
  0.0 59.6 jit_solution(5111209013333680174)
XLA Ops:
  0.6 55.7 %exchange.1 = (bf16[192,1024]{1,0:T(8,128)(2,1)S(1)}, f32[16,1024]{1,0:T(8,128)S(1)}, bf16[1024,384]{1,0:T(8,128)(2,1)S(1)}, f32[1024,1024]{1,0:T(8,128)S(1)}, bf16[1024,1024]{1,0:T(8,128)(2,1)S(1)}) custom-call(bf16[192,1024]{1,0:T(8,128)(2,1)} %rates_hbm.1, bf16[192,1024]{1,0:T(8,128)(2,1)} %targets_hbm.1, f32[16,192]{1,0:T(8,128)} %goal_hbm.1, ...), custom_call_target="tpu_custom_call" | custom-call | tf_op jit(solution)/shard_map/exchange/pallas_call | solution.py:632
  56.4 3.1 %update.1 = (f32[1024,1024]{1,0:T(8,128)}, bf16[1024,1024]{1,0:T(8,128)(2,1)}, f32[16,1024]{1,0:T(8,128)}) custom-call(bf16[192,1024]{1,0:T(8,128)(2,1)S(1)} %get-tuple-element.8.scaled, f32[16,1024]{1,0:T(8,128)S(1)} %get-tuple-element.9.readout_new, bf16[1024,384]{1,0:T(8,128)(2,1)S(1)} %get-tuple-element.10.left, ...), custom_call_target="tpu_custom_call" | custom-call | tf_op jit(solution)/shard_map/update/pallas_call | solution.py:708

commit v11 on v10

--- a/solution.py
+++ b/solution.py
@@ -336,10 +336,9 @@
 
     def prod_quarter(d, out):
         corr_loads[d].wait()
-        hi, lo = split2(corr_v[quarter(x + d), :])
-        value = jnp.dot(hi, rates_t[...], preferred_element_type=F32) + jnp.dot(
-            lo, rates_t[...], preferred_element_type=F32
-        )
+        both = jnp.concatenate(split2(corr_v[quarter(x + d), :]), axis=0)
+        both = jnp.dot(both, rates_t[...], preferred_element_type=F32)
+        value = both[:QUARTER] + both[QUARTER:]
         for g, part in enumerate(groups(value)):
             out[g] = fold(part)
 
@@ -585,10 +584,8 @@
     serve_core()
 
     m_hi, m_lo = split2(minv[...])
-    value = sum(
-        lax.dot_general(m, g, NT, preferred_element_type=F32)
-        for m, g in ((m_hi, g_lo[...]), (m_lo, g_hi[...]), (m_hi, g_hi[...]))
-    )
+    both = lax.dot_general(jnp.concatenate([m_hi, m_lo], axis=0), g_hi[...], NT, preferred_element_type=F32)
+    value = both[:STEPS] + (both[STEPS:] + lax.dot_general(m_hi, g_lo[...], NT, preferred_element_type=F32))
     scaled[...] = value.astype(BF)
     goal_load.wait()
     guess = jnp.concatenate([cap[3 * BLOCK : 3 * BLOCK + OUTS, :], cap[3 * BLOCK + OUTS :, : STEPS - LANES]], axis=1)

time: 60 us -> 59.6 us (level)
  Pallas kernels: 58.8 us -> 57.9 us
    pallas_call x1, Pallas kernels: 55.7 us -> 54.9 us  [gather_all(): pl.pallas_call(comm_kernel, out_shape=[jax.ShapeDtypeStruct((STEPS, LOCAL...]
where the time goes in v11:
time: 59.6 us; the launch traced here: 58.7 us
  Pallas kernels  57.9 us (97%)
  between operations  0.8 us (1%)
    pallas_call x1, Pallas kernels, gather_all(): pl.pallas_call(comm_kernel, out_shape=[jax.ShapeDtypeStruct((STEPS, LOCAL...  54.9 us
    pallas_call x1, Pallas kernels, update(): pl.pallas_call(update_kernel, out_shape=[jax.ShapeDtypeStruct((LOCAL, LOC...  3.07 us

profile of v11, /device:TPU:1, one launch (start us, length us, event | category | flops | bytes accessed | tf_op | source)
XLA Modules:
  0.0 58.7 jit_solution(12373626547720846469)
XLA Ops:
  0.6 54.9 %exchange.1 = (bf16[192,1024]{1,0:T(8,128)(2,1)S(1)}, f32[16,1024]{1,0:T(8,128)S(1)}, bf16[1024,384]{1,0:T(8,128)(2,1)S(1)}, f32[1024,1024]{1,0:T(8,128)S(1)}, bf16[1024,1024]{1,0:T(8,128)(2,1)S(1)}) custom-call(bf16[192,1024]{1,0:T(8,128)(2,1)} %rates_hbm.1, bf16[192,1024]{1,0:T(8,128)(2,1)} %targets_hbm.1, f32[16,192]{1,0:T(8,128)} %goal_hbm.1, ...), custom_call_target="tpu_custom_call" | custom-call | tf_op jit(solution)/shard_map/exchange/pallas_call | solution.py:629
  55.5 3.1 %update.1 = (f32[1024,1024]{1,0:T(8,128)}, bf16[1024,1024]{1,0:T(8,128)(2,1)}, f32[16,1024]{1,0:T(8,128)}) custom-call(bf16[192,1024]{1,0:T(8,128)(2,1)S(1)} %get-tuple-element.8.scaled, f32[16,1024]{1,0:T(8,128)S(1)} %get-tuple-element.9.readout_new, bf16[1024,384]{1,0:T(8,128)(2,1)S(1)} %get-tuple-element.10.left, ...), custom_call_target="tpu_custom_call" | custom-call | tf_op jit(solution)/shard_map/update/pallas_call | solution.py:705
